TPU v7x, 128 devices: a whole 4x4x4 slice. The times are simulated.
128 devices in a mesh: dp: 8 (over z, core), mp: 16 (over x, y).
Axes of the slice: x: 4, y: 4, z: 4, core: 2. Of those that a mesh axis runs over, the one named last changes fastest.
Arguments:
- grad_parts: bfloat16 [8, 2560, 128, 128], P('dp', 'mp'), may hold values from -6 to 6
- master: float32 [2560, 128, 128], P(('mp', 'dp')), may hold values from -0.018 to 0.018
- moment_first: float32 [2560, 128, 128], P(('mp', 'dp')), may hold values from -2 to 2
- moment_second: float32 [2560, 128, 128], P(('mp', 'dp')), may hold values from 0.02 to 1
- serving: bfloat16 [5120, 8192], P(None, 'mp'), may hold values from -0.017944336 to 0.017944336
- changed: int32 [2560], P(('mp', 'dp')), may hold values from 0 to 1, as said below
- hidden_pool: bfloat16 [1024, 5120], P(None, 'mp'), may hold values from -6 to 6
- row_ids: int32 [128], P('dp'), may hold values from 0 to 1023
- head_gain: float32 [128], replicated, may hold values from 0.5 to 1.5
Outputs:
- master_new: float32 [2560, 128, 128], P(('mp', 'dp'))
- first_new: float32 [2560, 128, 128], P(('mp', 'dp'))
- second_new: float32 [2560, 128, 128], P(('mp', 'dp'))
- serving_new: bfloat16 [5120, 8192], P(None, 'mp')
- scores: bfloat16 [128, 8192], P('dp', 'mp')
Inputs may be any that keep to these rules, and one draw needn't show every extreme that they name: `changed`: in every draw all blocks of some run of 20 consecutive entries of the block order, run k being entries k * 20 to k * 20 + 19, are 1.
All inputs are finite; a program needn't handle non-finite values.
Results may differ from a plain program's by a relative error of at most 0.013.
Values may be sent and summed in bfloat16 or wider, within the bound.
No kernel may reach another device: no remote copies, remote signals or barrier semaphores. Data moves between devices by JAX's collectives and lax.ppermute only.
A program may use at most 128 MiB of HBM per device.

v0:
```python
import jax
import jax.numpy as jnp
from jax import lax
from jax.sharding import PartitionSpec as P

beta_one = 0.9
beta_two = 0.999
correct_one = 1.0 - (0.9**10) ** 10
correct_two = 1.0 - (0.999**10) ** 10
adam_eps = 1e-08
learn_rate = 0.001
weight_decay = 0.1


def adam_update(gradient, master, moment_first, moment_second):
    first_new = beta_one * moment_first + (1.0 - beta_one) * gradient
    second_new = beta_two * moment_second + (1.0 - beta_two) * gradient * gradient
    update = (
        first_new / correct_one / (jnp.sqrt(second_new / correct_two) + adam_eps)
        + weight_decay * master
    )
    return (master - learn_rate * update, first_new, second_new)


def on_device(
    grad_parts,
    master,
    moment_first,
    moment_second,
    serving,
    changed,
    hidden_pool,
    row_ids,
    head_gain,
):
    block = master.shape[1]
    per_owner = master.shape[0]
    groups = lax.axis_size("mp")
    replicas = lax.axis_size("dp")
    row_blocks = serving.shape[0] // block
    local_cols = serving.shape[1] // block
    row_width = groups * local_cols
    capacity = -(-per_owner // groups)
    sentinel = row_blocks * local_cols
    picked = jnp.take(hidden_pool, row_ids, axis=0)
    gradient = lax.psum_scatter(grad_parts, "dp", scatter_dimension=1, tiled=True).astype(
        jnp.float32
    )[0]
    master_new, first_new, second_new = adam_update(gradient, master, moment_first, moment_second)
    fresh = master_new.astype(jnp.bfloat16)
    owner = lax.axis_index("mp") * replicas + lax.axis_index("dp")
    position = owner * per_owner + jnp.arange(per_owner, dtype=jnp.int32)
    within = position % row_width
    group = within % groups
    target = position // row_width * local_cols + within // groups
    marked = changed == 1
    onehot = (
        (group[:, None] == jnp.arange(groups, dtype=jnp.int32)[None, :]) & marked[:, None]
    ).astype(jnp.int32)
    slot_rank = jnp.maximum(jnp.sum(jnp.cumsum(onehot, axis=0) * onehot, axis=1) - 1, 0)
    destination = jnp.where(marked, group, groups)
    outgoing = jnp.zeros((groups, capacity, block, block), jnp.bfloat16)
    outgoing = outgoing.at[destination, slot_rank].set(fresh, mode="drop")
    labels = jnp.full((groups, capacity), sentinel, jnp.int32)
    labels = labels.at[destination, slot_rank].set(target, mode="drop")
    spread = jnp.broadcast_to(outgoing[None], (replicas,) + outgoing.shape).reshape(
        (-1, block, block)
    )
    spread_labels = jnp.broadcast_to(labels[None], (replicas,) + labels.shape).reshape(-1)
    arrived, arrived_labels = (
        lax.all_to_all(spread, ("dp", "mp"), split_axis=0, concat_axis=0, tiled=True),
        lax.all_to_all(spread_labels, ("dp", "mp"), split_axis=0, concat_axis=0, tiled=True),
    )
    view = serving.reshape(row_blocks, block, local_cols, block)
    placed = view.at[arrived_labels // local_cols, :, arrived_labels % local_cols, :].set(
        arrived, mode="drop"
    )
    serving_new = placed.reshape(serving.shape)
    query = jnp.dot(
        lax.all_gather(picked, "mp", axis=1, tiled=True),
        serving_new,
        preferred_element_type=jnp.float32,
    )
    heads = query.reshape(query.shape[0], -1, head_gain.shape[0])
    normed = heads * lax.rsqrt(jnp.mean(heads * heads, axis=-1, keepdims=True) + 1e-06) * head_gain
    scores = normed.reshape(query.shape).astype(jnp.bfloat16)
    return (master_new, first_new, second_new, serving_new, scores)


def solution(mesh):
    return jax.shard_map(
        on_device,
        mesh=mesh,
        in_specs=(
            P("dp", "mp", None, None),
            P(("mp", "dp"), None, None),
            P(("mp", "dp"), None, None),
            P(("mp", "dp"), None, None),
            P(None, "mp"),
            P(("mp", "dp")),
            P(None, "mp"),
            P("dp"),
            P(),
        ),
        out_specs=(
            P(("mp", "dp"), None, None),
            P(("mp", "dp"), None, None),
            P(("mp", "dp"), None, None),
            P(None, "mp"),
            P("dp", "mp"),
        ),
        check_vma=False,
    )
```

profile of v0, /device:TPU:32, one launch (start us, length us, event | category | flops | bytes accessed | tf_op | source)
XLA Modules:
  0.0 266.6 jit_solution(16909271515307293665)
XLA Ops:
  7.2 0.0 copy-start.3
  7.2 0.0 reduce-scatter.2.cloned.1.call-start
  7.2 0.7 reduce-scatter.2.cloned.1.call-update
  7.9 0.0 copy-start
  8.0 0.0 copy-done.3
  8.0 0.1 fusion.4
  8.1 0.2 select_reduce_fusion
  8.3 2.0 scatter_fusion
  10.3 0.1 copy.27
  10.4 0.6 broadcast_in_dim.26
  11.1 10.2 %all-to-all-start = ((s32[128,2,1]{1,2,0:T(1,128)}), s32[128,2,1]{1,2,0:T(1,128)S(1)}, u32[]{:S(2)}, u32[]{:S(2)}) async-start(s32[128,2,1]{1,2,0:T(1,128)} %bitcast.5), calls=%async_computation.1 | async-start | bytes 131072 | tf_op jit(solution)/shard_map/all_to_all | solution.py:72
  21.3 28.0 %reduce-scatter.2.cloned.1.call-done = bf16[1,20,128,128]{3,2,1,0:T(8,128)(2,1)} async-done(((bf16[1,160,128,128]{3,2,1,0:T(8,128)(2,1)}), bf16[1,20,128,128]{3,2,1,0:T(8,128)(2,1)}) %reduce-scatter.2.cloned.1.call-update) | async-done | bytes 655376 | tf_op jit(solution)/shard_map/reduce_scatter | solution.py:46
  49.3 0.0 copy-done
  49.3 4.6 %fusion.9 = (bf16[20,128,128]{2,1,0:T(8,128)(2,1)S(1)}, f32[20,128,128]{2,1,0:T(8,128)}, f32[20,128,128]{2,1,0:T(8,128)}, f32[20,128,128]{2,1,0:T(8,128)}) fusion(f32[20,128,128]{2,1,0:T(8,128)S(1)} %copy-done, bf16[1,20,128,128]{3,2,1,0:T(8,128)(2,1)} %reduce-scatter.2.cloned.1.call-done, f32[20,128,128]{2,1,0:T(8,128)} %param.11, f32[20,128,128]{2,1,0:T(8,128)} %param.12), kind=kLoop, calls=%fused_computation.55 | loop fusion | flops 5570560 | bytes 9175040 | tf_op jit(solution)/shard_map/convert_element_type | solution.py:50
  53.9 0.2 broadcast_in_dim.27
  54.1 2.0 scatter_fusion.1
  56.1 0.0 all-to-all-done
  56.1 5.3 %broadcast_in_dim.28 = bf16[8,16,2,128,128]{4,3,2,1,0:T(8,128)(2,1)} broadcast(bf16[16,2,128,128]{3,2,1,0:T(8,128)(2,1)S(1)} %scatter_fusion.1), dimensions={1,2,3,4} | broadcast | bytes 9437184 | tf_op jit(solution)/shard_map/broadcast_in_dim | solution.py:66
  61.5 12.0 %all-to-all-start.1 = ((bf16[256,128,128]{2,1,0:T(8,128)(2,1)}), bf16[256,128,128]{2,1,0:T(8,128)(2,1)}, u32[]{:S(2)}, u32[]{:S(2)}) async-start(bf16[256,128,128]{2,1,0:T(8,128)(2,1)} %bitcast.47), calls=%async_computation.2 | async-start | bytes 16777216 | tf_op jit(solution)/shard_map/all_to_all | solution.py:71
  73.5 8.3 %reshape.238 = bf16[40,128,4,128]{3,2,1,0:T(4,128)(2,1)} reshape(bf16[5120,512]{1,0:T(8,128)(2,1)} %param.13) | data formatting | bytes 10485760 | tf_op jit(solution)/shard_map/reshape | solution.py:74
  81.8 0.0 copy-start.1
  81.8 6.3 %copy.28 = bf16[40,128,4,128]{3,1,2,0:T(8,128)(2,1)} copy(bf16[40,128,4,128]{3,2,1,0:T(4,128)(2,1)} %reshape.238) | data formatting | bytes 10485760 | tf_op jit(solution)/shard_map/reshape | solution.py:74
  88.1 0.0 copy-done.1
  88.1 0.0 copy-start.4
  88.1 0.4 copy.30
  88.5 0.3 copy-done.4
  88.8 0.6 gather_fusion
  89.4 0.1 select_bitcast_fusion
  89.4 101.6 %all-gather = bf16[16,320,16]{1,2,0:T(8,128)(2,1)S(1)} all-gather(bf16[1,320,16]{1,2,0:T(8,128)(2,1)S(1)} %select_bitcast_fusion), channel_id=1, replica_groups=mesh['dp'=8,'mp'=16] {'mp'}, dimensions={0}, use_global_device_ids=true | all-gather | bytes 174080 | tf_op jit(solution)/shard_map/all_gather | solution.py:80
  191.1 0.2 reshape.237
  191.3 0.5 broadcast.368
  191.8 0.8 reduce.3
  192.6 0.1 all_to_all.13
  192.8 0.0 all-to-all-done.1
  192.8 39.3 %scatter_fusion.2 = bf16[40,128,4,128]{3,1,2,0:T(8,128)(2,1)} fusion(bf16[40,128,4,128]{3,1,2,0:T(8,128)(2,1)} %copy.28, s32[256]{0:T(256)S(1)} %bitcast.49, bf16[256,128,128]{2,1,0:T(8,128)(2,1)} %all-to-all-done.1), kind=kCustom, calls=%fused_computation.3 | custom fusion | bytes 25167872 | tf_op jit(solution)/shard_map/scatter | solution.py:75
  232.2 8.6 %copy.29 = bf16[40,128,4,128]{1,0,3,2:T(8,128)(2,1)} copy(bf16[40,128,4,128]{3,1,2,0:T(8,128)(2,1)} %scatter_fusion.2) | data formatting | bytes 10485760 | tf_op jit(solution)/shard_map/scatter | solution.py:75
  240.8 6.2 %copy.40 = bf16[64,8,40,128]{3,1,2,0:T(8,128)(2,1)} copy(bf16[64,8,40,128]{3,2,1,0:T(8,128)(2,1)} %bitcast.48) | data formatting | bytes 10485760
  247.0 7.9 %copy.33 = bf16[5120,512]{1,0:T(8,128)(2,1)} copy(bf16[5120,512]{0,1:T(8,128)(2,1)} %bitcast.45) | data formatting | bytes 10485760
  255.0 0.0 copy-start.2
  255.0 4.0 %multiply_reduce_fusion = (f32[16,4]{0,1:T(4,128)S(1)}, f32[16,4,128]{2,0,1:T(8,128)S(1)}) fusion(bf16[5120,16,1]{0,1,2:T(8,128)(2,1)S(1)} %reshape.237, bf16[4,128,5120]{2,1,0:T(8,128)(2,1)} %bitcast.46), kind=kOutput, calls=%fused_computation.12 | convolution fusion | flops 83902400 | bytes 5439744 | tf_op jit(solution)/shard_map/dot_general | solution.py:79
  259.0 0.0 copy-done.2
  259.0 0.7 copy_bitcast_fusion.1
  (11 shorter events, 0.2 us)
Async XLA Ops:
  7.2 0.8 copy-start.3
  7.2 42.1 %reduce-scatter.2.cloned.1.call-start = ((), (), s32[]{:S(2)}) async-start(), calls=%async_computation.3 | async-start | bytes 5898240 | tf_op jit(solution)/shard_map/reduce_scatter | solution.py:46
  7.9 41.4 %copy-start = (f32[20,128,128]{2,1,0:T(8,128)S(1)}, f32[20,128,128]{2,1,0:T(8,128)}, u32[]{:S(2)}) copy-start(f32[20,128,128]{2,1,0:T(8,128)} %param.10) | copy-start | bytes 3932164
  11.1 45.1 %all-to-all-start = ((s32[128,2,1]{1,2,0:T(1,128)}), s32[128,2,1]{1,2,0:T(1,128)S(1)}, u32[]{:S(2)}, u32[]{:S(2)}) async-start(s32[128,2,1]{1,2,0:T(1,128)} %bitcast.5), calls=%async_computation.1 | async-start | bytes 131072 | tf_op jit(solution)/shard_map/all_to_all | solution.py:72
  61.5 131.3 %all-to-all-start.1 = ((bf16[256,128,128]{2,1,0:T(8,128)(2,1)}), bf16[256,128,128]{2,1,0:T(8,128)(2,1)}, u32[]{:S(2)}, u32[]{:S(2)}) async-start(bf16[256,128,128]{2,1,0:T(8,128)(2,1)} %bitcast.47), calls=%async_computation.2 | async-start | bytes 16777216 | tf_op jit(solution)/shard_map/all_to_all | solution.py:71
  81.8 6.3 %copy-start.1 = (bf16[1024,320]{0,1:T(8,128)(2,1)S(1)}, bf16[1024,320]{0,1:T(8,128)(2,1)}, u32[]{:S(2)}) copy-start(bf16[1024,320]{0,1:T(8,128)(2,1)} %param.15) | copy-start | bytes 1966084
  88.1 0.7 copy-start.4
  255.0 4.1 %copy-start.2 = (f32[128]{0:T(128)S(1)}, f32[128]{0:T(128)}, u32[]{:S(2)}) copy-start(f32[128]{0:T(128)} %param.17) | copy-start | bytes 1540
Sparse Core Ops, SparseCore 0:
  10.4 38.8 reduce-scatter.1
where the time goes:
time: 268 us; the launch traced here: 267 us
  blocking collectives  102 us (38%)
  local copies, waits for them, and re-layouts  89.2 us (33%)
  waiting for transfers between devices  28.7 us (11%)
  starting transfers between devices  22.2 us (8%)
  between operations  14.2 us (5%)
  other arithmetic  6.52 us (2%)
  matrix products  4.03 us (2%)
    all_gather x1, blocking collectives, on_device(): lax.all_gather(picked, 'mp', axis=1, tiled=True)  102 us
    scatter x2, local copies, waits for them, and re-layouts, on_device(): view.at[arrived_labels // local_cols, :, arrived_labels % local_cols, :]  48 us
    reduce_scatter x1, waiting for transfers between devices, on_device(): lax.psum_scatter(grad_parts, 'dp', scatter_dimension=1, tiled=True)  28 us
    unnamed x14, local copies, waits for them, and re-layouts  15 us
    reshape x2, local copies, waits for them, and re-layouts, on_device(): view = serving.reshape(row_blocks, block, local_cols, block)  14.6 us
    all_to_all x1, starting transfers between devices, on_device(): lax.all_to_all(spread, ('dp', 'mp'), split_axis=0, concat_axis=0, tiled=T...  12 us
    all_to_all x1, starting transfers between devices, on_device(): lax.all_to_all(spread_labels, ('dp', 'mp'), split_axis=0, concat_axis=0,...  10.2 us
  transfers between devices with their start and end apart: 3, of which 1 were waited for; matrix products, arithmetic and copies ran while one was open for 10% of the time, Pallas kernels for 0%

commit v1 on v0

v1 whole, which is shorter than its diff:
```python
import functools

import jax
import jax.numpy as jnp
from jax import lax
from jax.experimental import pallas as pl
from jax.experimental.pallas import tpu as pltpu
from jax.sharding import PartitionSpec as P

beta_one = 0.9
beta_two = 0.999
correct_one = 1.0 - (0.9**10) ** 10
correct_two = 1.0 - (0.999**10) ** 10
adam_eps = 1e-08
learn_rate = 0.001
weight_decay = 0.1

f32 = jnp.float32
bf16 = jnp.bfloat16
MiB = 1024 * 1024

Z_UP = [(i, (i + 2) % 8) for i in range(8)]
Z_DOWN = [(i, (i - 2) % 8) for i in range(8)]
CORE = [(i, i ^ 1) for i in range(8)]
SWAP = [
    (d * 16 + x * 4 + y, (d // 4 * 4 + x) * 16 + (d % 4) * 4 + y)
    for d in range(8)
    for x in range(4)
    for y in range(4)
]


def along_x(s):
    return [(x * 4 + y, (x + s) % 4 * 4 + y) for x in range(4) for y in range(4)]


def along_y(s):
    return [(x * 4 + y, x * 4 + (y + s) % 4) for x in range(4) for y in range(4)]


def on_dp(value, pairs):
    return lax.ppermute(value, "dp", pairs)


def on_mp(value, pairs):
    return lax.ppermute(value, "mp", pairs)


def add(a, b):
    return (a.astype(f32) + b.astype(f32)).astype(bf16)


def adam_kernel(
    place,
    marked,
    own,
    other,
    below_a,
    below_b,
    above_a,
    above_b,
    master,
    first,
    second,
    master_out,
    first_out,
    second_out,
    *slots,
):
    step = pl.program_id(0)
    x, y, e = place[1], place[2], place[3]
    slot = jnp.where(step == 4, 4, (step + e - x + 4) % 4)
    for block in range(4):
        halves = []
        for rows, below, above in (
            (pl.ds(0, 64), below_a, above_a),
            (pl.ds(64, 64), below_b, above_b),
        ):
            gradient = (
                own[0, block, rows].astype(f32)
                + other[block, rows].astype(f32)
                + below[block].astype(f32)
                + above[block].astype(f32)
            )
            weight = master[block, rows]
            first_new = beta_one * first[block, rows] + (1.0 - beta_one) * gradient
            second_new = (
                beta_two * second[block, rows] + (1.0 - beta_two) * gradient * gradient
            )
            update = (
                first_new / correct_one / (jnp.sqrt(second_new / correct_two) + adam_eps)
                + weight_decay * weight
            )
            weight_new = weight - learn_rate * update
            master_out[block, rows] = weight_new
            first_out[block, rows] = first_new
            second_out[block, rows] = second_new
            halves.append(weight_new)
        flag = marked[step * 4 + block]
        fresh = jnp.concatenate(halves, axis=0)
        fresh = jnp.where(flag == 1, fresh, jnp.inf).astype(bf16)
        at = (block - y + 4) % 4
        for i in range(5):

            @pl.when(slot == i)
            def _():
                slots[i][at] = fresh


def adam(place, changed, grad_parts, other, below_a, below_b, above_a, above_b, *state):
    def rows(height):
        return pl.BlockSpec((4, height, 128), lambda i, place, marked: (i, 0, 0))

    own = pl.BlockSpec((1, 4, 128, 128), lambda i, place, marked: (0, place[0] * 5 + i, 0, 0))
    whole = pl.BlockSpec((4, 128, 128), lambda i, place, marked: (0, 0, 0))
    return pl.pallas_call(
        adam_kernel,
        grid_spec=pltpu.PrefetchScalarGridSpec(
            num_scalar_prefetch=2,
            grid=(5,),
            in_specs=[own, rows(128)] + [rows(64)] * 4 + [rows(128)] * 3,
            out_specs=[rows(128)] * 3 + [whole] * 5,
        ),
        out_shape=[jax.ShapeDtypeStruct((20, 128, 128), f32)] * 3
        + [jax.ShapeDtypeStruct((4, 128, 128), bf16)] * 5,
        compiler_params=pltpu.CompilerParams(vmem_limit_bytes=32 * MiB),
        cost_estimate=pl.CostEstimate(
            flops=20 * 128 * 128 * 20, bytes_accessed=11 * MiB, transcendentals=2 * 20 * 128 * 128
        ),
    )(place, changed, grad_parts, other, below_a, below_b, above_a, above_b, *state)


def place_kernel(place, serving, features, gain, *refs):
    pieces, out, scores = refs[:16], refs[16], refs[17]
    x, y, z, core = place[1], place[2], place[4], place[5]
    for number in range(16):
        k, q, h = number // 4, number // 2 % 2, number % 2
        piece = pieces[number]
        z_from = (z + k) % 4
        core_from = core ^ q
        e_from = 2 * (z_from % 2) + core_from
        base = 5 * (z_from // 2)

        def put(u, carry):
            y_from = (y - (2 * h + u) + 4) % 4
            for s in range(5):
                if s < 4:
                    x_from = (x - s + 4) % 4
                    t = 10 * (4 * x_from + y_from) + base + e_from + (e_from > x).astype(jnp.int32)
                else:
                    t = 10 * (4 * e_from + y_from) + base + x + 1
                rows = pl.ds(pl.multiple_of(t // 4 * 128, 128), 128)
                columns = pl.ds(pl.multiple_of(t % 4 * 128, 128), 128)
                block = piece[u * 5 + s]
                held = serving[rows, columns]
                out[rows, columns] = jnp.where(block.astype(f32) == jnp.inf, held, block)
            return carry

        lax.fori_loop(0, 2, put, 0)

    total = jnp.zeros((16, 512), f32)
    for u in range(4):
        for s in range(4):
            x_from = (x - s + 4) % 4
            y_from = (y - u + 4) % 4
            rows = pl.ds(pl.multiple_of((4 * x_from + y_from) * 320, 64), 320)
            total += jnp.dot(features[u * 4 + s], out[rows, :], preferred_element_type=f32)
    for head in range(4):
        query = total[:, head * 128 : head * 128 + 128]
        scale = lax.rsqrt(jnp.mean(query * query, axis=-1, keepdims=True) + 1e-06)
        scores[:, head * 128 : head * 128 + 128] = (query * scale * gain[...]).astype(bf16)


def put_and_score(place, serving, features, gain, pieces):
    vmem = pl.BlockSpec(memory_space=pltpu.VMEM)
    return pl.pallas_call(
        place_kernel,
        in_specs=[pl.BlockSpec(memory_space=pltpu.SMEM)] + [vmem] * 19,
        out_specs=[vmem] * 2,
        out_shape=[
            jax.ShapeDtypeStruct((5120, 512), bf16),
            jax.ShapeDtypeStruct((16, 512), bf16),
        ],
        compiler_params=pltpu.CompilerParams(vmem_limit_bytes=48 * MiB),
        cost_estimate=pl.CostEstimate(
            flops=2 * 16 * 5120 * 512, bytes_accessed=16 * MiB, transcendentals=0
        ),
    )(place, serving, features, gain, *pieces)


def on_device(
    grad_parts,
    master,
    moment_first,
    moment_second,
    serving,
    changed,
    hidden_pool,
    row_ids,
    head_gain,
):
    dp = lax.axis_index("dp")
    mp = lax.axis_index("mp")
    z, core = dp // 2, dp % 2
    x, y = mp // 4, mp % 4
    place = jnp.stack([dp, x, y, dp % 4, z, core]).astype(jnp.int32)

    picked = jnp.take(hidden_pool, row_ids, axis=0, mode="clip")
    row = jnp.stack([picked] + [on_mp(picked, along_x(s)) for s in (1, 2, 3)])
    features = jnp.concatenate([row] + [on_mp(row, along_y(s)) for s in (1, 2, 3)])

    parts = grad_parts.reshape(4, 2, 20, 128, 128)

    def part(k, c):
        start = ((z + k) % 4, c, 0, 0, 0)
        return lax.dynamic_slice(parts, start, (1, 1, 20, 128, 128))[0, 0]

    sums = {}
    for k in (2, 1, 3):
        sums[k] = add(part(k, core), on_dp(part(k, 1 - core), CORE))
    far_a = on_dp(sums[2][:, :64], Z_UP)
    far_b = on_dp(sums[2][:, 64:], Z_DOWN)
    below_b = on_dp(sums[1][:, 64:], Z_UP)
    above_a = on_dp(sums[3][:, :64], Z_DOWN)
    other = on_dp(part(0, 1 - core), CORE)
    below_a = on_dp(add(sums[1][:, :64], far_a), Z_UP)
    above_b = on_dp(add(sums[3][:, 64:], far_b), Z_DOWN)

    master_new, first_new, second_new, *slots = adam(
        place,
        changed,
        grad_parts,
        other,
        below_a,
        below_b,
        above_a,
        above_b,
        master,
        moment_first,
        moment_second,
    )

    row = [slots[0]] + [on_mp(slots[s], along_x(s)) for s in (1, 2, 3)]
    row.append(lax.ppermute(slots[4], ("dp", "mp"), SWAP))
    plane = []
    for u in range(4):
        group = jnp.stack([r[u] for r in row])
        plane.append(on_mp(group, along_y(u)) if u else group)

    a = jnp.concatenate(plane[:2])
    b = jnp.concatenate(plane[2:])
    below_a = on_dp(a, Z_UP)
    above_b = on_dp(b, Z_DOWN)
    below_b = on_dp(b, Z_UP)
    above_a = on_dp(a, Z_DOWN)
    far_a = on_dp(below_a, Z_UP)
    far_b = on_dp(above_b, Z_DOWN)
    pieces = []
    for pair in ((a, b), (above_a, above_b), (far_a, far_b), (below_a, below_b)):
        pieces += list(pair) + [on_dp(value, CORE) for value in pair]

    serving_new, scores = put_and_score(
        place, serving, features, head_gain.reshape(1, 128), pieces
    )
    return (master_new, first_new, second_new, serving_new, scores)


def solution(mesh):
    return jax.shard_map(
        on_device,
        mesh=mesh,
        in_specs=(
            P("dp", "mp", None, None),
            P(("mp", "dp"), None, None),
            P(("mp", "dp"), None, None),
            P(("mp", "dp"), None, None),
            P(None, "mp"),
            P(("mp", "dp")),
            P(None, "mp"),
            P("dp"),
            P(),
        ),
        out_specs=(
            P(("mp", "dp"), None, None),
            P(("mp", "dp"), None, None),
            P(("mp", "dp"), None, None),
            P(None, "mp"),
            P("dp", "mp"),
        ),
        check_vma=False,
    )
```

time: 268 us -> 118 us (0.44)
  the two profiles are of different devices: /device:TPU:32 before, /device:TPU:1 now
where the time goes in v1:
time: 118 us; the launch traced here: 117 us
  starting transfers between devices  51.1 us (43%)
  waiting for transfers between devices  36.6 us (31%)
  Pallas kernels  15.3 us (13%)
  local copies, waits for them, and re-layouts  9.38 us (8%)
  other arithmetic  4.05 us (3%)
    ppermute x24, starting transfers between devices, on_dp(): return lax.ppermute(value, 'dp', pairs)  28.5 us
    ppermute x24, waiting for transfers between devices, on_dp(): return lax.ppermute(value, 'dp', pairs)  27.8 us
    ppermute x12, starting transfers between devices, on_mp(): return lax.ppermute(value, 'mp', pairs)  18.2 us
    pallas_call x1, Pallas kernels, put_and_score(): pl.pallas_call(place_kernel, in_specs=[pl.BlockSpec(memory_space=pltpu.SM...  9.26 us
    ppermute x12, waiting for transfers between devices, on_mp(): return lax.ppermute(value, 'mp', pairs)  6.28 us
    pallas_call x1, Pallas kernels, adam(): pl.pallas_call(adam_kernel, grid_spec=pltpu.PrefetchScalarGridSpec(num_sc...  6.05 us
    ppermute x1, starting transfers between devices, on_device(): row.append(lax.ppermute(slots[4], ('dp', 'mp'), SWAP))  4.46 us
    unnamed x28, local copies, waits for them, and re-layouts  4.31 us
  transfers between devices with their start and end apart: 37, of which 15 were waited for; matrix products, arithmetic and copies ran while one was open for 4% of the time, Pallas kernels for 0%

profile of v1, /device:TPU:1, one launch (start us, length us, event | category | flops | bytes accessed | tf_op | source)
XLA Modules:
  0.0 117.4 jit_solution(1101105795564481063)
XLA Ops:
  0.7 2.8 %dynamic-slice_bitcast_fusion = (bf16[20,128,128]{2,1,0:T(8,128)(2,1)S(1)}, bf16[20,128,128]{2,1,0:T(8,128)(2,1)S(1)}, bf16[20,128,128]{2,1,0:T(8,128)(2,1)S(1)}, bf16[20,128,128]{2,1,0:T(8,128)(2,1)}) fusion(bf16[4,2,20,128,128]{4,3,2,1,0:T(8,128)(2,1)} %bitcast.33, s32[]{:T(128)S(6)} %select_n.84, s32[]{:T(128)S(6)} %select_n.77, s32[]{:T(128)S(6)} %select_n.82, ...), kind=kLoop, calls=%fused_computation.8 | loop fusion | bytes 5242900 | tf_op jit(solution)/shard_map/squeeze | solution.py:216
  3.5 1.4 %collective-permute-start.6 = (bf16[20,128,128]{2,1,0:T(8,128)(2,1)S(1)}, bf16[20,128,128]{2,1,0:T(8,128)(2,1)S(1)}, u32[]{:S(2)}, u32[]{:S(2)}) collective-permute-start(bf16[20,128,128]{2,1,0:T(8,128)(2,1)S(1)} %get-tuple-element.28), channel_id=1, source_target_pairs={{0,16},{16,0},{32,48},{48,32},{64,80},{80,64},{96,112},{112,96},{1... | collective-permute-start | bytes 1966088 | tf_op jit(solution)/shard_map/ppermute | solution.py:42
  4.9 0.5 collective-permute-start.1
  5.4 1.2 %collective-permute-done.6 = bf16[20,128,128]{2,1,0:T(8,128)(2,1)S(1)} collective-permute-done((bf16[20,128,128]{2,1,0:T(8,128)(2,1)S(1)}, bf16[20,128,128]{2,1,0:T(8,128)(2,1)S(1)}, u32[]{:S(2)}, u32[]{:S(2)}) %collective-permute-start.6) | collective-permute-done | bytes 655392 | tf_op jit(solution)/shard_map/ppermute | solution.py:42
  6.7 1.9 %collective-permute-done.2 = bf16[20,128,128]{2,1,0:T(8,128)(2,1)S(1)} collective-permute-done((bf16[20,128,128]{2,1,0:T(8,128)(2,1)S(1)}, bf16[20,128,128]{2,1,0:T(8,128)(2,1)S(1)}, u32[]{:S(2)}, u32[]{:S(2)}) %collective-permute-start.2) | collective-permute-done | bytes 655392 | tf_op jit(solution)/shard_map/ppermute | solution.py:42
  8.7 2.4 %fusion = (bf16[20,128,128]{2,1,0:T(8,128)(2,1)S(1)}, bf16[20,128,128]{2,1,0:T(8,128)(2,1)S(1)}, bf16[20,128,128]{2,1,0:T(8,128)(2,1)S(1)}) fusion(bf16[20,128,128]{2,1,0:T(8,128)(2,1)S(1)} %collective-permute-done.6, bf16[4,2,20,128,128]{4,3,2,1,0:T(8,128)(2,1)} %bitcast.34, s32[]{:T(128)S(6)} %select_n.84, s32[]{:T(128)S(6)} %select_n.80, ...), kind=kLoop, calls=%fused_computation.2 | loop fusion | flops 3932160 | bytes 5898256 | tf_op jit(solution)/shard_map/convert_element_type | solution.py:50
  11.1 3.9 %collective-permute-start.8 = (bf16[20,64,128]{2,1,0:T(8,128)(2,1)S(1)}, bf16[20,64,128]{2,1,0:T(8,128)(2,1)S(1)}, u32[]{:S(2)}, u32[]{:S(2)}) collective-permute-start(bf16[20,64,128]{2,1,0:T(8,128)(2,1)S(1)} %get-tuple-element.32), channel_id=1, source_target_pairs={{0,96},{16,112},{32,0},{48,16},{64,32},{80,48},{96,64},{112,80},{1... | collective-permute-start | bytes 983048 | tf_op jit(solution)/shard_map/ppermute | solution.py:42
  15.0 0.7 collective-permute-start
  15.7 0.8 slice.109
  16.4 0.8 slice.108
  17.2 3.0 %collective-permute-start.7 = (bf16[20,64,128]{2,1,0:T(8,128)(2,1)}, bf16[20,64,128]{2,1,0:T(8,128)(2,1)}, u32[]{:S(2)}, u32[]{:S(2)}) collective-permute-start(bf16[20,64,128]{2,1,0:T(8,128)(2,1)} %slice.109), channel_id=1, source_target_pairs={{0,96},{16,112},{32,0},{48,16},{64,32},{80,48},{96,64},{112,80},{1... | collective-permute-start | bytes 983048 | tf_op jit(solution)/shard_map/ppermute | solution.py:42
  20.1 1.6 %collective-permute-done.8 = bf16[20,64,128]{2,1,0:T(8,128)(2,1)S(1)} collective-permute-done((bf16[20,64,128]{2,1,0:T(8,128)(2,1)S(1)}, bf16[20,64,128]{2,1,0:T(8,128)(2,1)S(1)}, u32[]{:S(2)}, u32[]{:S(2)}) %collective-permute-start.8) | collective-permute-done | bytes 327712 | tf_op jit(solution)/shard_map/ppermute | solution.py:42
  21.7 0.8 add_convert_fusion
  22.6 3.4 %collective-permute-start.9 = (bf16[20,64,128]{2,1,0:T(8,128)(2,1)}, bf16[20,64,128]{2,1,0:T(8,128)(2,1)}, u32[]{:S(2)}, u32[]{:S(2)}) collective-permute-start(bf16[20,64,128]{2,1,0:T(8,128)(2,1)} %add_convert_fusion), channel_id=1, source_target_pairs={{0,96},{16,112},{32,0},{48,16},{64,32},{80,48},{96,64},{112,80},{1... | collective-permute-start | bytes 983048 | tf_op jit(solution)/shard_map/ppermute | solution.py:42
  26.0 0.8 add_convert_fusion.1
  26.9 5.1 %collective-permute-done.5.below_b = bf16[20,64,128]{2,1,0:T(8,128)(2,1)} collective-permute-done((bf16[20,64,128]{2,1,0:T(8,128)(2,1)}, bf16[20,64,128]{2,1,0:T(8,128)(2,1)}, u32[]{:S(2)}, u32[]{:S(2)}) %collective-permute-start.5) | collective-permute-done | bytes 327712 | tf_op jit(solution)/shard_map/ppermute | solution.py:42
  32.0 3.9 %collective-permute-done.9.above_b = bf16[20,64,128]{2,1,0:T(8,128)(2,1)} collective-permute-done((bf16[20,64,128]{2,1,0:T(8,128)(2,1)}, bf16[20,64,128]{2,1,0:T(8,128)(2,1)}, u32[]{:S(2)}, u32[]{:S(2)}) %collective-permute-start.9) | collective-permute-done | bytes 327712 | tf_op jit(solution)/shard_map/ppermute | solution.py:42
  35.9 3.1 %collective-permute-done.4.below_a = bf16[20,64,128]{2,1,0:T(8,128)(2,1)} collective-permute-done((bf16[20,64,128]{2,1,0:T(8,128)(2,1)}, bf16[20,64,128]{2,1,0:T(8,128)(2,1)}, u32[]{:S(2)}, u32[]{:S(2)}) %collective-permute-start.4) | collective-permute-done | bytes 327712 | tf_op jit(solution)/shard_map/ppermute | solution.py:42
  39.0 2.5 %copy-done = bf16[1,160,128,128]{3,2,1,0:T(8,128)(2,1)S(1)} copy-done((bf16[1,160,128,128]{3,2,1,0:T(8,128)(2,1)S(1)}, bf16[1,160,128,128]{3,2,1,0:T(8,128)(2,1)}, u32[]{:S(2)}) %copy-start) | copy-done | bytes 5242904
  41.5 1.3 %copy-done.3 = f32[20,128,128]{2,1,0:T(8,128)S(1)} copy-done((f32[20,128,128]{2,1,0:T(8,128)S(1)}, f32[20,128,128]{2,1,0:T(8,128)}, u32[]{:S(2)}) %copy-start.3) | copy-done | bytes 1310744
  42.8 6.0 %shard_map.128 = (f32[20,128,128]{2,1,0:T(8,128)}, f32[20,128,128]{2,1,0:T(8,128)}, f32[20,128,128]{2,1,0:T(8,128)}, bf16[4,128,128]{2,1,0:T(8,128)(2,1)S(1)}, b...) custom-call(s32[6]{0:T(128)S(1)} %stack.51.place, ...), custom_call_target="tpu_custom_call" | custom-call | flops 6553600 | bytes 11534336 | tf_op jit(solution)/shard_map/pallas_call | solution.py:116
  48.8 1.3 %collective-permute-start.16 = (bf16[4,128,128]{2,1,0:T(8,128)(2,1)S(1)}, bf16[4,128,128]{2,1,0:T(8,128)(2,1)S(1)}, u32[]{:S(2)}, u32[]{:S(2)}) collective-permute-start(bf16[4,128,128]{2,1,0:T(8,128)(2,1)S(1)} %get-tuple-element.19), channel_id=1, source_target_pairs={{0,4},{1,5},{2,6},{3,7},{4,8},{5,9},{6,10},{7,11},{8,12},{9,13},{1... | collective-permute-start | bytes 393224 | tf_op jit(solution)/shard_map/ppermute | solution.py:46
  50.1 2.5 %collective-permute-start.17 = (bf16[4,128,128]{2,1,0:T(8,128)(2,1)S(1)}, bf16[4,128,128]{2,1,0:T(8,128)(2,1)S(1)}, u32[]{:S(2)}, u32[]{:S(2)}) collective-permute-start(bf16[4,128,128]{2,1,0:T(8,128)(2,1)S(1)} %get-tuple-element.20), channel_id=1, source_target_pairs={{0,8},{1,9},{2,10},{3,11},{4,12},{5,13},{6,14},{7,15},{8,0},{9,1},... | collective-permute-start | bytes 393224 | tf_op jit(solution)/shard_map/ppermute | solution.py:46
  52.6 1.2 collective-permute-start.18
  53.7 4.5 %collective-permute-start.19 = (bf16[4,128,128]{2,1,0:T(8,128)(2,1)S(1)}, bf16[4,128,128]{2,1,0:T(8,128)(2,1)S(1)}, u32[]{:S(2)}, u32[]{:S(2)}) collective-permute-start(bf16[4,128,128]{2,1,0:T(8,128)(2,1)S(1)} %get-tuple-element.22), channel_id=1, source_target_pairs={{0,0},{1,1},{2,2},{3,3},{4,16},{5,17},{6,18},{7,19},{8,32},{9,33},... | collective-permute-start | bytes 393224 | tf_op jit(solution)/shard_map/ppermute | solution.py:244
  58.3 2.5 %collective-permute-done.19 = bf16[4,128,128]{2,1,0:T(8,128)(2,1)S(1)} collective-permute-done((bf16[4,128,128]{2,1,0:T(8,128)(2,1)S(1)}, bf16[4,128,128]{2,1,0:T(8,128)(2,1)S(1)}, u32[]{:S(2)}, u32[]{:S(2)}) %collective-permute-start.19) | collective-permute-done | bytes 131104 | tf_op jit(solution)/shard_map/ppermute | solution.py:244
  60.9 1.4 %collective-permute-start.20 = (bf16[5,128,128]{2,1,0:T(8,128)(2,1)S(1)}, bf16[5,128,128]{2,1,0:T(8,128)(2,1)S(1)}, u32[]{:S(2)}, u32[]{:S(2)}) collective-permute-start(bf16[5,128,128]{2,1,0:T(8,128)(2,1)S(1)} %get-tuple-element.36), channel_id=1, source_target_pairs={{0,1},{1,2},{2,3},{3,0},{4,5},{5,6},{6,7},{7,4},{8,9},{9,10},{10,1... | collective-permute-start | bytes 491528 | tf_op jit(solution)/shard_map/ppermute | solution.py:46
  62.6 0.6 gather_fusion
  63.2 2.1 %collective-permute-start.11 = (bf16[16,320]{1,0:T(8,128)(2,1)S(1)}, bf16[16,320]{1,0:T(8,128)(2,1)S(1)}, u32[]{:S(2)}, u32[]{:S(2)}) collective-permute-start(bf16[16,320]{1,0:T(8,128)(2,1)S(1)} %gather_fusion), channel_id=1, source_target_pairs={{0,8},{1,9},{2,10},{3,11},{4,12},{5,13},{6,14},{7,15},{8,0},{9,1},... | collective-permute-start | bytes 30728 | tf_op jit(solution)/shard_map/ppermute | solution.py:46
  65.3 2.7 %collective-permute-start.12 = (bf16[16,320]{1,0:T(8,128)(2,1)S(1)}, bf16[16,320]{1,0:T(8,128)(2,1)S(1)}, u32[]{:S(2)}, u32[]{:S(2)}) collective-permute-start(bf16[16,320]{1,0:T(8,128)(2,1)S(1)} %gather_fusion), channel_id=1, source_target_pairs={{0,12},{1,13},{2,14},{3,15},{4,0},{5,1},{6,2},{7,3},{8,4},{9,5},{1... | collective-permute-start | bytes 30728 | tf_op jit(solution)/shard_map/ppermute | solution.py:46
  68.0 2.6 %collective-permute-start.21 = (bf16[5,128,128]{2,1,0:T(8,128)(2,1)S(1)}, bf16[5,128,128]{2,1,0:T(8,128)(2,1)S(1)}, u32[]{:S(2)}, u32[]{:S(2)}) collective-permute-start(bf16[5,128,128]{2,1,0:T(8,128)(2,1)S(1)} %get-tuple-element.35), channel_id=1, source_target_pairs={{0,2},{1,3},{2,0},{3,1},{4,6},{5,7},{6,4},{7,5},{8,10},{9,11},{10,... | collective-permute-start | bytes 491528 | tf_op jit(solution)/shard_map/ppermute | solution.py:46
  70.7 1.1 collective-permute-start.15
  72.3 2.3 %collective-permute-start.22 = (bf16[5,128,128]{2,1,0:T(8,128)(2,1)S(1)}, bf16[5,128,128]{2,1,0:T(8,128)(2,1)S(1)}, u32[]{:S(2)}, u32[]{:S(2)}) collective-permute-start(bf16[5,128,128]{2,1,0:T(8,128)(2,1)S(1)} %get-tuple-element.34), channel_id=1, source_target_pairs={{0,3},{1,0},{2,1},{3,2},{4,7},{5,4},{6,5},{7,6},{8,11},{9,8},{10,9... | collective-permute-start | bytes 491528 | tf_op jit(solution)/shard_map/ppermute | solution.py:46
  74.7 2.7 %collective-permute-start.25 = (bf16[10,128,128]{2,1,0:T(8,128)(2,1)S(1)}, bf16[10,128,128]{2,1,0:T(8,128)(2,1)S(1)}, u32[]{:S(2)}, u32[]{:S(2)}) collective-permute-start(bf16[10,128,128]{2,1,0:T(8,128)(2,1)S(1)} %constant_dynamic-update-slice_fusion.12.refs_0_), channel_id=1, source_target_pairs={{0,96},{16,112},{32,0},{48,16},{64,32},{80,48},{96,64},{112,80},{1... | collective-permute-start | bytes 983048 | tf_op jit(solution)/shard_map/ppermute | solution.py:42
  77.4 1.9 %collective-permute-done.22 = bf16[5,128,128]{2,1,0:T(8,128)(2,1)S(1)} collective-permute-done((bf16[5,128,128]{2,1,0:T(8,128)(2,1)S(1)}, bf16[5,128,128]{2,1,0:T(8,128)(2,1)S(1)}, u32[]{:S(2)}, u32[]{:S(2)}) %collective-permute-start.22) | collective-permute-done | bytes 163872 | tf_op jit(solution)/shard_map/ppermute | solution.py:46
  79.3 3.7 %collective-permute-start.23 = (bf16[10,128,128]{2,1,0:T(8,128)(2,1)S(1)}, bf16[10,128,128]{2,1,0:T(8,128)(2,1)S(1)}, u32[]{:S(2)}, u32[]{:S(2)}) collective-permute-start(bf16[10,128,128]{2,1,0:T(8,128)(2,1)S(1)} %constant_dynamic-update-slice_fusion.12.refs_0_), channel_id=1, source_target_pairs={{0,16},{16,0},{32,48},{48,32},{64,80},{80,64},{96,112},{112,96},{1... | collective-permute-start | bytes 983048 | tf_op jit(solution)/shard_map/ppermute | solution.py:42
  83.1 0.6 collective-permute-start.13
  83.7 4.3 %collective-permute-done.13 = bf16[4,16,320]{2,1,0:T(8,128)(2,1)S(1)} collective-permute-done((bf16[4,16,320]{2,1,0:T(8,128)(2,1)S(1)}, bf16[4,16,320]{2,1,0:T(8,128)(2,1)S(1)}, u32[]{:S(2)}, u32[]{:S(2)}) %collective-permute-start.13) | collective-permute-done | bytes 40992 | tf_op jit(solution)/shard_map/ppermute | solution.py:46
  88.0 0.8 collective-permute-start.34
  88.8 1.6 %collective-permute-start.24 = (bf16[10,128,128]{2,1,0:T(8,128)(2,1)S(1)}, bf16[10,128,128]{2,1,0:T(8,128)(2,1)S(1)}, u32[]{:S(2)}, u32[]{:S(2)}) collective-permute-start(bf16[10,128,128]{2,1,0:T(8,128)(2,1)S(1)} %constant_dynamic-update-slice_fusion.28.refs_1_), channel_id=1, source_target_pairs={{0,16},{16,0},{32,48},{48,32},{64,80},{80,64},{96,112},{112,96},{1... | collective-permute-start | bytes 983048 | tf_op jit(solution)/shard_map/ppermute | solution.py:42
  90.9 1.9 %collective-permute-done.26.refs_5_ = bf16[10,128,128]{2,1,0:T(8,128)(2,1)S(1)} collective-permute-done((bf16[10,128,128]{2,1,0:T(8,128)(2,1)S(1)}, bf16[10,128,128]{2,1,0:T(8,128)(2,1)S(1)}, u32[]{:S(2)}, u32[]{:S(2)}) %collective-permute-start.26) | collective-permute-done | bytes 327712 | tf_op jit(solution)/shard_map/ppermute | solution.py:42
  92.9 1.6 %collective-permute-start.31 = (bf16[10,128,128]{2,1,0:T(8,128)(2,1)S(1)}, bf16[10,128,128]{2,1,0:T(8,128)(2,1)S(1)}, u32[]{:S(2)}, u32[]{:S(2)}) collective-permute-start(bf16[10,128,128]{2,1,0:T(8,128)(2,1)S(1)} %collective-permute-done.26.refs_5_), channel_id=1, source_target_pairs={{0,96},{16,112},{32,0},{48,16},{64,32},{80,48},{96,64},{112,80},{1... | collective-permute-start | bytes 983048 | tf_op jit(solution)/shard_map/ppermute | solution.py:42
  94.4 3.4 %collective-permute-done.34.refs_13_ = bf16[10,128,128]{2,1,0:T(8,128)(2,1)S(1)} collective-permute-done((bf16[10,128,128]{2,1,0:T(8,128)(2,1)S(1)}, bf16[10,128,128]{2,1,0:T(8,128)(2,1)S(1)}, u32[]{:S(2)}, u32[]{:S(2)}) %collective-permute-start.34) | collective-permute-done | bytes 327712 | tf_op jit(solution)/shard_map/ppermute | solution.py:42
  97.8 2.6 %collective-permute-start.28 = (bf16[10,128,128]{2,1,0:T(8,128)(2,1)S(1)}, bf16[10,128,128]{2,1,0:T(8,128)(2,1)S(1)}, u32[]{:S(2)}, u32[]{:S(2)}) collective-permute-start(bf16[10,128,128]{2,1,0:T(8,128)(2,1)S(1)} %collective-permute-done.26.refs_5_), channel_id=1, source_target_pairs={{0,16},{16,0},{32,48},{48,32},{64,80},{80,64},{96,112},{112,96},{1... | collective-permute-start | bytes 983048 | tf_op jit(solution)/shard_map/ppermute | solution.py:42
  101.0 3.9 %collective-permute-done.30.refs_8_ = bf16[10,128,128]{2,1,0:T(8,128)(2,1)S(1)} collective-permute-done((bf16[10,128,128]{2,1,0:T(8,128)(2,1)S(1)}, bf16[10,128,128]{2,1,0:T(8,128)(2,1)S(1)}, u32[]{:S(2)}, u32[]{:S(2)}) %collective-permute-start.30) | collective-permute-done | bytes 327712 | tf_op jit(solution)/shard_map/ppermute | solution.py:42
  104.9 1.5 %collective-permute-start.32 = (bf16[10,128,128]{2,1,0:T(8,128)(2,1)S(1)}, bf16[10,128,128]{2,1,0:T(8,128)(2,1)S(1)}, u32[]{:S(2)}, u32[]{:S(2)}) collective-permute-start(bf16[10,128,128]{2,1,0:T(8,128)(2,1)S(1)} %collective-permute-done.30.refs_8_), channel_id=1, source_target_pairs={{0,16},{16,0},{32,48},{48,32},{64,80},{80,64},{96,112},{112,96},{1... | collective-permute-start | bytes 983048 | tf_op jit(solution)/shard_map/ppermute | solution.py:42
  106.5 1.2 collective-permute-done.32.refs_10_
  108.1 9.3 %shard_map.129 = (bf16[5120,512]{1,0:T(8,128)(2,1)}, bf16[16,512]{1,0:T(8,128)(2,1)}) custom-call(s32[6]{0:T(128)S(1)} %stack.51.place, bf16[5120,512]{1,0:T(8,128)(2,1)} %serving.1, bf16[16,16,320]{2,1,0:T(8,128)(2,1)S(1)} %constant_dynamic-update-slice_fusion.features, f32[1,128]{1,0:T(1,128)S(1)} %bitcast.35, ...), custom_call_target="tpu_custom_call" | custom-call | flops 83886080 | bytes 16777216 | tf_op jit(solution)/shard_map/pallas_call | solution.py:176
  (71 shorter events, 3.0 us)
Async XLA Ops:
  3.5 3.1 %collective-permute-start.6 = (bf16[20,128,128]{2,1,0:T(8,128)(2,1)S(1)}, bf16[20,128,128]{2,1,0:T(8,128)(2,1)S(1)}, u32[]{:S(2)}, u32[]{:S(2)}) collective-permute-start(bf16[20,128,128]{2,1,0:T(8,128)(2,1)S(1)} %get-tuple-element.28), channel_id=1, source_target_pairs={{0,16},{16,0},{32,48},{48,32},{64,80},{80,64},{96,112},{112,96},{1... | collective-permute-start | bytes 1966088 | tf_op jit(solution)/shard_map/ppermute | solution.py:42
  4.9 3.6 %collective-permute-start.2 = (bf16[20,128,128]{2,1,0:T(8,128)(2,1)S(1)}, bf16[20,128,128]{2,1,0:T(8,128)(2,1)S(1)}, u32[]{:S(2)}, u32[]{:S(2)}) collective-permute-start(bf16[20,128,128]{2,1,0:T(8,128)(2,1)S(1)} %get-tuple-element.29), channel_id=1, source_target_pairs={{0,16},{16,0},{32,48},{48,32},{64,80},{80,64},{96,112},{112,96},{1... | collective-permute-start | bytes 1966088 | tf_op jit(solution)/shard_map/ppermute | solution.py:42
  4.9 3.7 %collective-permute-start.1 = (bf16[20,128,128]{2,1,0:T(8,128)(2,1)S(1)}, bf16[20,128,128]{2,1,0:T(8,128)(2,1)}, u32[]{:S(2)}, u32[]{:S(2)}) collective-permute-start(bf16[20,128,128]{2,1,0:T(8,128)(2,1)S(1)} %get-tuple-element.30), channel_id=1, source_target_pairs={{0,16},{16,0},{32,48},{48,32},{64,80},{80,64},{96,112},{112,96},{1... | collective-permute-start | bytes 1966088 | tf_op jit(solution)/shard_map/ppermute | solution.py:42
  11.1 10.6 %collective-permute-start.8 = (bf16[20,64,128]{2,1,0:T(8,128)(2,1)S(1)}, bf16[20,64,128]{2,1,0:T(8,128)(2,1)S(1)}, u32[]{:S(2)}, u32[]{:S(2)}) collective-permute-start(bf16[20,64,128]{2,1,0:T(8,128)(2,1)S(1)} %get-tuple-element.32), channel_id=1, source_target_pairs={{0,96},{16,112},{32,0},{48,16},{64,32},{80,48},{96,64},{112,80},{1... | collective-permute-start | bytes 983048 | tf_op jit(solution)/shard_map/ppermute | solution.py:42
  15.0 11.0 %collective-permute-start.3 = (bf16[20,64,128]{2,1,0:T(8,128)(2,1)S(1)}, bf16[20,64,128]{2,1,0:T(8,128)(2,1)S(1)}, u32[]{:S(2)}, u32[]{:S(2)}) collective-permute-start(bf16[20,64,128]{2,1,0:T(8,128)(2,1)S(1)} %get-tuple-element.33), channel_id=1, source_target_pairs={{0,32},{16,48},{32,64},{48,80},{64,96},{80,112},{96,0},{112,16},{1... | collective-permute-start | bytes 983048 | tf_op jit(solution)/shard_map/ppermute | solution.py:42
  15.0 11.9 %collective-permute-start = (bf16[20,128,128]{2,1,0:T(8,128)(2,1)}, bf16[20,128,128]{2,1,0:T(8,128)(2,1)S(1)}, u32[]{:S(2)}, u32[]{:S(2)}) collective-permute-start(bf16[20,128,128]{2,1,0:T(8,128)(2,1)} %get-tuple-element.31), channel_id=1, source_target_pairs={{0,16},{16,0},{32,48},{48,32},{64,80},{80,64},{96,112},{112,96},{1... | collective-permute-start | bytes 1966088 | tf_op jit(solution)/shard_map/ppermute | solution.py:42
  16.4 22.6 %copy-start.1 = (f32[20,128,128]{2,1,0:T(8,128)S(1)}, f32[20,128,128]{2,1,0:T(8,128)}, u32[]{:S(2)}) copy-start(f32[20,128,128]{2,1,0:T(8,128)} %master.1) | copy-start | bytes 3932164
  16.4 22.6 %copy-start.2 = (f32[20,128,128]{2,1,0:T(8,128)S(1)}, f32[20,128,128]{2,1,0:T(8,128)}, u32[]{:S(2)}) copy-start(f32[20,128,128]{2,1,0:T(8,128)} %first.1) | copy-start | bytes 3932164
  16.4 22.6 %copy-start.4 = (s32[20]{0:T(128)S(1)}, s32[20]{0:T(128)}, u32[]{:S(2)}) copy-start(s32[20]{0:T(128)} %marked.1) | copy-start | bytes 244
  17.2 14.8 %collective-permute-start.5 = (bf16[20,64,128]{2,1,0:T(8,128)(2,1)}, bf16[20,64,128]{2,1,0:T(8,128)(2,1)}, u32[]{:S(2)}, u32[]{:S(2)}) collective-permute-start(bf16[20,64,128]{2,1,0:T(8,128)(2,1)} %slice.108), channel_id=1, source_target_pairs={{0,32},{16,48},{32,64},{48,80},{64,96},{80,112},{96,0},{112,16},{1... | collective-permute-start | bytes 983048 | tf_op jit(solution)/shard_map/ppermute | solution.py:42
  17.2 14.8 %collective-permute-start.7 = (bf16[20,64,128]{2,1,0:T(8,128)(2,1)}, bf16[20,64,128]{2,1,0:T(8,128)(2,1)}, u32[]{:S(2)}, u32[]{:S(2)}) collective-permute-start(bf16[20,64,128]{2,1,0:T(8,128)(2,1)} %slice.109), channel_id=1, source_target_pairs={{0,96},{16,112},{32,0},{48,16},{64,32},{80,48},{96,64},{112,80},{1... | collective-permute-start | bytes 983048 | tf_op jit(solution)/shard_map/ppermute | solution.py:42
  22.6 13.3 %collective-permute-start.9 = (bf16[20,64,128]{2,1,0:T(8,128)(2,1)}, bf16[20,64,128]{2,1,0:T(8,128)(2,1)}, u32[]{:S(2)}, u32[]{:S(2)}) collective-permute-start(bf16[20,64,128]{2,1,0:T(8,128)(2,1)} %add_convert_fusion), channel_id=1, source_target_pairs={{0,96},{16,112},{32,0},{48,16},{64,32},{80,48},{96,64},{112,80},{1... | collective-permute-start | bytes 983048 | tf_op jit(solution)/shard_map/ppermute | solution.py:42
  26.8 12.2 %collective-permute-start.4 = (bf16[20,64,128]{2,1,0:T(8,128)(2,1)}, bf16[20,64,128]{2,1,0:T(8,128)(2,1)}, u32[]{:S(2)}, u32[]{:S(2)}) collective-permute-start(bf16[20,64,128]{2,1,0:T(8,128)(2,1)} %add_convert_fusion.1), channel_id=1, source_target_pairs={{0,32},{16,48},{32,64},{48,80},{64,96},{80,112},{96,0},{112,16},{1... | collective-permute-start | bytes 983048 | tf_op jit(solution)/shard_map/ppermute | solution.py:42
  39.0 2.5 %copy-start = (bf16[1,160,128,128]{3,2,1,0:T(8,128)(2,1)S(1)}, bf16[1,160,128,128]{3,2,1,0:T(8,128)(2,1)}, u32[]{:S(2)}) copy-start(bf16[1,160,128,128]{3,2,1,0:T(8,128)(2,1)} %own.1) | copy-start | bytes 15728644
  41.5 1.3 %copy-start.3 = (f32[20,128,128]{2,1,0:T(8,128)S(1)}, f32[20,128,128]{2,1,0:T(8,128)}, u32[]{:S(2)}) copy-start(f32[20,128,128]{2,1,0:T(8,128)} %second.1) | copy-start | bytes 3932164
  48.8 13.4 %copy-start.7 = (s32[16]{0:T(128)S(1)}, s32[16]{0:T(128)}, u32[]{:S(2)}) copy-start(s32[16]{0:T(128)} %param.16) | copy-start | bytes 196
  48.8 13.4 %copy-start.6 = (bf16[1024,320]{0,1:T(8,128)(2,1)S(1)}, bf16[1024,320]{0,1:T(8,128)(2,1)}, u32[]{:S(2)}) copy-start(bf16[1024,320]{0,1:T(8,128)(2,1)} %param.15) | copy-start | bytes 1966084
  48.8 9.4 %collective-permute-start.16 = (bf16[4,128,128]{2,1,0:T(8,128)(2,1)S(1)}, bf16[4,128,128]{2,1,0:T(8,128)(2,1)S(1)}, u32[]{:S(2)}, u32[]{:S(2)}) collective-permute-start(bf16[4,128,128]{2,1,0:T(8,128)(2,1)S(1)} %get-tuple-element.19), channel_id=1, source_target_pairs={{0,4},{1,5},{2,6},{3,7},{4,8},{5,9},{6,10},{7,11},{8,12},{9,13},{1... | collective-permute-start | bytes 393224 | tf_op jit(solution)/shard_map/ppermute | solution.py:46
  50.1 8.1 %collective-permute-start.17 = (bf16[4,128,128]{2,1,0:T(8,128)(2,1)S(1)}, bf16[4,128,128]{2,1,0:T(8,128)(2,1)S(1)}, u32[]{:S(2)}, u32[]{:S(2)}) collective-permute-start(bf16[4,128,128]{2,1,0:T(8,128)(2,1)S(1)} %get-tuple-element.20), channel_id=1, source_target_pairs={{0,8},{1,9},{2,10},{3,11},{4,12},{5,13},{6,14},{7,15},{8,0},{9,1},... | collective-permute-start | bytes 393224 | tf_op jit(solution)/shard_map/ppermute | solution.py:46
  52.6 5.7 %collective-permute-start.18 = (bf16[4,128,128]{2,1,0:T(8,128)(2,1)S(1)}, bf16[4,128,128]{2,1,0:T(8,128)(2,1)S(1)}, u32[]{:S(2)}, u32[]{:S(2)}) collective-permute-start(bf16[4,128,128]{2,1,0:T(8,128)(2,1)S(1)} %get-tuple-element.21), channel_id=1, source_target_pairs={{0,12},{1,13},{2,14},{3,15},{4,0},{5,1},{6,2},{7,3},{8,4},{9,5},{1... | collective-permute-start | bytes 393224 | tf_op jit(solution)/shard_map/ppermute | solution.py:46
  53.7 7.1 %collective-permute-start.19 = (bf16[4,128,128]{2,1,0:T(8,128)(2,1)S(1)}, bf16[4,128,128]{2,1,0:T(8,128)(2,1)S(1)}, u32[]{:S(2)}, u32[]{:S(2)}) collective-permute-start(bf16[4,128,128]{2,1,0:T(8,128)(2,1)S(1)} %get-tuple-element.22), channel_id=1, source_target_pairs={{0,0},{1,1},{2,2},{3,3},{4,16},{5,17},{6,18},{7,19},{8,32},{9,33},... | collective-permute-start | bytes 393224 | tf_op jit(solution)/shard_map/ppermute | solution.py:244
  60.9 13.8 %collective-permute-start.20 = (bf16[5,128,128]{2,1,0:T(8,128)(2,1)S(1)}, bf16[5,128,128]{2,1,0:T(8,128)(2,1)S(1)}, u32[]{:S(2)}, u32[]{:S(2)}) collective-permute-start(bf16[5,128,128]{2,1,0:T(8,128)(2,1)S(1)} %get-tuple-element.36), channel_id=1, source_target_pairs={{0,1},{1,2},{2,3},{3,0},{4,5},{5,6},{6,7},{7,4},{8,9},{9,10},{10,1... | collective-permute-start | bytes 491528 | tf_op jit(solution)/shard_map/ppermute | solution.py:46
  62.2 45.9 %copy-start.5 = (f32[128]{0:T(128)S(1)}, f32[128]{0:T(128)}, u32[]{:S(2)}) copy-start(f32[128]{0:T(128)} %param.17) | copy-start | bytes 1540
  63.2 7.4 %collective-permute-start.11 = (bf16[16,320]{1,0:T(8,128)(2,1)S(1)}, bf16[16,320]{1,0:T(8,128)(2,1)S(1)}, u32[]{:S(2)}, u32[]{:S(2)}) collective-permute-start(bf16[16,320]{1,0:T(8,128)(2,1)S(1)} %gather_fusion), channel_id=1, source_target_pairs={{0,8},{1,9},{2,10},{3,11},{4,12},{5,13},{6,14},{7,15},{8,0},{9,1},... | collective-permute-start | bytes 30728 | tf_op jit(solution)/shard_map/ppermute | solution.py:46
  65.3 5.3 %collective-permute-start.10 = (bf16[16,320]{1,0:T(8,128)(2,1)S(1)}, bf16[16,320]{1,0:T(8,128)(2,1)S(1)}, u32[]{:S(2)}, u32[]{:S(2)}) collective-permute-start(bf16[16,320]{1,0:T(8,128)(2,1)S(1)} %gather_fusion), channel_id=1, source_target_pairs={{0,4},{1,5},{2,6},{3,7},{4,8},{5,9},{6,10},{7,11},{8,12},{9,13},{1... | collective-permute-start | bytes 30728 | tf_op jit(solution)/shard_map/ppermute | solution.py:46
  65.3 5.3 %collective-permute-start.12 = (bf16[16,320]{1,0:T(8,128)(2,1)S(1)}, bf16[16,320]{1,0:T(8,128)(2,1)S(1)}, u32[]{:S(2)}, u32[]{:S(2)}) collective-permute-start(bf16[16,320]{1,0:T(8,128)(2,1)S(1)} %gather_fusion), channel_id=1, source_target_pairs={{0,12},{1,13},{2,14},{3,15},{4,0},{5,1},{6,2},{7,3},{8,4},{9,5},{1... | collective-permute-start | bytes 30728 | tf_op jit(solution)/shard_map/ppermute | solution.py:46
  68.0 6.7 %collective-permute-start.21 = (bf16[5,128,128]{2,1,0:T(8,128)(2,1)S(1)}, bf16[5,128,128]{2,1,0:T(8,128)(2,1)S(1)}, u32[]{:S(2)}, u32[]{:S(2)}) collective-permute-start(bf16[5,128,128]{2,1,0:T(8,128)(2,1)S(1)} %get-tuple-element.35), channel_id=1, source_target_pairs={{0,2},{1,3},{2,0},{3,1},{4,6},{5,7},{6,4},{7,5},{8,10},{9,11},{10,... | collective-permute-start | bytes 491528 | tf_op jit(solution)/shard_map/ppermute | solution.py:46
  70.7 12.3 %collective-permute-start.15 = (bf16[4,16,320]{2,1,0:T(8,128)(2,1)S(1)}, bf16[4,16,320]{2,1,0:T(8,128)(2,1)S(1)}, u32[]{:S(2)}, u32[]{:S(2)}) collective-permute-start(bf16[4,16,320]{2,1,0:T(8,128)(2,1)S(1)} %pad_maximum_fusion), channel_id=1, source_target_pairs={{0,3},{1,0},{2,1},{3,2},{4,7},{5,4},{6,5},{7,6},{8,11},{9,8},{10,9... | collective-permute-start | bytes 122888 | tf_op jit(solution)/shard_map/ppermute | solution.py:46
  71.8 11.3 %collective-permute-start.14 = (bf16[4,16,320]{2,1,0:T(8,128)(2,1)S(1)}, bf16[4,16,320]{2,1,0:T(8,128)(2,1)S(1)}, u32[]{:S(2)}, u32[]{:S(2)}) collective-permute-start(bf16[4,16,320]{2,1,0:T(8,128)(2,1)S(1)} %pad_maximum_fusion), channel_id=1, source_target_pairs={{0,2},{1,3},{2,0},{3,1},{4,6},{5,7},{6,4},{7,5},{8,10},{9,11},{10,... | collective-permute-start | bytes 122888 | tf_op jit(solution)/shard_map/ppermute | solution.py:46
  72.3 7.0 %collective-permute-start.22 = (bf16[5,128,128]{2,1,0:T(8,128)(2,1)S(1)}, bf16[5,128,128]{2,1,0:T(8,128)(2,1)S(1)}, u32[]{:S(2)}, u32[]{:S(2)}) collective-permute-start(bf16[5,128,128]{2,1,0:T(8,128)(2,1)S(1)} %get-tuple-element.34), channel_id=1, source_target_pairs={{0,3},{1,0},{2,1},{3,2},{4,7},{5,4},{6,5},{7,6},{8,11},{9,8},{10,9... | collective-permute-start | bytes 491528 | tf_op jit(solution)/shard_map/ppermute | solution.py:46
  74.6 14.2 %collective-permute-start.29 = (bf16[10,128,128]{2,1,0:T(8,128)(2,1)S(1)}, bf16[10,128,128]{2,1,0:T(8,128)(2,1)S(1)}, u32[]{:S(2)}, u32[]{:S(2)}) collective-permute-start(bf16[10,128,128]{2,1,0:T(8,128)(2,1)S(1)} %constant_dynamic-update-slice_fusion.12.refs_0_), channel_id=1, source_target_pairs={{0,32},{16,48},{32,64},{48,80},{64,96},{80,112},{96,0},{112,16},{1... | collective-permute-start | bytes 983048 | tf_op jit(solution)/shard_map/ppermute | solution.py:42
  74.7 15.7 %collective-permute-start.25 = (bf16[10,128,128]{2,1,0:T(8,128)(2,1)S(1)}, bf16[10,128,128]{2,1,0:T(8,128)(2,1)S(1)}, u32[]{:S(2)}, u32[]{:S(2)}) collective-permute-start(bf16[10,128,128]{2,1,0:T(8,128)(2,1)S(1)} %constant_dynamic-update-slice_fusion.12.refs_0_), channel_id=1, source_target_pairs={{0,96},{16,112},{32,0},{48,16},{64,32},{80,48},{96,64},{112,80},{1... | collective-permute-start | bytes 983048 | tf_op jit(solution)/shard_map/ppermute | solution.py:42
  79.3 11.6 %collective-permute-start.23 = (bf16[10,128,128]{2,1,0:T(8,128)(2,1)S(1)}, bf16[10,128,128]{2,1,0:T(8,128)(2,1)S(1)}, u32[]{:S(2)}, u32[]{:S(2)}) collective-permute-start(bf16[10,128,128]{2,1,0:T(8,128)(2,1)S(1)} %constant_dynamic-update-slice_fusion.12.refs_0_), channel_id=1, source_target_pairs={{0,16},{16,0},{32,48},{48,32},{64,80},{80,64},{96,112},{112,96},{1... | collective-permute-start | bytes 983048 | tf_op jit(solution)/shard_map/ppermute | solution.py:42
  83.0 9.9 %collective-permute-start.26 = (bf16[10,128,128]{2,1,0:T(8,128)(2,1)S(1)}, bf16[10,128,128]{2,1,0:T(8,128)(2,1)S(1)}, u32[]{:S(2)}, u32[]{:S(2)}) collective-permute-start(bf16[10,128,128]{2,1,0:T(8,128)(2,1)S(1)} %constant_dynamic-update-slice_fusion.28.refs_1_), channel_id=1, source_target_pairs={{0,96},{16,112},{32,0},{48,16},{64,32},{80,48},{96,64},{112,80},{1... | collective-permute-start | bytes 983048 | tf_op jit(solution)/shard_map/ppermute | solution.py:42
  83.1 4.9 %collective-permute-start.13 = (bf16[4,16,320]{2,1,0:T(8,128)(2,1)S(1)}, bf16[4,16,320]{2,1,0:T(8,128)(2,1)S(1)}, u32[]{:S(2)}, u32[]{:S(2)}) collective-permute-start(bf16[4,16,320]{2,1,0:T(8,128)(2,1)S(1)} %pad_maximum_fusion), channel_id=1, source_target_pairs={{0,1},{1,2},{2,3},{3,0},{4,5},{5,6},{6,7},{7,4},{8,9},{9,10},{10,1... | collective-permute-start | bytes 122888 | tf_op jit(solution)/shard_map/ppermute | solution.py:46
  88.0 9.8 %collective-permute-start.34 = (bf16[10,128,128]{2,1,0:T(8,128)(2,1)S(1)}, bf16[10,128,128]{2,1,0:T(8,128)(2,1)S(1)}, u32[]{:S(2)}, u32[]{:S(2)}) collective-permute-start(bf16[10,128,128]{2,1,0:T(8,128)(2,1)S(1)} %constant_dynamic-update-slice_fusion.28.refs_1_), channel_id=1, source_target_pairs={{0,32},{16,48},{32,64},{48,80},{64,96},{80,112},{96,0},{112,16},{1... | collective-permute-start | bytes 983048 | tf_op jit(solution)/shard_map/ppermute | solution.py:42
  88.8 11.7 %collective-permute-start.24 = (bf16[10,128,128]{2,1,0:T(8,128)(2,1)S(1)}, bf16[10,128,128]{2,1,0:T(8,128)(2,1)S(1)}, u32[]{:S(2)}, u32[]{:S(2)}) collective-permute-start(bf16[10,128,128]{2,1,0:T(8,128)(2,1)S(1)} %constant_dynamic-update-slice_fusion.28.refs_1_), channel_id=1, source_target_pairs={{0,16},{16,0},{32,48},{48,32},{64,80},{80,64},{96,112},{112,96},{1... | collective-permute-start | bytes 983048 | tf_op jit(solution)/shard_map/ppermute | solution.py:42
  90.4 10.1 %collective-permute-start.35 = (bf16[10,128,128]{2,1,0:T(8,128)(2,1)S(1)}, bf16[10,128,128]{2,1,0:T(8,128)(2,1)S(1)}, u32[]{:S(2)}, u32[]{:S(2)}) collective-permute-start(bf16[10,128,128]{2,1,0:T(8,128)(2,1)S(1)} %collective-permute-done.29.refs_12_), channel_id=1, source_target_pairs={{0,16},{16,0},{32,48},{48,32},{64,80},{80,64},{96,112},{112,96},{1... | collective-permute-start | bytes 983048 | tf_op jit(solution)/shard_map/ppermute | solution.py:42
  90.9 13.9 %collective-permute-start.30 = (bf16[10,128,128]{2,1,0:T(8,128)(2,1)S(1)}, bf16[10,128,128]{2,1,0:T(8,128)(2,1)S(1)}, u32[]{:S(2)}, u32[]{:S(2)}) collective-permute-start(bf16[10,128,128]{2,1,0:T(8,128)(2,1)S(1)} %collective-permute-done.29.refs_12_), channel_id=1, source_target_pairs={{0,32},{16,48},{32,64},{48,80},{64,96},{80,112},{96,0},{112,16},{1... | collective-permute-start | bytes 983048 | tf_op jit(solution)/shard_map/ppermute | solution.py:42
  92.9 13.5 %collective-permute-start.31 = (bf16[10,128,128]{2,1,0:T(8,128)(2,1)S(1)}, bf16[10,128,128]{2,1,0:T(8,128)(2,1)S(1)}, u32[]{:S(2)}, u32[]{:S(2)}) collective-permute-start(bf16[10,128,128]{2,1,0:T(8,128)(2,1)S(1)} %collective-permute-done.26.refs_5_), channel_id=1, source_target_pairs={{0,96},{16,112},{32,0},{48,16},{64,32},{80,48},{96,64},{112,80},{1... | collective-permute-start | bytes 983048 | tf_op jit(solution)/shard_map/ppermute | solution.py:42
  97.8 8.6 %collective-permute-start.28 = (bf16[10,128,128]{2,1,0:T(8,128)(2,1)S(1)}, bf16[10,128,128]{2,1,0:T(8,128)(2,1)S(1)}, u32[]{:S(2)}, u32[]{:S(2)}) collective-permute-start(bf16[10,128,128]{2,1,0:T(8,128)(2,1)S(1)} %collective-permute-done.26.refs_5_), channel_id=1, source_target_pairs={{0,16},{16,0},{32,48},{48,32},{64,80},{80,64},{96,112},{112,96},{1... | collective-permute-start | bytes 983048 | tf_op jit(solution)/shard_map/ppermute | solution.py:42
  100.5 6.0 %collective-permute-start.27 = (bf16[10,128,128]{2,1,0:T(8,128)(2,1)S(1)}, bf16[10,128,128]{2,1,0:T(8,128)(2,1)S(1)}, u32[]{:S(2)}, u32[]{:S(2)}) collective-permute-start(bf16[10,128,128]{2,1,0:T(8,128)(2,1)S(1)} %collective-permute-done.25.refs_4_), channel_id=1, source_target_pairs={{0,16},{16,0},{32,48},{48,32},{64,80},{80,64},{96,112},{112,96},{1... | collective-permute-start | bytes 983048 | tf_op jit(solution)/shard_map/ppermute | solution.py:42
  100.5 6.0 %collective-permute-start.36 = (bf16[10,128,128]{2,1,0:T(8,128)(2,1)S(1)}, bf16[10,128,128]{2,1,0:T(8,128)(2,1)S(1)}, u32[]{:S(2)}, u32[]{:S(2)}) collective-permute-start(bf16[10,128,128]{2,1,0:T(8,128)(2,1)S(1)} %collective-permute-done.34.refs_13_), channel_id=1, source_target_pairs={{0,16},{16,0},{32,48},{48,32},{64,80},{80,64},{96,112},{112,96},{1... | collective-permute-start | bytes 983048 | tf_op jit(solution)/shard_map/ppermute | solution.py:42
  104.9 2.8 %collective-permute-start.32 = (bf16[10,128,128]{2,1,0:T(8,128)(2,1)S(1)}, bf16[10,128,128]{2,1,0:T(8,128)(2,1)S(1)}, u32[]{:S(2)}, u32[]{:S(2)}) collective-permute-start(bf16[10,128,128]{2,1,0:T(8,128)(2,1)S(1)} %collective-permute-done.30.refs_8_), channel_id=1, source_target_pairs={{0,16},{16,0},{32,48},{48,32},{64,80},{80,64},{96,112},{112,96},{1... | collective-permute-start | bytes 983048 | tf_op jit(solution)/shard_map/ppermute | solution.py:42
  106.4 1.7 %collective-permute-start.33 = (bf16[10,128,128]{2,1,0:T(8,128)(2,1)S(1)}, bf16[10,128,128]{2,1,0:T(8,128)(2,1)S(1)}, u32[]{:S(2)}, u32[]{:S(2)}) collective-permute-start(bf16[10,128,128]{2,1,0:T(8,128)(2,1)S(1)} %collective-permute-done.31.refs_9_), channel_id=1, source_target_pairs={{0,16},{16,0},{32,48},{48,32},{64,80},{80,64},{96,112},{112,96},{1... | collective-permute-start | bytes 983048 | tf_op jit(solution)/shard_map/ppermute | solution.py:42

commit v2 on v0

v2 whole, which is shorter than its diff:
```python
import functools

import jax
import jax.numpy as jnp
from jax import lax
from jax.experimental import pallas as pl
from jax.experimental.pallas import tpu as pltpu
from jax.sharding import PartitionSpec as P

beta_one = 0.9
beta_two = 0.999
correct_one = 1.0 - (0.9**10) ** 10
correct_two = 1.0 - (0.999**10) ** 10
adam_eps = 1e-08
learn_rate = 0.001
weight_decay = 0.1

f32 = jnp.float32
bf16 = jnp.bfloat16
MiB = 1024 * 1024

Z_WAY = [(2 * z + c, 2 * ((z + 1 - 2 * c) % 4) + c) for z in range(4) for c in range(2)]
Z_BACK = [(2 * z + c, 2 * ((z + 3 + 2 * c) % 4) + c) for z in range(4) for c in range(2)]
CORE = [(i, i ^ 1) for i in range(8)]
SWAP = [
    (d * 16 + x * 4 + y, (d // 4 * 4 + x) * 16 + (d % 4) * 4 + y)
    for d in range(8)
    for x in range(4)
    for y in range(4)
]


def along_x(s):
    return [(x * 4 + y, (x + s) % 4 * 4 + y) for x in range(4) for y in range(4)]


def along_y(s):
    return [(x * 4 + y, x * 4 + (y + s) % 4) for x in range(4) for y in range(4)]


def on_dp(value, pairs):
    return lax.ppermute(value, "dp", pairs)


def on_mp(value, pairs):
    return lax.ppermute(value, "mp", pairs)


VMEM = pl.BlockSpec(memory_space=pltpu.VMEM)
SMEM = pl.BlockSpec(memory_space=pltpu.SMEM)
ANY = pl.BlockSpec(memory_space=pl.ANY)
BRIEF = pl.CostEstimate(flops=1000, bytes_accessed=1000, transcendentals=0)


def add(*terms):
    return sum(term.astype(f32) for term in terms).astype(bf16)


def tie(value, *earlier):
    return pl.pallas_call(
        lambda *refs: None,
        in_specs=[ANY] * (1 + len(earlier)),
        out_specs=ANY,
        out_shape=jax.ShapeDtypeStruct(value.shape, value.dtype),
        input_output_aliases={0: 0},
        compiler_params=pltpu.CompilerParams(vmem_limit_bytes=MiB),
        cost_estimate=BRIEF,
    )(value, *earlier)


def adam_kernel(place, marked, picked, near, relay, master, first, second, *refs):
    outs, slots = refs[:3], refs[3:]
    step = pl.program_id(0)
    x, y, e = place[1], place[2], place[3]
    to = jnp.where(step == 4, 4, (step + e - x + 4) % 4)
    for block in range(4):
        gradient = near[block] + relay[block].astype(f32)
        weight = master[block]
        first_new = beta_one * first[block] + (1.0 - beta_one) * gradient
        second_new = beta_two * second[block] + (1.0 - beta_two) * gradient * gradient
        update = (
            first_new / correct_one / (jnp.sqrt(second_new / correct_two) + adam_eps)
            + weight_decay * weight
        )
        weight_new = weight - learn_rate * update
        outs[0][block] = weight_new
        outs[1][block] = first_new
        outs[2][block] = second_new
        flag = marked[step * 4 + block]
        fresh = jnp.where(flag == 1, weight_new, jnp.inf).astype(bf16)
        rows = pl.ds(pl.multiple_of((block - y + 4) % 4 * 128, 128), 128)
        for number, slot in enumerate(slots):

            @pl.when(to == number)
            def _():
                slot[rows, :] = fresh

    @pl.when(step == 0)
    def _():
        for slot in slots[:4]:
            for j in range(3):
                slot[512 + 16 * j : 528 + 16 * j, :] = picked[:, 128 * j : 128 * j + 128]


def adam(place, changed, picked, terms, state):
    rows = pl.BlockSpec((4, 128, 128), lambda i, place, marked: (i, 0, 0))

    def whole(height, width):
        return pl.BlockSpec((height, width), lambda i, place, marked: (0, 0))

    heights = (560, 560, 560, 560, 512)
    return pl.pallas_call(
        adam_kernel,
        grid_spec=pltpu.PrefetchScalarGridSpec(
            num_scalar_prefetch=2,
            grid=(5,),
            in_specs=[whole(16, 384)] + [rows] * 5,
            out_specs=[rows] * 3 + [whole(height, 128) for height in heights],
        ),
        out_shape=[jax.ShapeDtypeStruct((20, 128, 128), f32)] * 3
        + [jax.ShapeDtypeStruct((height, 128), bf16) for height in heights],
        compiler_params=pltpu.CompilerParams(vmem_limit_bytes=16 * MiB),
        cost_estimate=BRIEF,
    )(place, changed, picked, *terms, *state)


def origin(place, steps, crossed, u, s):
    x, y, z, core = place[1], place[2], place[4], place[5]
    z_from = (z + steps * (1 - 2 * core) + 4) % 4
    e_from = 2 * (z_from % 2) + (core ^ crossed)
    y_from = (y - u + 4) % 4
    x_from = (x - s + 4) % 4
    late = (e_from > x).astype(jnp.int32)
    t = jnp.where(
        s < 4,
        10 * (4 * x_from + y_from) + e_from + late,
        10 * (4 * e_from + y_from) + x + 1,
    )
    t = t + 5 * (z_from // 2)
    return t // 4, t % 4


def blocks(place, where_from, pieces, body):
    for number, (piece, (steps, crossed)) in enumerate(zip(pieces, where_from)):

        def group(u, carry):
            for s in range(5):
                row, column = origin(place, steps, crossed, u, s)
                i = u * 5 + s
                body(number * 20 + i, None if piece is None else piece[i], row, column)
            return carry

        lax.fori_loop(0, 4, group, 0)


def spot(row, column):
    rows = pl.ds(pl.multiple_of(row * 128, 128), 128)
    return rows, pl.ds(pl.multiple_of(column * 128, 128), 128)


FIRST = ((0, 0), (0, 1))
SECOND = ((-1, 0), (1, 1), (-1, 1), (1, 0))
LAST = ((2, 0), (2, 1))


def first_kernel(place, serving, mine, paired, out, old, sem):
    copy = pltpu.make_async_copy(serving, out, sem)
    copy.start()
    copy.wait()

    def put(i, block, row, column):
        at = spot(row, column)
        out[at] = jnp.where(block == jnp.inf, out[at], block)

    def keep(i, block, row, column):
        at = spot(row, column)
        old[i] = out[at]
        out[at] = jnp.zeros((128, 128), bf16)

    blocks(place, FIRST, (mine, paired), put)
    blocks(place, LAST, (None, None), keep)


def second_kernel(place, picked, *refs):
    pieces, (_, work, out, total, features, sems) = refs[:4], refs[4:]
    features[...] = jnp.zeros((40, 16, 128), bf16)
    for u in range(4):
        for s in range(4):
            at = 4 * ((place[1] - s + 4) % 4) + (place[2] - u + 4) % 4
            tile = 5 * (at // 2) + 2 * (at % 2)
            for j in range(3):
                features[tile + j] += picked[u, pl.ds(s * 48 + j * 16, 16), :]

    def put(i, block, row, column):
        at = spot(row, column)
        work[at] = jnp.where(block == jnp.inf, work[at], block)

    def write(i):
        rows = pl.ds(i * 640, 640)
        return pltpu.make_async_copy(work.at[rows], out.at[rows], sems.at[i])

    blocks(place, SECOND, pieces, put)
    for i in range(8):
        write(i).start()
    query = jnp.zeros((16, 512), f32)
    for i in range(8):
        left = jnp.concatenate([features[5 * i + j] for j in range(5)], axis=1)
        query += jnp.dot(left, work[640 * i : 640 * i + 640, :], preferred_element_type=f32)
    for column in range(4):
        total[column] = query[:, column * 128 : column * 128 + 128]
    for i in range(8):
        write(i).wait()


def last_kernel(
    place, features, gain, before, old, piece, crossed, _, out, scores, total, held, sems
):
    total[...] = before[...]
    writes = []
    for number, (source, (steps, cross)) in enumerate(zip((piece, crossed), LAST)):
        for odd in range(2):
            for wanted in ((0, 1, 2, 3), (4,)):
                first = len(writes)
                left = []
                for s in wanted:
                    for u in (odd, odd + 2):
                        row, column = origin(place, steps, cross, u, s)
                        i, n = u * 5 + s, len(writes)
                        block = source[i]
                        held[n] = jnp.where(block == jnp.inf, old[number * 20 + i], block)
                        to = out.at[spot(row, column)]
                        writes.append(pltpu.make_async_copy(held.at[n], to, sems.at[n]))
                        writes[n].start()
                        left.append(features[row])
                right = held[first : len(writes)].reshape(-1, 128)
                left = jnp.concatenate(left, axis=1)
                total[column] += jnp.dot(left, right, preferred_element_type=f32)
    for head in range(4):
        query = total[head]
        scale = lax.rsqrt(jnp.mean(query * query, axis=-1, keepdims=True) + 1e-06)
        scores[:, head * 128 : head * 128 + 128] = (query * scale * gain[...]).astype(bf16)
    for write in writes:
        write.wait()


SERVING = jax.ShapeDtypeStruct((5120, 512), bf16)
OLD = jax.ShapeDtypeStruct((40, 128, 128), bf16)
FEATURES = jax.ShapeDtypeStruct((40, 16, 128), bf16)
TOTAL = jax.ShapeDtypeStruct((4, 16, 128), f32)
SCORES = jax.ShapeDtypeStruct((16, 512), bf16)


def local(kernel, in_specs, out_specs, out_shape, scratch=(), aliases={}):
    return pl.pallas_call(
        kernel,
        in_specs=in_specs,
        out_specs=out_specs,
        out_shape=out_shape,
        scratch_shapes=scratch,
        input_output_aliases=aliases,
        compiler_params=pltpu.CompilerParams(vmem_limit_bytes=16 * MiB),
        cost_estimate=BRIEF,
    )


def on_device(
    grad_parts,
    master,
    moment_first,
    moment_second,
    serving,
    changed,
    hidden_pool,
    row_ids,
    head_gain,
):
    dp = lax.axis_index("dp")
    mp = lax.axis_index("mp")
    z, core = dp // 2, dp % 2
    x, y = mp // 4, mp % 4
    place = jnp.stack([dp, x, y, dp % 4, z, core]).astype(jnp.int32)

    other = 1 - core
    up = (z + 5 - 2 * core) % 4
    down = (z + 3 + 2 * core) % 4
    opposite = (z + 2) % 4

    picked = jnp.take(hidden_pool, row_ids, axis=0, mode="clip")
    even, odd = (jnp.pad(picked, ((0, 0), ends)) for ends in ((0, 64), (64, 0)))
    picked = jnp.where(y % 2 == 1, odd, even)

    parts = grad_parts.reshape(4, 2, 20, 128, 128)

    def part(chip, c, at=0, count=20):
        start = (chip, c, at, 0, 0)
        return lax.dynamic_slice(parts, start, (1, 1, count, 128, 128))[0, 0]

    def after(*values):
        nonlocal parts
        parts, *values = lax.optimization_barrier((parts, *values))
        return values

    far_out, far_keep = part(opposite, other), part(opposite, core)
    (far_out,) = after(far_out)
    direct_out, relay_out = part(up, other), part(down, other)
    far_in = tie(on_dp(far_out, CORE), direct_out, relay_out)
    (far,) = after(add(far_keep, far_in))
    far = on_dp(far, Z_WAY)
    direct_in = tie(on_dp(direct_out, CORE), picked)
    (direct,) = after(add(part(down, core), direct_in))
    (relay,) = after(add(part(up, core), on_dp(relay_out, CORE)))
    far = tie(far, direct, relay)
    direct = on_dp(direct, Z_BACK)
    relay = on_dp(add(relay, far), Z_WAY)
    own, own_out = after(part(z, core), part(z, other))
    near = own.astype(f32) + on_dp(own_out, CORE).astype(f32) + direct.astype(f32)

    state = (master, moment_first, moment_second)
    *state_new, row0, row1, row2, row3, extra = adam(
        place, changed, picked, (near, relay), state
    )

    extra = lax.ppermute(extra, ("dp", "mp"), SWAP)
    row = [row0] + [on_mp(r, along_x(s)) for s, r in ((1, row1), (2, row2), (3, row3))]
    plane, features = [], []
    for u in range(4):
        group = [r[128 * u : 128 * u + 128] for r in row + [extra]]
        group = jnp.concatenate(group + [r[512:] for r in row])
        if u:
            group = on_mp(group, along_y(u))
        plane.append(group[:640])
        features.append(group[640:])
    features = jnp.stack(features)
    mine = jnp.concatenate(plane).reshape(20, 128, 128)

    near = on_dp(mine, Z_WAY)
    paired = on_dp(mine, CORE)
    near_paired = on_dp(paired, Z_WAY)

    work, old = local(
        first_kernel,
        [SMEM, ANY, VMEM, VMEM],
        [VMEM] * 2,
        [SERVING, OLD],
        [pltpu.SemaphoreType.DMA(())],
    )(place, serving, mine, paired)
    near = tie(near, old)
    far = on_dp(near, Z_WAY)
    pieces = (near, on_dp(near, CORE), near_paired, on_dp(near_paired, CORE))
    _, out, total, features = local(
        second_kernel,
        [SMEM] + [VMEM] * 6,
        [VMEM, ANY, VMEM, VMEM],
        [SERVING, SERVING, TOTAL, FEATURES],
        [pltpu.SemaphoreType.DMA((8,))],
        {6: 0},
    )(place, features, *pieces, work)
    far = tie(far, total)
    serving_new, scores = local(
        last_kernel,
        [SMEM] + [VMEM] * 6 + [ANY],
        [ANY, VMEM],
        [SERVING, SCORES],
        [
            pltpu.VMEM(TOTAL.shape, f32),
            pltpu.VMEM(OLD.shape, bf16),
            pltpu.SemaphoreType.DMA((40,)),
        ],
        {7: 0},
    )(
        place,
        features,
        head_gain.reshape(1, 128),
        total,
        old,
        far,
        on_dp(far, CORE),
        out,
    )
    return (*state_new, serving_new, scores)


def solution(mesh):
    return jax.shard_map(
        on_device,
        mesh=mesh,
        in_specs=(
            P("dp", "mp", None, None),
            P(("mp", "dp"), None, None),
            P(("mp", "dp"), None, None),
            P(("mp", "dp"), None, None),
            P(None, "mp"),
            P(("mp", "dp")),
            P(None, "mp"),
            P("dp"),
            P(),
        ),
        out_specs=(
            P(("mp", "dp"), None, None),
            P(("mp", "dp"), None, None),
            P(("mp", "dp"), None, None),
            P(None, "mp"),
            P("dp", "mp"),
        ),
        check_vma=False,
    )
```

time: 268 us -> 103 us (0.38)
  the two profiles are of different devices: /device:TPU:32 before, /device:TPU:1 now
where the time goes in v2:
time: 103 us
  starting transfers between devices  38 us (37%)
  waiting for transfers between devices  36.3 us (35%)
  Pallas kernels  14.8 us (14%)
  local copies, waits for them, and re-layouts  6.78 us (7%)
  other arithmetic  5.81 us (6%)
  between operations  1.05 us (1%)
    ppermute x14, waiting for transfers between devices, on_dp(): return lax.ppermute(value, 'dp', pairs)  24.7 us
    ppermute x14, starting transfers between devices, on_dp(): return lax.ppermute(value, 'dp', pairs)  23.7 us
    ppermute x6, waiting for transfers between devices, on_mp(): return lax.ppermute(value, 'mp', pairs)  8.97 us
    ppermute x6, starting transfers between devices, on_mp(): return lax.ppermute(value, 'mp', pairs)  8.05 us
    ppermute x1, starting transfers between devices, on_device(): extra = lax.ppermute(extra, ('dp', 'mp'), SWAP)  6.19 us
    pallas_call x1, Pallas kernels, on_device(): local(second_kernel, [SMEM] + [VMEM] * 6, [VMEM, ANY, VMEM, VMEM], [SERVI...  4.83 us
    squeeze x3, local copies, waits for them, and re-layouts, part(): return lax.dynamic_slice(parts, start, (1, 1, count, 128, 128))[0, 0]  4.37 us
    pallas_call x1, Pallas kernels, adam(): pl.pallas_call(adam_kernel, grid_spec=pltpu.PrefetchScalarGridSpec(num_sc...  4.25 us
  transfers between devices with their start and end apart: 21, of which 10 were waited for; matrix products, arithmetic and copies ran while one was open for 10% of the time, Pallas kernels for 7%

profile of v2, /device:TPU:1, one launch (start us, length us, event | category | flops | bytes accessed | tf_op | source)
XLA Modules:
  0.0 102.7 jit_solution(16781727245029938194)
XLA Ops:
  0.7 2.0 %dynamic-slice_bitcast_fusion.4 = bf16[20,128,128]{2,1,0:T(8,128)(2,1)} fusion(bf16[4,2,20,128,128]{4,3,2,1,0:T(8,128)(2,1)} %bitcast.42, s32[]{:T(128)S(6)} %select_n.83, s32[]{:T(128)S(6)} %select_n.84), kind=kLoop, calls=%fused_computation.13 | loop fusion | bytes 1310728 | tf_op jit(solution)/shard_map/squeeze | solution.py:296
  2.7 1.4 %collective-permute-start = (bf16[20,128,128]{2,1,0:T(8,128)(2,1)}, bf16[20,128,128]{2,1,0:T(8,128)(2,1)S(1)}, u32[]{:S(2)}, u32[]{:S(2)}) collective-permute-start(bf16[20,128,128]{2,1,0:T(8,128)(2,1)} %dynamic-slice_bitcast_fusion.4), channel_id=1, source_target_pairs={{0,16},{16,0},{32,48},{48,32},{64,80},{80,64},{96,112},{112,96},{1... | collective-permute-start | bytes 1966088 | tf_op jit(solution)/shard_map/ppermute | solution.py:42
  4.1 1.4 %dynamic-slice_bitcast_fusion.2 = (bf16[20,128,128]{2,1,0:T(8,128)(2,1)S(1)}, bf16[20,128,128]{2,1,0:T(8,128)(2,1)S(1)}) fusion(bf16[4,2,20,128,128]{4,3,2,1,0:T(8,128)(2,1)} %bitcast.43, s32[]{:T(128)S(6)} %select_n.89, s32[]{:T(128)S(6)} %select_n.84, s32[]{:T(128)S(6)} %select_n.87), kind=kLoop, calls=%fused_computation.11 | loop fusion | bytes 2621452 | tf_op jit(solution)/shard_map/squeeze | solution.py:296
  5.5 0.1 collective-permute-start.1
  5.6 0.5 collective-permute-start.2
  6.1 1.4 %copy.21 = bf16[1024,320]{1,0:T(8,128)(2,1)S(1)} copy(bf16[1024,320]{0,1:T(8,128)(2,1)} %param.15) | data formatting | bytes 1310720 | tf_op args[6]
  7.6 0.6 gather_fusion
  8.2 0.1 pad_select_fusion.refs_1_.picked
  8.3 1.4 %fusion.2 = bf16[20,128,128]{2,1,0:T(8,128)(2,1)S(1)} fusion(bf16[20,128,128]{2,1,0:T(8,128)(2,1)S(1)} %shard_map.128, bf16[4,2,20,128,128]{4,3,2,1,0:T(8,128)(2,1)} %bitcast.44, s32[]{:T(128)S(6)} %select_n.83, s32[]{:T(128)S(6)} %select_n.85), kind=kLoop, calls=%fused_computation.6 | loop fusion | flops 1310720 | bytes 1966088 | tf_op jit(solution)/shard_map/convert_element_type | solution.py:56
  9.7 3.9 %collective-permute-start.5 = (bf16[20,128,128]{2,1,0:T(8,128)(2,1)S(1)}, bf16[20,128,128]{2,1,0:T(8,128)(2,1)S(1)}, u32[]{:S(2)}, u32[]{:S(2)}) collective-permute-start(bf16[20,128,128]{2,1,0:T(8,128)(2,1)S(1)} %fusion.2), channel_id=1, source_target_pairs={{0,32},{16,112},{32,64},{48,16},{64,96},{80,48},{96,0},{112,80},{1... | collective-permute-start | bytes 1966088 | tf_op jit(solution)/shard_map/ppermute | solution.py:42
  13.6 0.2 fusion.1.refs_1_
  13.8 0.1 collective-permute-start.4
  13.9 1.3 %fusion.refs_2_ = bf16[20,128,128]{2,1,0:T(8,128)(2,1)S(1)} fusion(bf16[20,128,128]{2,1,0:T(8,128)(2,1)} %collective-permute-done.2, bf16[4,2,20,128,128]{4,3,2,1,0:T(8,128)(2,1)S(1)} %bitcast.46, s32[]{:T(128)S(6)} %select_n.87, s32[]{:T(128)S(6)} %select_n.85), kind=kLoop, calls=%fused_computation.2 | loop fusion | flops 1310720 | bytes 1966088 | tf_op jit(solution)/shard_map/convert_element_type | solution.py:56
  15.2 1.0 dynamic-slice_bitcast_fusion
  16.2 1.5 %collective-permute-start.3 = (bf16[20,128,128]{2,1,0:T(8,128)(2,1)}, bf16[20,128,128]{2,1,0:T(8,128)(2,1)}, u32[]{:S(2)}, u32[]{:S(2)}) collective-permute-start(bf16[20,128,128]{2,1,0:T(8,128)(2,1)} %get-tuple-element.36), channel_id=1, source_target_pairs={{0,16},{16,0},{32,48},{48,32},{64,80},{80,64},{96,112},{112,96},{1... | collective-permute-start | bytes 1966088 | tf_op jit(solution)/shard_map/ppermute | solution.py:42
  17.7 8.4 %collective-permute-done.5.refs_0_ = bf16[20,128,128]{2,1,0:T(8,128)(2,1)S(1)} collective-permute-done((bf16[20,128,128]{2,1,0:T(8,128)(2,1)S(1)}, bf16[20,128,128]{2,1,0:T(8,128)(2,1)S(1)}, u32[]{:S(2)}, u32[]{:S(2)}) %collective-permute-start.5) | collective-permute-done | bytes 655392 | tf_op jit(solution)/shard_map/ppermute | solution.py:42
  26.1 1.1 %add_convert_fusion = bf16[20,128,128]{2,1,0:T(8,128)(2,1)} fusion(bf16[20,128,128]{2,1,0:T(8,128)(2,1)S(1)} %shard_map.130, bf16[20,128,128]{2,1,0:T(8,128)(2,1)S(1)} %fusion.refs_2_), kind=kLoop, calls=%fused_computation.7 | loop fusion | flops 1310720 | bytes 1966080 | tf_op jit(solution)/shard_map/convert_element_type | solution.py:56
  27.2 3.5 %collective-permute-start.6 = (bf16[20,128,128]{2,1,0:T(8,128)(2,1)}, bf16[20,128,128]{2,1,0:T(8,128)(2,1)S(1)}, u32[]{:S(2)}, u32[]{:S(2)}) collective-permute-start(bf16[20,128,128]{2,1,0:T(8,128)(2,1)} %add_convert_fusion), channel_id=1, source_target_pairs={{0,32},{16,112},{32,64},{48,16},{64,96},{80,48},{96,0},{112,80},{1... | collective-permute-start | bytes 1966088 | tf_op jit(solution)/shard_map/ppermute | solution.py:42
  30.7 0.1 stack.42.place
  30.8 1.7 %convert_add_fusion.3.near = f32[20,128,128]{2,1,0:T(8,128)S(1)} fusion(bf16[20,128,128]{2,1,0:T(8,128)(2,1)} %collective-permute-done.4, bf16[20,128,128]{2,1,0:T(8,128)(2,1)} %collective-permute-done.3, bf16[20,128,128]{2,1,0:T(8,128)(2,1)S(1)} %get-tuple-element.35), kind=kLoop, calls=%fused_computation.8 | loop fusion | flops 1638400 | bytes 3276800 | tf_op jit(solution)/shard_map/add | solution.py:316
  32.6 0.0 slice-start.1
  32.6 6.0 %collective-permute-done.6.relay = bf16[20,128,128]{2,1,0:T(8,128)(2,1)S(1)} collective-permute-done((bf16[20,128,128]{2,1,0:T(8,128)(2,1)}, bf16[20,128,128]{2,1,0:T(8,128)(2,1)S(1)}, u32[]{:S(2)}, u32[]{:S(2)}) %collective-permute-start.6) | collective-permute-done | bytes 655392 | tf_op jit(solution)/shard_map/ppermute | solution.py:42
  38.6 4.3 %shard_map.131 = (f32[20,128,128]{2,1,0:T(8,128)}, f32[20,128,128]{2,1,0:T(8,128)}, f32[20,128,128]{2,1,0:T(8,128)}, bf16[560,128]{1,0:T(8,128)(2,1)S(1)}, bf16[...) custom-call(s32[6]{0:T(128)S(1)} %stack.42.place, ...), custom_call_target="tpu_custom_call" | custom-call | flops 1000 | bytes 1000 | tf_op jit(solution)/shard_map/pallas_call | solution.py:112
  42.8 2.5 %collective-permute-start.9 = (bf16[560,128]{1,0:T(8,128)(2,1)S(1)}, bf16[560,128]{1,0:T(8,128)(2,1)S(1)}, u32[]{:S(2)}, u32[]{:S(2)}) collective-permute-start(bf16[560,128]{1,0:T(8,128)(2,1)S(1)} %get-tuple-element.46), channel_id=1, source_target_pairs={{0,12},{1,13},{2,14},{3,15},{4,0},{5,1},{6,2},{7,3},{8,4},{9,5},{1... | collective-permute-start | bytes 430088 | tf_op jit(solution)/shard_map/ppermute | solution.py:46
  45.3 0.5 collective-permute-start.8
  45.8 0.6 collective-permute-start.7
  46.4 6.2 %collective-permute-start.10 = (bf16[512,128]{1,0:T(8,128)(2,1)S(1)}, bf16[512,128]{1,0:T(8,128)(2,1)S(1)}, u32[]{:S(2)}, u32[]{:S(2)}) collective-permute-start(bf16[512,128]{1,0:T(8,128)(2,1)S(1)} %get-tuple-element.47), channel_id=1, source_target_pairs={{0,0},{1,1},{2,2},{3,3},{4,16},{5,17},{6,18},{7,19},{8,32},{9,33},... | collective-permute-start | bytes 393224 | tf_op jit(solution)/shard_map/ppermute | solution.py:323
  52.6 0.2 collective-permute-done.7
  52.9 2.6 %collective-permute-done.10 = bf16[512,128]{1,0:T(8,128)(2,1)S(1)} collective-permute-done((bf16[512,128]{1,0:T(8,128)(2,1)S(1)}, bf16[512,128]{1,0:T(8,128)(2,1)S(1)}, u32[]{:S(2)}, u32[]{:S(2)}) %collective-permute-start.10) | collective-permute-done | bytes 131104 | tf_op jit(solution)/shard_map/ppermute | solution.py:323
  55.7 1.4 %collective-permute-start.11 = (bf16[832,128]{1,0:T(8,128)(2,1)S(1)}, bf16[832,128]{1,0:T(8,128)(2,1)S(1)}, u32[]{:S(2)}, u32[]{:S(2)}) collective-permute-start(bf16[832,128]{1,0:T(8,128)(2,1)S(1)} %get-tuple-element.88), channel_id=1, source_target_pairs={{0,1},{1,2},{2,3},{3,0},{4,5},{5,6},{6,7},{7,4},{8,9},{9,10},{10,1... | collective-permute-start | bytes 638984 | tf_op jit(solution)/shard_map/ppermute | solution.py:46
  57.0 1.5 %collective-permute-start.13 = (bf16[832,128]{1,0:T(8,128)(2,1)S(1)}, bf16[832,128]{1,0:T(8,128)(2,1)S(1)}, u32[]{:S(2)}, u32[]{:S(2)}) collective-permute-start(bf16[832,128]{1,0:T(8,128)(2,1)S(1)} %get-tuple-element.90), channel_id=1, source_target_pairs={{0,3},{1,0},{2,1},{3,2},{4,7},{5,4},{6,5},{7,6},{8,11},{9,8},{10,9... | collective-permute-start | bytes 638984 | tf_op jit(solution)/shard_map/ppermute | solution.py:46
  58.5 1.6 %collective-permute-start.12 = (bf16[832,128]{1,0:T(8,128)(2,1)S(1)}, bf16[832,128]{1,0:T(8,128)(2,1)S(1)}, u32[]{:S(2)}, u32[]{:S(2)}) collective-permute-start(bf16[832,128]{1,0:T(8,128)(2,1)S(1)} %get-tuple-element.89), channel_id=1, source_target_pairs={{0,2},{1,3},{2,0},{3,1},{4,6},{5,7},{6,4},{7,5},{8,10},{9,11},{10,... | collective-permute-start | bytes 638984 | tf_op jit(solution)/shard_map/ppermute | solution.py:46
  60.1 3.1 %collective-permute-done.11 = bf16[832,128]{1,0:T(8,128)(2,1)S(1)} collective-permute-done((bf16[832,128]{1,0:T(8,128)(2,1)S(1)}, bf16[832,128]{1,0:T(8,128)(2,1)S(1)}, u32[]{:S(2)}, u32[]{:S(2)}) %collective-permute-start.11) | collective-permute-done | bytes 213024 | tf_op jit(solution)/shard_map/ppermute | solution.py:46
  63.3 5.6 %collective-permute-done.12 = bf16[832,128]{1,0:T(8,128)(2,1)S(1)} collective-permute-done((bf16[832,128]{1,0:T(8,128)(2,1)S(1)}, bf16[832,128]{1,0:T(8,128)(2,1)S(1)}, u32[]{:S(2)}, u32[]{:S(2)}) %collective-permute-start.12) | collective-permute-done | bytes 213024 | tf_op jit(solution)/shard_map/ppermute | solution.py:46
  69.0 1.6 %collective-permute-start.15 = (bf16[20,128,128]{2,1,0:T(8,128)(2,1)S(1)}, bf16[20,128,128]{2,1,0:T(8,128)(2,1)S(1)}, u32[]{:S(2)}, u32[]{:S(2)}) collective-permute-start(bf16[20,128,128]{2,1,0:T(8,128)(2,1)S(1)} %bitcast.38), channel_id=1, source_target_pairs={{0,16},{16,0},{32,48},{48,32},{64,80},{80,64},{96,112},{112,96},{1... | collective-permute-start | bytes 1966088 | tf_op jit(solution)/shard_map/ppermute | solution.py:42
  70.6 4.4 %collective-permute-start.14 = (bf16[20,128,128]{2,1,0:T(8,128)(2,1)S(1)}, bf16[20,128,128]{2,1,0:T(8,128)(2,1)S(1)}, u32[]{:S(2)}, u32[]{:S(2)}) collective-permute-start(bf16[20,128,128]{2,1,0:T(8,128)(2,1)S(1)} %bitcast.39), channel_id=1, source_target_pairs={{0,32},{16,112},{32,64},{48,16},{64,96},{80,48},{96,0},{112,80},{1... | collective-permute-start | bytes 1966088 | tf_op jit(solution)/shard_map/ppermute | solution.py:42
  75.0 1.7 %collective-permute-start.17 = (bf16[20,128,128]{2,1,0:T(8,128)(2,1)S(1)}, bf16[20,128,128]{2,1,0:T(8,128)(2,1)S(1)}, u32[]{:S(2)}, u32[]{:S(2)}) collective-permute-start(bf16[20,128,128]{2,1,0:T(8,128)(2,1)S(1)} %collective-permute-done.15.paired), channel_id=1, source_target_pairs={{0,32},{16,112},{32,64},{48,16},{64,96},{80,48},{96,0},{112,80},{1... | collective-permute-start | bytes 1966088 | tf_op jit(solution)/shard_map/ppermute | solution.py:42
  76.7 2.7 %shard_map.132 = (bf16[5120,512]{1,0:T(8,128)(2,1)S(1)}, bf16[40,128,128]{2,1,0:T(8,128)(2,1)S(1)}) custom-call(s32[6]{0:T(128)S(1)} %stack.42.place, bf16[5120,512]{1,0:T(8,128)(2,1)S(1)} %bitcast.37, bf16[20,128,128]{2,1,0:T(8,128)(2,1)S(1)} %bitcast.40, bf16[20,128,128]{2,1,0:T(8,128)(2,1)S(1)} %collective-permute-done.15.paired), custom_call_target="tpu_custom_call" | custom-call | flops 1000 | bytes 1000 | tf_op jit(solution)/shard_map/pallas_call | solution.py:340
  79.5 3.1 %collective-permute-done.14.refs_0_ = bf16[20,128,128]{2,1,0:T(8,128)(2,1)S(1)} collective-permute-done((bf16[20,128,128]{2,1,0:T(8,128)(2,1)S(1)}, bf16[20,128,128]{2,1,0:T(8,128)(2,1)S(1)}, u32[]{:S(2)}, u32[]{:S(2)}) %collective-permute-start.14) | collective-permute-done | bytes 655392 | tf_op jit(solution)/shard_map/ppermute | solution.py:42
  82.5 1.4 %collective-permute-start.16 = (bf16[20,128,128]{2,1,0:T(8,128)(2,1)S(1)}, bf16[20,128,128]{2,1,0:T(8,128)(2,1)S(1)}, u32[]{:S(2)}, u32[]{:S(2)}) collective-permute-start(bf16[20,128,128]{2,1,0:T(8,128)(2,1)S(1)} %shard_map.133.refs_0_), channel_id=1, source_target_pairs={{0,16},{16,0},{32,48},{48,32},{64,80},{80,64},{96,112},{112,96},{1... | collective-permute-start | bytes 1966088 | tf_op jit(solution)/shard_map/ppermute | solution.py:42
  83.9 1.7 %collective-permute-start.19 = (bf16[20,128,128]{2,1,0:T(8,128)(2,1)S(1)}, bf16[20,128,128]{2,1,0:T(8,128)(2,1)S(1)}, u32[]{:S(2)}, u32[]{:S(2)}) collective-permute-start(bf16[20,128,128]{2,1,0:T(8,128)(2,1)S(1)} %shard_map.133.refs_0_), channel_id=1, source_target_pairs={{0,32},{16,112},{32,64},{48,16},{64,96},{80,48},{96,0},{112,80},{1... | collective-permute-start | bytes 1966088 | tf_op jit(solution)/shard_map/ppermute | solution.py:42
  85.7 3.9 %collective-permute-done.17.refs_2_ = bf16[20,128,128]{2,1,0:T(8,128)(2,1)S(1)} collective-permute-done((bf16[20,128,128]{2,1,0:T(8,128)(2,1)S(1)}, bf16[20,128,128]{2,1,0:T(8,128)(2,1)S(1)}, u32[]{:S(2)}, u32[]{:S(2)}) %collective-permute-start.17) | collective-permute-done | bytes 655392 | tf_op jit(solution)/shard_map/ppermute | solution.py:42
  89.6 1.4 %collective-permute-start.18 = (bf16[20,128,128]{2,1,0:T(8,128)(2,1)S(1)}, bf16[20,128,128]{2,1,0:T(8,128)(2,1)S(1)}, u32[]{:S(2)}, u32[]{:S(2)}) collective-permute-start(bf16[20,128,128]{2,1,0:T(8,128)(2,1)S(1)} %collective-permute-done.17.refs_2_), channel_id=1, source_target_pairs={{0,16},{16,0},{32,48},{48,32},{64,80},{80,64},{96,112},{112,96},{1... | collective-permute-start | bytes 1966088 | tf_op jit(solution)/shard_map/ppermute | solution.py:42
  91.0 1.7 %collective-permute-done.18.refs_3_ = bf16[20,128,128]{2,1,0:T(8,128)(2,1)S(1)} collective-permute-done((bf16[20,128,128]{2,1,0:T(8,128)(2,1)S(1)}, bf16[20,128,128]{2,1,0:T(8,128)(2,1)S(1)}, u32[]{:S(2)}, u32[]{:S(2)}) %collective-permute-start.18) | collective-permute-done | bytes 655392 | tf_op jit(solution)/shard_map/ppermute | solution.py:42
  92.7 4.8 %shard_map.134 = (bf16[5120,512]{1,0:T(8,128)(2,1)S(1)}, bf16[5120,512]{1,0:T(8,128)(2,1)}, f32[4,16,128]{2,1,0:T(8,128)S(1)}, bf16[40,16,128]{2,1,0:T(8,128)(2,1)S(1)}) custom-call(s32[6]{0:T(128)S(1)} %stack.42.place, bf16[4,192,128]{2,1,0:T(8,128)(2,1)S(1)} %pad_maximum_fusion.picked, ...), custom_call_target="tpu_custom_call", output_to_operand_aliasing={{0}: (6, {})} | custom-call | flops 1000 | bytes 1000 | tf_op jit(solution)/shard_map/pallas_call | solution.py:350
  97.5 0.5 collective-permute-start.20
  98.0 1.7 %collective-permute-done.20.crossed = bf16[20,128,128]{2,1,0:T(8,128)(2,1)S(1)} collective-permute-done((bf16[20,128,128]{2,1,0:T(8,128)(2,1)S(1)}, bf16[20,128,128]{2,1,0:T(8,128)(2,1)S(1)}, u32[]{:S(2)}, u32[]{:S(2)}) %collective-permute-start.20) | collective-permute-done | bytes 655392 | tf_op jit(solution)/shard_map/ppermute | solution.py:42
  99.7 3.0 %shard_map.136 = (bf16[5120,512]{1,0:T(8,128)(2,1)}, bf16[16,512]{1,0:T(8,128)(2,1)}) custom-call(s32[6]{0:T(128)S(1)} %stack.42.place, bf16[40,16,128]{2,1,0:T(8,128)(2,1)S(1)} %get-tuple-element.50.features, f32[1,128]{1,0:T(1,128)S(1)} %bitcast.41, f32[4,16,128]{2,1,0:T(8,128)S(1)} %get-tuple-element.51.refs_1_.before, ...), custom_call_target="tpu_custom_call", output_to_operand_aliasing={{0}: (7, {})} | custom-call | flops 1000 | bytes 1000 | tf_op jit(solution)/shard_map/pallas_call | solution.py:359
  (52 shorter events, 0.4 us)
Async XLA Ops:
  2.7 5.6 %collective-permute-start = (bf16[20,128,128]{2,1,0:T(8,128)(2,1)}, bf16[20,128,128]{2,1,0:T(8,128)(2,1)S(1)}, u32[]{:S(2)}, u32[]{:S(2)}) collective-permute-start(bf16[20,128,128]{2,1,0:T(8,128)(2,1)} %dynamic-slice_bitcast_fusion.4), channel_id=1, source_target_pairs={{0,16},{16,0},{32,48},{48,32},{64,80},{80,64},{96,112},{112,96},{1... | collective-permute-start | bytes 1966088 | tf_op jit(solution)/shard_map/ppermute | solution.py:42
  4.1 2.0 %copy-start.6 = (s32[16]{0:T(128)S(1)}, s32[16]{0:T(128)}, u32[]{:S(2)}) copy-start(s32[16]{0:T(128)} %param.16) | copy-start | bytes 196
  5.5 8.1 %collective-permute-start.1 = (bf16[20,128,128]{2,1,0:T(8,128)(2,1)S(1)}, bf16[20,128,128]{2,1,0:T(8,128)(2,1)S(1)}, u32[]{:S(2)}, u32[]{:S(2)}) collective-permute-start(bf16[20,128,128]{2,1,0:T(8,128)(2,1)S(1)} %get-tuple-element.58.refs_1_), channel_id=1, source_target_pairs={{0,16},{16,0},{32,48},{48,32},{64,80},{80,64},{96,112},{112,96},{1... | collective-permute-start | bytes 1966088 | tf_op jit(solution)/shard_map/ppermute | solution.py:42
  5.6 8.3 %collective-permute-start.2 = (bf16[20,128,128]{2,1,0:T(8,128)(2,1)S(1)}, bf16[20,128,128]{2,1,0:T(8,128)(2,1)}, u32[]{:S(2)}, u32[]{:S(2)}) collective-permute-start(bf16[20,128,128]{2,1,0:T(8,128)(2,1)S(1)} %get-tuple-element.57.refs_2_), channel_id=1, source_target_pairs={{0,16},{16,0},{32,48},{48,32},{64,80},{80,64},{96,112},{112,96},{1... | collective-permute-start | bytes 1966088 | tf_op jit(solution)/shard_map/ppermute | solution.py:42
  8.3 5.4 %copy-start.5 = (bf16[1,160,128,128]{3,2,1,0:T(8,128)(2,1)S(1)}, bf16[1,160,128,128]{3,2,1,0:T(8,128)(2,1)}, u32[]{:S(2)}) copy-start(bf16[1,160,128,128]{3,2,1,0:T(8,128)(2,1)} %param.9) | copy-start | bytes 15728644
  9.7 16.4 %collective-permute-start.5 = (bf16[20,128,128]{2,1,0:T(8,128)(2,1)S(1)}, bf16[20,128,128]{2,1,0:T(8,128)(2,1)S(1)}, u32[]{:S(2)}, u32[]{:S(2)}) collective-permute-start(bf16[20,128,128]{2,1,0:T(8,128)(2,1)S(1)} %fusion.2), channel_id=1, source_target_pairs={{0,32},{16,112},{32,64},{48,16},{64,96},{80,48},{96,0},{112,80},{1... | collective-permute-start | bytes 1966088 | tf_op jit(solution)/shard_map/ppermute | solution.py:42
  13.8 17.0 %collective-permute-start.4 = (bf16[20,128,128]{2,1,0:T(8,128)(2,1)S(1)}, bf16[20,128,128]{2,1,0:T(8,128)(2,1)}, u32[]{:S(2)}, u32[]{:S(2)}) collective-permute-start(bf16[20,128,128]{2,1,0:T(8,128)(2,1)S(1)} %fusion.1.refs_1_), channel_id=1, source_target_pairs={{0,96},{16,48},{32,0},{48,80},{64,32},{80,112},{96,64},{112,16},{1... | collective-permute-start | bytes 1966088 | tf_op jit(solution)/shard_map/ppermute | solution.py:42
  16.2 14.6 %collective-permute-start.3 = (bf16[20,128,128]{2,1,0:T(8,128)(2,1)}, bf16[20,128,128]{2,1,0:T(8,128)(2,1)}, u32[]{:S(2)}, u32[]{:S(2)}) collective-permute-start(bf16[20,128,128]{2,1,0:T(8,128)(2,1)} %get-tuple-element.36), channel_id=1, source_target_pairs={{0,16},{16,0},{32,48},{48,32},{64,80},{80,64},{96,112},{112,96},{1... | collective-permute-start | bytes 1966088 | tf_op jit(solution)/shard_map/ppermute | solution.py:42
  26.1 12.4 %copy-start.2 = (f32[20,128,128]{2,1,0:T(8,128)S(1)}, f32[20,128,128]{2,1,0:T(8,128)}, u32[]{:S(2)}) copy-start(f32[20,128,128]{2,1,0:T(8,128)} %second.1) | copy-start | bytes 3932164
  27.2 11.4 %collective-permute-start.6 = (bf16[20,128,128]{2,1,0:T(8,128)(2,1)}, bf16[20,128,128]{2,1,0:T(8,128)(2,1)S(1)}, u32[]{:S(2)}, u32[]{:S(2)}) collective-permute-start(bf16[20,128,128]{2,1,0:T(8,128)(2,1)} %add_convert_fusion), channel_id=1, source_target_pairs={{0,32},{16,112},{32,64},{48,16},{64,96},{80,48},{96,0},{112,80},{1... | collective-permute-start | bytes 1966088 | tf_op jit(solution)/shard_map/ppermute | solution.py:42
  30.8 7.8 %copy-start = (f32[20,128,128]{2,1,0:T(8,128)S(1)}, f32[20,128,128]{2,1,0:T(8,128)}, u32[]{:S(2)}) copy-start(f32[20,128,128]{2,1,0:T(8,128)} %master.1) | copy-start | bytes 3932164
  30.8 7.8 %copy-start.1 = (f32[20,128,128]{2,1,0:T(8,128)S(1)}, f32[20,128,128]{2,1,0:T(8,128)}, u32[]{:S(2)}) copy-start(f32[20,128,128]{2,1,0:T(8,128)} %first.1) | copy-start | bytes 3932164
  30.8 7.8 %copy-start.3 = (s32[20]{0:T(128)S(1)}, s32[20]{0:T(128)}, u32[]{:S(2)}) copy-start(s32[20]{0:T(128)} %marked.1) | copy-start | bytes 244
  30.8 45.9 %slice-start = ((s8[5242880]{0:T(1024)(128)(4,1)}), s8[4194304]{0:T(1024)(128)(4,1)S(1)}, s32[]{:S(2)}) async-start(s8[5242880]{0:T(1024)(128)(4,1)} %bitcast.36), calls=%async_computation | async-start | bytes 8388608
  32.6 44.2 %slice-start.1 = ((s8[5242880]{0:T(1024)(128)(4,1)}), s8[1048576]{0:T(1024)(128)(4,1)S(1)}, s32[]{:S(2)}) async-start(s8[5242880]{0:T(1024)(128)(4,1)} %bitcast.36), calls=%async_computation.1 | async-start | bytes 2097152
  42.8 10.1 %collective-permute-start.9 = (bf16[560,128]{1,0:T(8,128)(2,1)S(1)}, bf16[560,128]{1,0:T(8,128)(2,1)S(1)}, u32[]{:S(2)}, u32[]{:S(2)}) collective-permute-start(bf16[560,128]{1,0:T(8,128)(2,1)S(1)} %get-tuple-element.46), channel_id=1, source_target_pairs={{0,12},{1,13},{2,14},{3,15},{4,0},{5,1},{6,2},{7,3},{8,4},{9,5},{1... | collective-permute-start | bytes 430088 | tf_op jit(solution)/shard_map/ppermute | solution.py:46
  45.3 7.5 %collective-permute-start.8 = (bf16[560,128]{1,0:T(8,128)(2,1)S(1)}, bf16[560,128]{1,0:T(8,128)(2,1)S(1)}, u32[]{:S(2)}, u32[]{:S(2)}) collective-permute-start(bf16[560,128]{1,0:T(8,128)(2,1)S(1)} %get-tuple-element.45), channel_id=1, source_target_pairs={{0,8},{1,9},{2,10},{3,11},{4,12},{5,13},{6,14},{7,15},{8,0},{9,1},... | collective-permute-start | bytes 430088 | tf_op jit(solution)/shard_map/ppermute | solution.py:46
  45.8 7.0 %collective-permute-start.7 = (bf16[560,128]{1,0:T(8,128)(2,1)S(1)}, bf16[560,128]{1,0:T(8,128)(2,1)S(1)}, u32[]{:S(2)}, u32[]{:S(2)}) collective-permute-start(bf16[560,128]{1,0:T(8,128)(2,1)S(1)} %get-tuple-element.44), channel_id=1, source_target_pairs={{0,4},{1,5},{2,6},{3,7},{4,8},{5,9},{6,10},{7,11},{8,12},{9,13},{1... | collective-permute-start | bytes 430088 | tf_op jit(solution)/shard_map/ppermute | solution.py:46
  46.4 9.1 %collective-permute-start.10 = (bf16[512,128]{1,0:T(8,128)(2,1)S(1)}, bf16[512,128]{1,0:T(8,128)(2,1)S(1)}, u32[]{:S(2)}, u32[]{:S(2)}) collective-permute-start(bf16[512,128]{1,0:T(8,128)(2,1)S(1)} %get-tuple-element.47), channel_id=1, source_target_pairs={{0,0},{1,1},{2,2},{3,3},{4,16},{5,17},{6,18},{7,19},{8,32},{9,33},... | collective-permute-start | bytes 393224 | tf_op jit(solution)/shard_map/ppermute | solution.py:323
  55.7 7.6 %collective-permute-start.11 = (bf16[832,128]{1,0:T(8,128)(2,1)S(1)}, bf16[832,128]{1,0:T(8,128)(2,1)S(1)}, u32[]{:S(2)}, u32[]{:S(2)}) collective-permute-start(bf16[832,128]{1,0:T(8,128)(2,1)S(1)} %get-tuple-element.88), channel_id=1, source_target_pairs={{0,1},{1,2},{2,3},{3,0},{4,5},{5,6},{6,7},{7,4},{8,9},{9,10},{10,1... | collective-permute-start | bytes 638984 | tf_op jit(solution)/shard_map/ppermute | solution.py:46
  57.0 11.9 %collective-permute-start.13 = (bf16[832,128]{1,0:T(8,128)(2,1)S(1)}, bf16[832,128]{1,0:T(8,128)(2,1)S(1)}, u32[]{:S(2)}, u32[]{:S(2)}) collective-permute-start(bf16[832,128]{1,0:T(8,128)(2,1)S(1)} %get-tuple-element.90), channel_id=1, source_target_pairs={{0,3},{1,0},{2,1},{3,2},{4,7},{5,4},{6,5},{7,6},{8,11},{9,8},{10,9... | collective-permute-start | bytes 638984 | tf_op jit(solution)/shard_map/ppermute | solution.py:46
  58.5 10.4 %collective-permute-start.12 = (bf16[832,128]{1,0:T(8,128)(2,1)S(1)}, bf16[832,128]{1,0:T(8,128)(2,1)S(1)}, u32[]{:S(2)}, u32[]{:S(2)}) collective-permute-start(bf16[832,128]{1,0:T(8,128)(2,1)S(1)} %get-tuple-element.89), channel_id=1, source_target_pairs={{0,2},{1,3},{2,0},{3,1},{4,6},{5,7},{6,4},{7,5},{8,10},{9,11},{10,... | collective-permute-start | bytes 638984 | tf_op jit(solution)/shard_map/ppermute | solution.py:46
  69.0 6.0 %collective-permute-start.15 = (bf16[20,128,128]{2,1,0:T(8,128)(2,1)S(1)}, bf16[20,128,128]{2,1,0:T(8,128)(2,1)S(1)}, u32[]{:S(2)}, u32[]{:S(2)}) collective-permute-start(bf16[20,128,128]{2,1,0:T(8,128)(2,1)S(1)} %bitcast.38), channel_id=1, source_target_pairs={{0,16},{16,0},{32,48},{48,32},{64,80},{80,64},{96,112},{112,96},{1... | collective-permute-start | bytes 1966088 | tf_op jit(solution)/shard_map/ppermute | solution.py:42
  70.6 12.0 %collective-permute-start.14 = (bf16[20,128,128]{2,1,0:T(8,128)(2,1)S(1)}, bf16[20,128,128]{2,1,0:T(8,128)(2,1)S(1)}, u32[]{:S(2)}, u32[]{:S(2)}) collective-permute-start(bf16[20,128,128]{2,1,0:T(8,128)(2,1)S(1)} %bitcast.39), channel_id=1, source_target_pairs={{0,32},{16,112},{32,64},{48,16},{64,96},{80,48},{96,0},{112,80},{1... | collective-permute-start | bytes 1966088 | tf_op jit(solution)/shard_map/ppermute | solution.py:42
  75.0 14.5 %collective-permute-start.17 = (bf16[20,128,128]{2,1,0:T(8,128)(2,1)S(1)}, bf16[20,128,128]{2,1,0:T(8,128)(2,1)S(1)}, u32[]{:S(2)}, u32[]{:S(2)}) collective-permute-start(bf16[20,128,128]{2,1,0:T(8,128)(2,1)S(1)} %collective-permute-done.15.paired), channel_id=1, source_target_pairs={{0,32},{16,112},{32,64},{48,16},{64,96},{80,48},{96,0},{112,80},{1... | collective-permute-start | bytes 1966088 | tf_op jit(solution)/shard_map/ppermute | solution.py:42
  82.5 8.5 %collective-permute-start.16 = (bf16[20,128,128]{2,1,0:T(8,128)(2,1)S(1)}, bf16[20,128,128]{2,1,0:T(8,128)(2,1)S(1)}, u32[]{:S(2)}, u32[]{:S(2)}) collective-permute-start(bf16[20,128,128]{2,1,0:T(8,128)(2,1)S(1)} %shard_map.133.refs_0_), channel_id=1, source_target_pairs={{0,16},{16,0},{32,48},{48,32},{64,80},{80,64},{96,112},{112,96},{1... | collective-permute-start | bytes 1966088 | tf_op jit(solution)/shard_map/ppermute | solution.py:42
  83.9 13.6 %collective-permute-start.19 = (bf16[20,128,128]{2,1,0:T(8,128)(2,1)S(1)}, bf16[20,128,128]{2,1,0:T(8,128)(2,1)S(1)}, u32[]{:S(2)}, u32[]{:S(2)}) collective-permute-start(bf16[20,128,128]{2,1,0:T(8,128)(2,1)S(1)} %shard_map.133.refs_0_), channel_id=1, source_target_pairs={{0,32},{16,112},{32,64},{48,16},{64,96},{80,48},{96,0},{112,80},{1... | collective-permute-start | bytes 1966088 | tf_op jit(solution)/shard_map/ppermute | solution.py:42
  89.6 3.1 %collective-permute-start.18 = (bf16[20,128,128]{2,1,0:T(8,128)(2,1)S(1)}, bf16[20,128,128]{2,1,0:T(8,128)(2,1)S(1)}, u32[]{:S(2)}, u32[]{:S(2)}) collective-permute-start(bf16[20,128,128]{2,1,0:T(8,128)(2,1)S(1)} %collective-permute-done.17.refs_2_), channel_id=1, source_target_pairs={{0,16},{16,0},{32,48},{48,32},{64,80},{80,64},{96,112},{112,96},{1... | collective-permute-start | bytes 1966088 | tf_op jit(solution)/shard_map/ppermute | solution.py:42
  97.5 2.2 %copy-start.4 = (f32[128]{0:T(128)S(1)}, f32[128]{0:T(128)}, u32[]{:S(2)}) copy-start(f32[128]{0:T(128)} %param.17) | copy-start | bytes 1540
  97.5 2.2 %collective-permute-start.20 = (bf16[20,128,128]{2,1,0:T(8,128)(2,1)S(1)}, bf16[20,128,128]{2,1,0:T(8,128)(2,1)S(1)}, u32[]{:S(2)}, u32[]{:S(2)}) collective-permute-start(bf16[20,128,128]{2,1,0:T(8,128)(2,1)S(1)} %shard_map.135.piece), channel_id=1, source_target_pairs={{0,16},{16,0},{32,48},{48,32},{64,80},{80,64},{96,112},{112,96},{1... | collective-permute-start | bytes 1966088 | tf_op jit(solution)/shard_map/ppermute | solution.py:42

commit v3 on v2

--- a/solution.py
+++ b/solution.py
@@ -303,17 +303,17 @@
     far_out, far_keep = part(opposite, other), part(opposite, core)
     (far_out,) = after(far_out)
     direct_out, relay_out = part(up, other), part(down, other)
-    far_in = tie(on_dp(far_out, CORE), direct_out, relay_out)
-    (far,) = after(add(far_keep, far_in))
+    (far,) = after(add(far_keep, on_dp(far_out, CORE)))
     far = on_dp(far, Z_WAY)
-    direct_in = tie(on_dp(direct_out, CORE), picked)
+    (relay,) = after(add(part(up, core), on_dp(relay_out, CORE)))
+    (own_out,) = after(part(z, other))
+    direct_in = tie(on_dp(direct_out, CORE), relay, own_out)
     (direct,) = after(add(part(down, core), direct_in))
-    (relay,) = after(add(part(up, core), on_dp(relay_out, CORE)))
-    far = tie(far, direct, relay)
+    far = tie(far, direct, picked)
     direct = on_dp(direct, Z_BACK)
     relay = on_dp(add(relay, far), Z_WAY)
-    own, own_out = after(part(z, core), part(z, other))
-    near = own.astype(f32) + on_dp(own_out, CORE).astype(f32) + direct.astype(f32)
+    own = part(z, core).astype(f32) + on_dp(own_out, CORE).astype(f32)
+    near = own + direct.astype(f32)
 
     state = (master, moment_first, moment_second)
     *state_new, row0, row1, row2, row3, extra = adam(

time: 103 us -> 99.8 us (0.969)
  waiting for transfers between devices: 36.3 us -> 33.3 us
  starting transfers between devices: 38 us -> 36.5 us
  other arithmetic: 5.81 us -> 6.87 us
    ppermute x14, waiting for transfers between devices: 24.7 us -> 21.7 us  [on_dp(): return lax.ppermute(value, 'dp', pairs)]
    ppermute x14, starting transfers between devices: 23.7 us -> 22.3 us  [on_dp(): return lax.ppermute(value, 'dp', pairs)]
    squeeze x3, local copies, waits for them, and re-layouts: 4.37 us -> 5.69 us  [part(): return lax.dynamic_slice(parts, start, (1, 1, count, 128, 128))[0, 0]]
    unnamed x26, local copies, waits for them, and re-layouts: 1.62 us -> 0.53 us
  transfers between devices with their start and end apart: 21 -> 21, of which waited for: 10 -> 11; matrix products, arithmetic and copies ran while one was open for 10% -> 12% of each run, Pallas kernels for 7% -> 8%
where the time goes in v3:
time: 99.8 us; the launch traced here: 99.5 us
  starting transfers between devices  36.5 us (37%)
  waiting for transfers between devices  33.3 us (33%)
  Pallas kernels  14.8 us (15%)
  local copies, waits for them, and re-layouts  7 us (7%)
  other arithmetic  6.87 us (7%)
  between operations  1.04 us (1%)
    ppermute x14, starting transfers between devices, on_dp(): return lax.ppermute(value, 'dp', pairs)  22.3 us
    ppermute x14, waiting for transfers between devices, on_dp(): return lax.ppermute(value, 'dp', pairs)  21.7 us
    ppermute x6, waiting for transfers between devices, on_mp(): return lax.ppermute(value, 'mp', pairs)  8.98 us
    ppermute x6, starting transfers between devices, on_mp(): return lax.ppermute(value, 'mp', pairs)  8.05 us
    ppermute x1, starting transfers between devices, on_device(): extra = lax.ppermute(extra, ('dp', 'mp'), SWAP)  6.17 us
    squeeze x3, local copies, waits for them, and re-layouts, part(): return lax.dynamic_slice(parts, start, (1, 1, count, 128, 128))[0, 0]  5.69 us
    pallas_call x1, Pallas kernels, on_device(): local(second_kernel, [SMEM] + [VMEM] * 6, [VMEM, ANY, VMEM, VMEM], [SERVI...  4.83 us
    convert_element_type x4, other arithmetic, add(): return sum((term.astype(f32) for term in terms)).astype(bf16)  4.82 us
  transfers between devices with their start and end apart: 21, of which 11 were waited for; matrix products, arithmetic and copies ran while one was open for 12% of the time, Pallas kernels for 8%

profile of v3, /device:TPU:1, one launch (start us, length us, event | category | flops | bytes accessed | tf_op | source)
XLA Modules:
  0.0 99.5 jit_solution(15249753708175690098)
XLA Ops:
  0.7 2.0 %dynamic-slice_bitcast_fusion.3 = bf16[20,128,128]{2,1,0:T(8,128)(2,1)} fusion(bf16[4,2,20,128,128]{4,3,2,1,0:T(8,128)(2,1)} %bitcast.43, s32[]{:T(128)S(6)} %select_n.83, s32[]{:T(128)S(6)} %select_n.84), kind=kLoop, calls=%fused_computation.13 | loop fusion | bytes 1310728 | tf_op jit(solution)/shard_map/squeeze | solution.py:296
  2.7 1.4 %collective-permute-start = (bf16[20,128,128]{2,1,0:T(8,128)(2,1)}, bf16[20,128,128]{2,1,0:T(8,128)(2,1)S(1)}, u32[]{:S(2)}, u32[]{:S(2)}) collective-permute-start(bf16[20,128,128]{2,1,0:T(8,128)(2,1)} %dynamic-slice_bitcast_fusion.3), channel_id=1, source_target_pairs={{0,16},{16,0},{32,48},{48,32},{64,80},{80,64},{96,112},{112,96},{1... | collective-permute-start | bytes 1966088 | tf_op jit(solution)/shard_map/ppermute | solution.py:42
  4.1 2.6 %dynamic-slice_bitcast_fusion = (bf16[20,128,128]{2,1,0:T(8,128)(2,1)}, bf16[20,128,128]{2,1,0:T(8,128)(2,1)}) fusion(bf16[4,2,20,128,128]{4,3,2,1,0:T(8,128)(2,1)} %bitcast.44, s32[]{:T(128)S(6)} %select_n.87, s32[]{:T(128)S(6)} %select_n.84, s32[]{:T(128)S(6)} %select_n.89), kind=kLoop, calls=%fused_computation.10 | loop fusion | bytes 2621452 | tf_op jit(solution)/shard_map/squeeze | solution.py:296
  6.7 0.0 collective-permute-start.1
  6.7 0.5 collective-permute-start.2
  7.2 0.4 copy.20
  7.6 0.6 gather_fusion
  8.2 1.3 %fusion.3 = bf16[20,128,128]{2,1,0:T(8,128)(2,1)S(1)} fusion(bf16[20,128,128]{2,1,0:T(8,128)(2,1)S(1)} %collective-permute-done, bf16[4,2,20,128,128]{4,3,2,1,0:T(8,128)(2,1)} %bitcast.45, s32[]{:T(128)S(6)} %select_n.83, s32[]{:T(128)S(6)} %select_n.85), kind=kLoop, calls=%fused_computation.8 | loop fusion | flops 1310720 | bytes 1966088 | tf_op jit(solution)/shard_map/convert_element_type | solution.py:56
  9.5 3.9 %collective-permute-start.5 = (bf16[20,128,128]{2,1,0:T(8,128)(2,1)S(1)}, bf16[20,128,128]{2,1,0:T(8,128)(2,1)S(1)}, u32[]{:S(2)}, u32[]{:S(2)}) collective-permute-start(bf16[20,128,128]{2,1,0:T(8,128)(2,1)S(1)} %fusion.3), channel_id=1, source_target_pairs={{0,32},{16,112},{32,64},{48,16},{64,96},{80,48},{96,0},{112,80},{1... | collective-permute-start | bytes 1966088 | tf_op jit(solution)/shard_map/ppermute | solution.py:42
  13.4 1.3 %fusion.2.refs_1_ = bf16[20,128,128]{2,1,0:T(8,128)(2,1)S(1)} fusion(bf16[20,128,128]{2,1,0:T(8,128)(2,1)S(1)} %collective-permute-done.1, bf16[4,2,20,128,128]{4,3,2,1,0:T(8,128)(2,1)} %bitcast.46, s32[]{:T(128)S(6)} %select_n.87, s32[]{:T(128)S(6)} %select_n.85), kind=kLoop, calls=%fused_computation.6 | loop fusion | flops 1310720 | bytes 1966088 | tf_op jit(solution)/shard_map/convert_element_type | solution.py:56
  14.7 1.1 %dynamic-slice_bitcast_fusion.1.refs_2_ = bf16[20,128,128]{2,1,0:T(8,128)(2,1)S(1)} fusion(bf16[4,2,20,128,128]{4,3,2,1,0:T(8,128)(2,1)} %bitcast.47, s32[]{:T(128)S(6)} %select_n.90, s32[]{:T(128)S(6)} %select_n.84), kind=kLoop, calls=%fused_computation.11 | loop fusion | bytes 1310728 | tf_op jit(solution)/shard_map/squeeze | solution.py:296
  15.8 0.1 collective-permute-start.3
  15.9 1.3 %fusion.1.refs_1_ = bf16[20,128,128]{2,1,0:T(8,128)(2,1)S(1)} fusion(bf16[20,128,128]{2,1,0:T(8,128)(2,1)S(1)} %shard_map.128, bf16[4,2,20,128,128]{4,3,2,1,0:T(8,128)(2,1)} %bitcast.48, s32[]{:T(128)S(6)} %select_n.89, s32[]{:T(128)S(6)} %select_n.85), kind=kLoop, calls=%fused_computation.4 | loop fusion | flops 1310720 | bytes 1966088 | tf_op jit(solution)/shard_map/convert_element_type | solution.py:56
  17.2 0.1 collective-permute-start.4
  17.3 0.1 pad_select_fusion.refs_2_.picked
  17.4 5.6 %collective-permute-done.5.refs_0_ = bf16[20,128,128]{2,1,0:T(8,128)(2,1)S(1)} collective-permute-done((bf16[20,128,128]{2,1,0:T(8,128)(2,1)S(1)}, bf16[20,128,128]{2,1,0:T(8,128)(2,1)S(1)}, u32[]{:S(2)}, u32[]{:S(2)}) %collective-permute-start.5) | collective-permute-done | bytes 655392 | tf_op jit(solution)/shard_map/ppermute | solution.py:42
  23.0 1.0 %add_convert_fusion = bf16[20,128,128]{2,1,0:T(8,128)(2,1)} fusion(bf16[20,128,128]{2,1,0:T(8,128)(2,1)S(1)} %shard_map.129, bf16[20,128,128]{2,1,0:T(8,128)(2,1)S(1)} %fusion.2.refs_1_), kind=kLoop, calls=%fused_computation.9 | loop fusion | flops 1310720 | bytes 1966080 | tf_op jit(solution)/shard_map/convert_element_type | solution.py:56
  24.0 3.5 %collective-permute-start.6 = (bf16[20,128,128]{2,1,0:T(8,128)(2,1)}, bf16[20,128,128]{2,1,0:T(8,128)(2,1)S(1)}, u32[]{:S(2)}, u32[]{:S(2)}) collective-permute-start(bf16[20,128,128]{2,1,0:T(8,128)(2,1)} %add_convert_fusion), channel_id=1, source_target_pairs={{0,32},{16,112},{32,64},{48,16},{64,96},{80,48},{96,0},{112,80},{1... | collective-permute-start | bytes 1966088 | tf_op jit(solution)/shard_map/ppermute | solution.py:42
  27.5 0.1 stack.42.place
  27.6 1.1 %collective-permute-done.4 = bf16[20,128,128]{2,1,0:T(8,128)(2,1)} collective-permute-done((bf16[20,128,128]{2,1,0:T(8,128)(2,1)S(1)}, bf16[20,128,128]{2,1,0:T(8,128)(2,1)}, u32[]{:S(2)}, u32[]{:S(2)}) %collective-permute-start.4) | collective-permute-done | bytes 655392 | tf_op jit(solution)/shard_map/ppermute | solution.py:42
  28.7 1.9 %fusion.near = f32[20,128,128]{2,1,0:T(8,128)S(1)} fusion(bf16[20,128,128]{2,1,0:T(8,128)(2,1)} %collective-permute-done.4, bf16[20,128,128]{2,1,0:T(8,128)(2,1)} %collective-permute-done.3, bf16[4,2,20,128,128]{4,3,2,1,0:T(8,128)(2,1)} %bitcast.49, s32[]{:T(128)S(6)} %select_n.90, s32[]{:T(128)S(6)} %select_n.85), kind=kLoop, calls=%fused_computation.2 | loop fusion | flops 1638400 | bytes 3276808 | tf_op jit(solution)/shard_map/add | solution.py:316
  30.6 4.7 %collective-permute-done.6.relay = bf16[20,128,128]{2,1,0:T(8,128)(2,1)S(1)} collective-permute-done((bf16[20,128,128]{2,1,0:T(8,128)(2,1)}, bf16[20,128,128]{2,1,0:T(8,128)(2,1)S(1)}, u32[]{:S(2)}, u32[]{:S(2)}) %collective-permute-start.6) | collective-permute-done | bytes 655392 | tf_op jit(solution)/shard_map/ppermute | solution.py:42
  35.3 4.3 %shard_map.130 = (f32[20,128,128]{2,1,0:T(8,128)}, f32[20,128,128]{2,1,0:T(8,128)}, f32[20,128,128]{2,1,0:T(8,128)}, bf16[560,128]{1,0:T(8,128)(2,1)S(1)}, bf16[...) custom-call(s32[6]{0:T(128)S(1)} %stack.42.place, ...), custom_call_target="tpu_custom_call" | custom-call | flops 1000 | bytes 1000 | tf_op jit(solution)/shard_map/pallas_call | solution.py:112
  39.6 2.5 %collective-permute-start.9 = (bf16[560,128]{1,0:T(8,128)(2,1)S(1)}, bf16[560,128]{1,0:T(8,128)(2,1)S(1)}, u32[]{:S(2)}, u32[]{:S(2)}) collective-permute-start(bf16[560,128]{1,0:T(8,128)(2,1)S(1)} %get-tuple-element.46), channel_id=1, source_target_pairs={{0,12},{1,13},{2,14},{3,15},{4,0},{5,1},{6,2},{7,3},{8,4},{9,5},{1... | collective-permute-start | bytes 430088 | tf_op jit(solution)/shard_map/ppermute | solution.py:46
  42.1 0.5 collective-permute-start.8
  42.6 0.6 collective-permute-start.7
  43.2 6.2 %collective-permute-start.10 = (bf16[512,128]{1,0:T(8,128)(2,1)S(1)}, bf16[512,128]{1,0:T(8,128)(2,1)S(1)}, u32[]{:S(2)}, u32[]{:S(2)}) collective-permute-start(bf16[512,128]{1,0:T(8,128)(2,1)S(1)} %get-tuple-element.47), channel_id=1, source_target_pairs={{0,0},{1,1},{2,2},{3,3},{4,16},{5,17},{6,18},{7,19},{8,32},{9,33},... | collective-permute-start | bytes 393224 | tf_op jit(solution)/shard_map/ppermute | solution.py:323
  49.4 0.2 collective-permute-done.7
  49.7 2.6 %collective-permute-done.10 = bf16[512,128]{1,0:T(8,128)(2,1)S(1)} collective-permute-done((bf16[512,128]{1,0:T(8,128)(2,1)S(1)}, bf16[512,128]{1,0:T(8,128)(2,1)S(1)}, u32[]{:S(2)}, u32[]{:S(2)}) %collective-permute-start.10) | collective-permute-done | bytes 131104 | tf_op jit(solution)/shard_map/ppermute | solution.py:323
  52.4 1.4 %collective-permute-start.11 = (bf16[832,128]{1,0:T(8,128)(2,1)S(1)}, bf16[832,128]{1,0:T(8,128)(2,1)S(1)}, u32[]{:S(2)}, u32[]{:S(2)}) collective-permute-start(bf16[832,128]{1,0:T(8,128)(2,1)S(1)} %get-tuple-element.86), channel_id=1, source_target_pairs={{0,1},{1,2},{2,3},{3,0},{4,5},{5,6},{6,7},{7,4},{8,9},{9,10},{10,1... | collective-permute-start | bytes 638984 | tf_op jit(solution)/shard_map/ppermute | solution.py:46
  53.8 1.5 %collective-permute-start.13 = (bf16[832,128]{1,0:T(8,128)(2,1)S(1)}, bf16[832,128]{1,0:T(8,128)(2,1)S(1)}, u32[]{:S(2)}, u32[]{:S(2)}) collective-permute-start(bf16[832,128]{1,0:T(8,128)(2,1)S(1)} %get-tuple-element.88), channel_id=1, source_target_pairs={{0,3},{1,0},{2,1},{3,2},{4,7},{5,4},{6,5},{7,6},{8,11},{9,8},{10,9... | collective-permute-start | bytes 638984 | tf_op jit(solution)/shard_map/ppermute | solution.py:46
  55.3 1.6 %collective-permute-start.12 = (bf16[832,128]{1,0:T(8,128)(2,1)S(1)}, bf16[832,128]{1,0:T(8,128)(2,1)S(1)}, u32[]{:S(2)}, u32[]{:S(2)}) collective-permute-start(bf16[832,128]{1,0:T(8,128)(2,1)S(1)} %get-tuple-element.87), channel_id=1, source_target_pairs={{0,2},{1,3},{2,0},{3,1},{4,6},{5,7},{6,4},{7,5},{8,10},{9,11},{10,... | collective-permute-start | bytes 638984 | tf_op jit(solution)/shard_map/ppermute | solution.py:46
  56.9 3.1 %collective-permute-done.11 = bf16[832,128]{1,0:T(8,128)(2,1)S(1)} collective-permute-done((bf16[832,128]{1,0:T(8,128)(2,1)S(1)}, bf16[832,128]{1,0:T(8,128)(2,1)S(1)}, u32[]{:S(2)}, u32[]{:S(2)}) %collective-permute-start.11) | collective-permute-done | bytes 213024 | tf_op jit(solution)/shard_map/ppermute | solution.py:46
  60.0 5.6 %collective-permute-done.12 = bf16[832,128]{1,0:T(8,128)(2,1)S(1)} collective-permute-done((bf16[832,128]{1,0:T(8,128)(2,1)S(1)}, bf16[832,128]{1,0:T(8,128)(2,1)S(1)}, u32[]{:S(2)}, u32[]{:S(2)}) %collective-permute-start.12) | collective-permute-done | bytes 213024 | tf_op jit(solution)/shard_map/ppermute | solution.py:46
  65.7 1.6 %collective-permute-start.15 = (bf16[20,128,128]{2,1,0:T(8,128)(2,1)S(1)}, bf16[20,128,128]{2,1,0:T(8,128)(2,1)S(1)}, u32[]{:S(2)}, u32[]{:S(2)}) collective-permute-start(bf16[20,128,128]{2,1,0:T(8,128)(2,1)S(1)} %bitcast.39), channel_id=1, source_target_pairs={{0,16},{16,0},{32,48},{48,32},{64,80},{80,64},{96,112},{112,96},{1... | collective-permute-start | bytes 1966088 | tf_op jit(solution)/shard_map/ppermute | solution.py:42
  67.3 4.5 %collective-permute-start.14 = (bf16[20,128,128]{2,1,0:T(8,128)(2,1)S(1)}, bf16[20,128,128]{2,1,0:T(8,128)(2,1)S(1)}, u32[]{:S(2)}, u32[]{:S(2)}) collective-permute-start(bf16[20,128,128]{2,1,0:T(8,128)(2,1)S(1)} %bitcast.40), channel_id=1, source_target_pairs={{0,32},{16,112},{32,64},{48,16},{64,96},{80,48},{96,0},{112,80},{1... | collective-permute-start | bytes 1966088 | tf_op jit(solution)/shard_map/ppermute | solution.py:42
  71.8 1.7 %collective-permute-start.17 = (bf16[20,128,128]{2,1,0:T(8,128)(2,1)S(1)}, bf16[20,128,128]{2,1,0:T(8,128)(2,1)S(1)}, u32[]{:S(2)}, u32[]{:S(2)}) collective-permute-start(bf16[20,128,128]{2,1,0:T(8,128)(2,1)S(1)} %collective-permute-done.15.paired), channel_id=1, source_target_pairs={{0,32},{16,112},{32,64},{48,16},{64,96},{80,48},{96,0},{112,80},{1... | collective-permute-start | bytes 1966088 | tf_op jit(solution)/shard_map/ppermute | solution.py:42
  73.5 2.7 %shard_map.131 = (bf16[5120,512]{1,0:T(8,128)(2,1)S(1)}, bf16[40,128,128]{2,1,0:T(8,128)(2,1)S(1)}) custom-call(s32[6]{0:T(128)S(1)} %stack.42.place, bf16[5120,512]{1,0:T(8,128)(2,1)S(1)} %bitcast.38, bf16[20,128,128]{2,1,0:T(8,128)(2,1)S(1)} %bitcast.41, bf16[20,128,128]{2,1,0:T(8,128)(2,1)S(1)} %collective-permute-done.15.paired), custom_call_target="tpu_custom_call" | custom-call | flops 1000 | bytes 1000 | tf_op jit(solution)/shard_map/pallas_call | solution.py:340
  76.2 3.1 %collective-permute-done.14.refs_0_ = bf16[20,128,128]{2,1,0:T(8,128)(2,1)S(1)} collective-permute-done((bf16[20,128,128]{2,1,0:T(8,128)(2,1)S(1)}, bf16[20,128,128]{2,1,0:T(8,128)(2,1)S(1)}, u32[]{:S(2)}, u32[]{:S(2)}) %collective-permute-start.14) | collective-permute-done | bytes 655392 | tf_op jit(solution)/shard_map/ppermute | solution.py:42
  79.3 1.4 %collective-permute-start.16 = (bf16[20,128,128]{2,1,0:T(8,128)(2,1)S(1)}, bf16[20,128,128]{2,1,0:T(8,128)(2,1)S(1)}, u32[]{:S(2)}, u32[]{:S(2)}) collective-permute-start(bf16[20,128,128]{2,1,0:T(8,128)(2,1)S(1)} %shard_map.132.refs_0_), channel_id=1, source_target_pairs={{0,16},{16,0},{32,48},{48,32},{64,80},{80,64},{96,112},{112,96},{1... | collective-permute-start | bytes 1966088 | tf_op jit(solution)/shard_map/ppermute | solution.py:42
  80.7 1.7 %collective-permute-start.19 = (bf16[20,128,128]{2,1,0:T(8,128)(2,1)S(1)}, bf16[20,128,128]{2,1,0:T(8,128)(2,1)S(1)}, u32[]{:S(2)}, u32[]{:S(2)}) collective-permute-start(bf16[20,128,128]{2,1,0:T(8,128)(2,1)S(1)} %shard_map.132.refs_0_), channel_id=1, source_target_pairs={{0,32},{16,112},{32,64},{48,16},{64,96},{80,48},{96,0},{112,80},{1... | collective-permute-start | bytes 1966088 | tf_op jit(solution)/shard_map/ppermute | solution.py:42
  82.4 3.9 %collective-permute-done.17.refs_2_ = bf16[20,128,128]{2,1,0:T(8,128)(2,1)S(1)} collective-permute-done((bf16[20,128,128]{2,1,0:T(8,128)(2,1)S(1)}, bf16[20,128,128]{2,1,0:T(8,128)(2,1)S(1)}, u32[]{:S(2)}, u32[]{:S(2)}) %collective-permute-start.17) | collective-permute-done | bytes 655392 | tf_op jit(solution)/shard_map/ppermute | solution.py:42
  86.3 1.4 %collective-permute-start.18 = (bf16[20,128,128]{2,1,0:T(8,128)(2,1)S(1)}, bf16[20,128,128]{2,1,0:T(8,128)(2,1)S(1)}, u32[]{:S(2)}, u32[]{:S(2)}) collective-permute-start(bf16[20,128,128]{2,1,0:T(8,128)(2,1)S(1)} %collective-permute-done.17.refs_2_), channel_id=1, source_target_pairs={{0,16},{16,0},{32,48},{48,32},{64,80},{80,64},{96,112},{112,96},{1... | collective-permute-start | bytes 1966088 | tf_op jit(solution)/shard_map/ppermute | solution.py:42
  87.8 1.7 %collective-permute-done.18.refs_3_ = bf16[20,128,128]{2,1,0:T(8,128)(2,1)S(1)} collective-permute-done((bf16[20,128,128]{2,1,0:T(8,128)(2,1)S(1)}, bf16[20,128,128]{2,1,0:T(8,128)(2,1)S(1)}, u32[]{:S(2)}, u32[]{:S(2)}) %collective-permute-start.18) | collective-permute-done | bytes 655392 | tf_op jit(solution)/shard_map/ppermute | solution.py:42
  89.5 4.8 %shard_map.133 = (bf16[5120,512]{1,0:T(8,128)(2,1)S(1)}, bf16[5120,512]{1,0:T(8,128)(2,1)}, f32[4,16,128]{2,1,0:T(8,128)S(1)}, bf16[40,16,128]{2,1,0:T(8,128)(2,1)S(1)}) custom-call(s32[6]{0:T(128)S(1)} %stack.42.place, bf16[4,192,128]{2,1,0:T(8,128)(2,1)S(1)} %pad_maximum_fusion.picked, ...), custom_call_target="tpu_custom_call", output_to_operand_aliasing={{0}: (6, {})} | custom-call | flops 1000 | bytes 1000 | tf_op jit(solution)/shard_map/pallas_call | solution.py:350
  94.3 0.5 collective-permute-start.20
  94.8 1.7 %collective-permute-done.20.crossed = bf16[20,128,128]{2,1,0:T(8,128)(2,1)S(1)} collective-permute-done((bf16[20,128,128]{2,1,0:T(8,128)(2,1)S(1)}, bf16[20,128,128]{2,1,0:T(8,128)(2,1)S(1)}, u32[]{:S(2)}, u32[]{:S(2)}) %collective-permute-start.20) | collective-permute-done | bytes 655392 | tf_op jit(solution)/shard_map/ppermute | solution.py:42
  96.5 3.0 %shard_map.135 = (bf16[5120,512]{1,0:T(8,128)(2,1)}, bf16[16,512]{1,0:T(8,128)(2,1)}) custom-call(s32[6]{0:T(128)S(1)} %stack.42.place, bf16[40,16,128]{2,1,0:T(8,128)(2,1)S(1)} %get-tuple-element.50.features, f32[1,128]{1,0:T(1,128)S(1)} %bitcast.42, f32[4,16,128]{2,1,0:T(8,128)S(1)} %get-tuple-element.51.refs_1_.before, ...), custom_call_target="tpu_custom_call", output_to_operand_aliasing={{0}: (7, {})} | custom-call | flops 1000 | bytes 1000 | tf_op jit(solution)/shard_map/pallas_call | solution.py:359
  (51 shorter events, 0.4 us)
Async XLA Ops:
  2.7 5.5 %collective-permute-start = (bf16[20,128,128]{2,1,0:T(8,128)(2,1)}, bf16[20,128,128]{2,1,0:T(8,128)(2,1)S(1)}, u32[]{:S(2)}, u32[]{:S(2)}) collective-permute-start(bf16[20,128,128]{2,1,0:T(8,128)(2,1)} %dynamic-slice_bitcast_fusion.3), channel_id=1, source_target_pairs={{0,16},{16,0},{32,48},{48,32},{64,80},{80,64},{96,112},{112,96},{1... | collective-permute-start | bytes 1966088 | tf_op jit(solution)/shard_map/ppermute | solution.py:42
  4.1 3.1 %copy-start.6 = (s32[16]{0:T(128)S(1)}, s32[16]{0:T(128)}, u32[]{:S(2)}) copy-start(s32[16]{0:T(128)} %param.16) | copy-start | bytes 196
  4.1 3.1 %copy-start.5 = (bf16[1024,320]{0,1:T(8,128)(2,1)S(1)}, bf16[1024,320]{0,1:T(8,128)(2,1)}, u32[]{:S(2)}) copy-start(bf16[1024,320]{0,1:T(8,128)(2,1)} %param.15) | copy-start | bytes 1966084
  6.7 6.8 %collective-permute-start.1 = (bf16[20,128,128]{2,1,0:T(8,128)(2,1)}, bf16[20,128,128]{2,1,0:T(8,128)(2,1)S(1)}, u32[]{:S(2)}, u32[]{:S(2)}) collective-permute-start(bf16[20,128,128]{2,1,0:T(8,128)(2,1)} %get-tuple-element.56), channel_id=1, source_target_pairs={{0,16},{16,0},{32,48},{48,32},{64,80},{80,64},{96,112},{112,96},{1... | collective-permute-start | bytes 1966088 | tf_op jit(solution)/shard_map/ppermute | solution.py:42
  6.7 9.3 %collective-permute-start.2 = (bf16[20,128,128]{2,1,0:T(8,128)(2,1)}, bf16[20,128,128]{2,1,0:T(8,128)(2,1)S(1)}, u32[]{:S(2)}, u32[]{:S(2)}) collective-permute-start(bf16[20,128,128]{2,1,0:T(8,128)(2,1)} %get-tuple-element.55), channel_id=1, source_target_pairs={{0,16},{16,0},{32,48},{48,32},{64,80},{80,64},{96,112},{112,96},{1... | collective-permute-start | bytes 1966088 | tf_op jit(solution)/shard_map/ppermute | solution.py:42
  9.5 13.5 %collective-permute-start.5 = (bf16[20,128,128]{2,1,0:T(8,128)(2,1)S(1)}, bf16[20,128,128]{2,1,0:T(8,128)(2,1)S(1)}, u32[]{:S(2)}, u32[]{:S(2)}) collective-permute-start(bf16[20,128,128]{2,1,0:T(8,128)(2,1)S(1)} %fusion.3), channel_id=1, source_target_pairs={{0,32},{16,112},{32,64},{48,16},{64,96},{80,48},{96,0},{112,80},{1... | collective-permute-start | bytes 1966088 | tf_op jit(solution)/shard_map/ppermute | solution.py:42
  15.8 12.9 %collective-permute-start.3 = (bf16[20,128,128]{2,1,0:T(8,128)(2,1)S(1)}, bf16[20,128,128]{2,1,0:T(8,128)(2,1)}, u32[]{:S(2)}, u32[]{:S(2)}) collective-permute-start(bf16[20,128,128]{2,1,0:T(8,128)(2,1)S(1)} %dynamic-slice_bitcast_fusion.1.refs_2_), channel_id=1, source_target_pairs={{0,16},{16,0},{32,48},{48,32},{64,80},{80,64},{96,112},{112,96},{1... | collective-permute-start | bytes 1966088 | tf_op jit(solution)/shard_map/ppermute | solution.py:42
  17.2 11.5 %collective-permute-start.4 = (bf16[20,128,128]{2,1,0:T(8,128)(2,1)S(1)}, bf16[20,128,128]{2,1,0:T(8,128)(2,1)}, u32[]{:S(2)}, u32[]{:S(2)}) collective-permute-start(bf16[20,128,128]{2,1,0:T(8,128)(2,1)S(1)} %fusion.1.refs_1_), channel_id=1, source_target_pairs={{0,96},{16,48},{32,0},{48,80},{64,32},{80,112},{96,64},{112,16},{1... | collective-permute-start | bytes 1966088 | tf_op jit(solution)/shard_map/ppermute | solution.py:42
  22.9 12.4 %copy-start.2 = (f32[20,128,128]{2,1,0:T(8,128)S(1)}, f32[20,128,128]{2,1,0:T(8,128)}, u32[]{:S(2)}) copy-start(f32[20,128,128]{2,1,0:T(8,128)} %second.1) | copy-start | bytes 3932164
  24.0 11.4 %collective-permute-start.6 = (bf16[20,128,128]{2,1,0:T(8,128)(2,1)}, bf16[20,128,128]{2,1,0:T(8,128)(2,1)S(1)}, u32[]{:S(2)}, u32[]{:S(2)}) collective-permute-start(bf16[20,128,128]{2,1,0:T(8,128)(2,1)} %add_convert_fusion), channel_id=1, source_target_pairs={{0,32},{16,112},{32,64},{48,16},{64,96},{80,48},{96,0},{112,80},{1... | collective-permute-start | bytes 1966088 | tf_op jit(solution)/shard_map/ppermute | solution.py:42
  27.6 7.8 %copy-start = (f32[20,128,128]{2,1,0:T(8,128)S(1)}, f32[20,128,128]{2,1,0:T(8,128)}, u32[]{:S(2)}) copy-start(f32[20,128,128]{2,1,0:T(8,128)} %master.1) | copy-start | bytes 3932164
  27.6 7.8 %copy-start.1 = (f32[20,128,128]{2,1,0:T(8,128)S(1)}, f32[20,128,128]{2,1,0:T(8,128)}, u32[]{:S(2)}) copy-start(f32[20,128,128]{2,1,0:T(8,128)} %first.1) | copy-start | bytes 3932164
  27.6 7.8 %copy-start.3 = (s32[20]{0:T(128)S(1)}, s32[20]{0:T(128)}, u32[]{:S(2)}) copy-start(s32[20]{0:T(128)} %marked.1) | copy-start | bytes 244
  28.7 44.8 %slice-start = ((s8[5242880]{0:T(1024)(128)(4,1)}), s8[4194304]{0:T(1024)(128)(4,1)S(1)}, s32[]{:S(2)}) async-start(s8[5242880]{0:T(1024)(128)(4,1)} %bitcast.37), calls=%async_computation | async-start | bytes 8388608
  30.6 42.9 %slice-start.1 = ((s8[5242880]{0:T(1024)(128)(4,1)}), s8[1048576]{0:T(1024)(128)(4,1)S(1)}, s32[]{:S(2)}) async-start(s8[5242880]{0:T(1024)(128)(4,1)} %bitcast.37), calls=%async_computation.1 | async-start | bytes 2097152
  39.6 10.1 %collective-permute-start.9 = (bf16[560,128]{1,0:T(8,128)(2,1)S(1)}, bf16[560,128]{1,0:T(8,128)(2,1)S(1)}, u32[]{:S(2)}, u32[]{:S(2)}) collective-permute-start(bf16[560,128]{1,0:T(8,128)(2,1)S(1)} %get-tuple-element.46), channel_id=1, source_target_pairs={{0,12},{1,13},{2,14},{3,15},{4,0},{5,1},{6,2},{7,3},{8,4},{9,5},{1... | collective-permute-start | bytes 430088 | tf_op jit(solution)/shard_map/ppermute | solution.py:46
  42.1 7.6 %collective-permute-start.8 = (bf16[560,128]{1,0:T(8,128)(2,1)S(1)}, bf16[560,128]{1,0:T(8,128)(2,1)S(1)}, u32[]{:S(2)}, u32[]{:S(2)}) collective-permute-start(bf16[560,128]{1,0:T(8,128)(2,1)S(1)} %get-tuple-element.45), channel_id=1, source_target_pairs={{0,8},{1,9},{2,10},{3,11},{4,12},{5,13},{6,14},{7,15},{8,0},{9,1},... | collective-permute-start | bytes 430088 | tf_op jit(solution)/shard_map/ppermute | solution.py:46
  42.6 7.0 %collective-permute-start.7 = (bf16[560,128]{1,0:T(8,128)(2,1)S(1)}, bf16[560,128]{1,0:T(8,128)(2,1)S(1)}, u32[]{:S(2)}, u32[]{:S(2)}) collective-permute-start(bf16[560,128]{1,0:T(8,128)(2,1)S(1)} %get-tuple-element.44), channel_id=1, source_target_pairs={{0,4},{1,5},{2,6},{3,7},{4,8},{5,9},{6,10},{7,11},{8,12},{9,13},{1... | collective-permute-start | bytes 430088 | tf_op jit(solution)/shard_map/ppermute | solution.py:46
  43.2 9.1 %collective-permute-start.10 = (bf16[512,128]{1,0:T(8,128)(2,1)S(1)}, bf16[512,128]{1,0:T(8,128)(2,1)S(1)}, u32[]{:S(2)}, u32[]{:S(2)}) collective-permute-start(bf16[512,128]{1,0:T(8,128)(2,1)S(1)} %get-tuple-element.47), channel_id=1, source_target_pairs={{0,0},{1,1},{2,2},{3,3},{4,16},{5,17},{6,18},{7,19},{8,32},{9,33},... | collective-permute-start | bytes 393224 | tf_op jit(solution)/shard_map/ppermute | solution.py:323
  52.4 7.6 %collective-permute-start.11 = (bf16[832,128]{1,0:T(8,128)(2,1)S(1)}, bf16[832,128]{1,0:T(8,128)(2,1)S(1)}, u32[]{:S(2)}, u32[]{:S(2)}) collective-permute-start(bf16[832,128]{1,0:T(8,128)(2,1)S(1)} %get-tuple-element.86), channel_id=1, source_target_pairs={{0,1},{1,2},{2,3},{3,0},{4,5},{5,6},{6,7},{7,4},{8,9},{9,10},{10,1... | collective-permute-start | bytes 638984 | tf_op jit(solution)/shard_map/ppermute | solution.py:46
  53.8 11.9 %collective-permute-start.13 = (bf16[832,128]{1,0:T(8,128)(2,1)S(1)}, bf16[832,128]{1,0:T(8,128)(2,1)S(1)}, u32[]{:S(2)}, u32[]{:S(2)}) collective-permute-start(bf16[832,128]{1,0:T(8,128)(2,1)S(1)} %get-tuple-element.88), channel_id=1, source_target_pairs={{0,3},{1,0},{2,1},{3,2},{4,7},{5,4},{6,5},{7,6},{8,11},{9,8},{10,9... | collective-permute-start | bytes 638984 | tf_op jit(solution)/shard_map/ppermute | solution.py:46
  55.3 10.4 %collective-permute-start.12 = (bf16[832,128]{1,0:T(8,128)(2,1)S(1)}, bf16[832,128]{1,0:T(8,128)(2,1)S(1)}, u32[]{:S(2)}, u32[]{:S(2)}) collective-permute-start(bf16[832,128]{1,0:T(8,128)(2,1)S(1)} %get-tuple-element.87), channel_id=1, source_target_pairs={{0,2},{1,3},{2,0},{3,1},{4,6},{5,7},{6,4},{7,5},{8,10},{9,11},{10,... | collective-permute-start | bytes 638984 | tf_op jit(solution)/shard_map/ppermute | solution.py:46
  65.7 6.1 %collective-permute-start.15 = (bf16[20,128,128]{2,1,0:T(8,128)(2,1)S(1)}, bf16[20,128,128]{2,1,0:T(8,128)(2,1)S(1)}, u32[]{:S(2)}, u32[]{:S(2)}) collective-permute-start(bf16[20,128,128]{2,1,0:T(8,128)(2,1)S(1)} %bitcast.39), channel_id=1, source_target_pairs={{0,16},{16,0},{32,48},{48,32},{64,80},{80,64},{96,112},{112,96},{1... | collective-permute-start | bytes 1966088 | tf_op jit(solution)/shard_map/ppermute | solution.py:42
  67.3 12.0 %collective-permute-start.14 = (bf16[20,128,128]{2,1,0:T(8,128)(2,1)S(1)}, bf16[20,128,128]{2,1,0:T(8,128)(2,1)S(1)}, u32[]{:S(2)}, u32[]{:S(2)}) collective-permute-start(bf16[20,128,128]{2,1,0:T(8,128)(2,1)S(1)} %bitcast.40), channel_id=1, source_target_pairs={{0,32},{16,112},{32,64},{48,16},{64,96},{80,48},{96,0},{112,80},{1... | collective-permute-start | bytes 1966088 | tf_op jit(solution)/shard_map/ppermute | solution.py:42
  71.8 14.5 %collective-permute-start.17 = (bf16[20,128,128]{2,1,0:T(8,128)(2,1)S(1)}, bf16[20,128,128]{2,1,0:T(8,128)(2,1)S(1)}, u32[]{:S(2)}, u32[]{:S(2)}) collective-permute-start(bf16[20,128,128]{2,1,0:T(8,128)(2,1)S(1)} %collective-permute-done.15.paired), channel_id=1, source_target_pairs={{0,32},{16,112},{32,64},{48,16},{64,96},{80,48},{96,0},{112,80},{1... | collective-permute-start | bytes 1966088 | tf_op jit(solution)/shard_map/ppermute | solution.py:42
  79.3 8.5 %collective-permute-start.16 = (bf16[20,128,128]{2,1,0:T(8,128)(2,1)S(1)}, bf16[20,128,128]{2,1,0:T(8,128)(2,1)S(1)}, u32[]{:S(2)}, u32[]{:S(2)}) collective-permute-start(bf16[20,128,128]{2,1,0:T(8,128)(2,1)S(1)} %shard_map.132.refs_0_), channel_id=1, source_target_pairs={{0,16},{16,0},{32,48},{48,32},{64,80},{80,64},{96,112},{112,96},{1... | collective-permute-start | bytes 1966088 | tf_op jit(solution)/shard_map/ppermute | solution.py:42
  80.7 13.6 %collective-permute-start.19 = (bf16[20,128,128]{2,1,0:T(8,128)(2,1)S(1)}, bf16[20,128,128]{2,1,0:T(8,128)(2,1)S(1)}, u32[]{:S(2)}, u32[]{:S(2)}) collective-permute-start(bf16[20,128,128]{2,1,0:T(8,128)(2,1)S(1)} %shard_map.132.refs_0_), channel_id=1, source_target_pairs={{0,32},{16,112},{32,64},{48,16},{64,96},{80,48},{96,0},{112,80},{1... | collective-permute-start | bytes 1966088 | tf_op jit(solution)/shard_map/ppermute | solution.py:42
  86.3 3.1 %collective-permute-start.18 = (bf16[20,128,128]{2,1,0:T(8,128)(2,1)S(1)}, bf16[20,128,128]{2,1,0:T(8,128)(2,1)S(1)}, u32[]{:S(2)}, u32[]{:S(2)}) collective-permute-start(bf16[20,128,128]{2,1,0:T(8,128)(2,1)S(1)} %collective-permute-done.17.refs_2_), channel_id=1, source_target_pairs={{0,16},{16,0},{32,48},{48,32},{64,80},{80,64},{96,112},{112,96},{1... | collective-permute-start | bytes 1966088 | tf_op jit(solution)/shard_map/ppermute | solution.py:42
  94.3 2.2 %copy-start.4 = (f32[128]{0:T(128)S(1)}, f32[128]{0:T(128)}, u32[]{:S(2)}) copy-start(f32[128]{0:T(128)} %param.17) | copy-start | bytes 1540
  94.3 2.2 %collective-permute-start.20 = (bf16[20,128,128]{2,1,0:T(8,128)(2,1)S(1)}, bf16[20,128,128]{2,1,0:T(8,128)(2,1)S(1)}, u32[]{:S(2)}, u32[]{:S(2)}) collective-permute-start(bf16[20,128,128]{2,1,0:T(8,128)(2,1)S(1)} %shard_map.134.piece), channel_id=1, source_target_pairs={{0,16},{16,0},{32,48},{48,32},{64,80},{80,64},{96,112},{112,96},{1... | collective-permute-start | bytes 1966088 | tf_op jit(solution)/shard_map/ppermute | solution.py:42

commit v4 on v3

--- a/solution.py
+++ b/solution.py
@@ -212,33 +212,35 @@
         write(i).wait()
 
 
-def last_kernel(
-    place, features, gain, before, old, piece, crossed, _, out, scores, total, held, sems
-):
+def last_kernel(number, place, features, gain, before, old, piece, _, *refs):
+    out, result, total, held, sems = refs
     total[...] = before[...]
     writes = []
-    for number, (source, (steps, cross)) in enumerate(zip((piece, crossed), LAST)):
-        for odd in range(2):
-            for wanted in ((0, 1, 2, 3), (4,)):
-                first = len(writes)
-                left = []
-                for s in wanted:
-                    for u in (odd, odd + 2):
-                        row, column = origin(place, steps, cross, u, s)
-                        i, n = u * 5 + s, len(writes)
-                        block = source[i]
-                        held[n] = jnp.where(block == jnp.inf, old[number * 20 + i], block)
-                        to = out.at[spot(row, column)]
-                        writes.append(pltpu.make_async_copy(held.at[n], to, sems.at[n]))
-                        writes[n].start()
-                        left.append(features[row])
-                right = held[first : len(writes)].reshape(-1, 128)
-                left = jnp.concatenate(left, axis=1)
-                total[column] += jnp.dot(left, right, preferred_element_type=f32)
-    for head in range(4):
-        query = total[head]
-        scale = lax.rsqrt(jnp.mean(query * query, axis=-1, keepdims=True) + 1e-06)
-        scores[:, head * 128 : head * 128 + 128] = (query * scale * gain[...]).astype(bf16)
+    for odd in range(2):
+        for wanted in ((0, 1, 2, 3), (4,)):
+            first = len(writes)
+            left = []
+            for s in wanted:
+                for u in (odd, odd + 2):
+                    row, column = origin(place, *LAST[number], u, s)
+                    i, n = u * 5 + s, len(writes)
+                    block = piece[i]
+                    held[n] = jnp.where(block == jnp.inf, old[number * 20 + i], block)
+                    to = out.at[spot(row, column)]
+                    writes.append(pltpu.make_async_copy(held.at[n], to, sems.at[n]))
+                    writes[n].start()
+                    left.append(features[row])
+            right = held[first : len(writes)].reshape(-1, 128)
+            left = jnp.concatenate(left, axis=1)
+            total[column] += jnp.dot(left, right, preferred_element_type=f32)
+    if number == 0:
+        result[...] = total[...]
+    else:
+        for head in range(4):
+            query = total[head]
+            scale = lax.rsqrt(jnp.mean(query * query, axis=-1, keepdims=True) + 1e-06)
+            columns = pl.ds(head * 128, 128)
+            result[:, columns] = (query * scale * gain[...]).astype(bf16)
     for write in writes:
         write.wait()
 
@@ -356,28 +358,22 @@
         {6: 0},
     )(place, features, *pieces, work)
     far = tie(far, total)
-    serving_new, scores = local(
-        last_kernel,
-        [SMEM] + [VMEM] * 6 + [ANY],
-        [ANY, VMEM],
-        [SERVING, SCORES],
-        [
-            pltpu.VMEM(TOTAL.shape, f32),
-            pltpu.VMEM(OLD.shape, bf16),
-            pltpu.SemaphoreType.DMA((40,)),
-        ],
-        {7: 0},
-    )(
-        place,
-        features,
-        head_gain.reshape(1, 128),
-        total,
-        old,
-        far,
-        on_dp(far, CORE),
-        out,
-    )
-    return (*state_new, serving_new, scores)
+    gain = head_gain.reshape(1, 128)
+    pieces = far, on_dp(far, CORE)
+    for number, shape in enumerate((TOTAL, SCORES)):
+        out, total = local(
+            functools.partial(last_kernel, number),
+            [SMEM] + [VMEM] * 5 + [ANY],
+            [ANY, VMEM],
+            [SERVING, shape],
+            [
+                pltpu.VMEM(TOTAL.shape, f32),
+                pltpu.VMEM((20, 128, 128), bf16),
+                pltpu.SemaphoreType.DMA((20,)),
+            ],
+            {6: 0},
+        )(place, features, gain, total, old, pieces[number], out)
+    return (*state_new, out, total)
 
 
 def solution(mesh):

time: 99.8 us -> 99.5 us (level)
  waiting for transfers between devices: 33.3 us -> 31.6 us
  Pallas kernels: 14.8 us -> 15.9 us
    ppermute x14, waiting for transfers between devices: 21.7 us -> 20 us  [on_dp(): return lax.ppermute(value, 'dp', pairs)]
    pallas_call x1 -> x2, Pallas kernels: 2.95 us -> 4.12 us  [on_device(): local(functools.partial(last_kernel, number), [SMEM] + [VMEM] * 5 + [ANY]...]
  transfers between devices with their start and end apart: 21 -> 21, of which waited for: 11 -> 10; matrix products, arithmetic and copies ran while one was open for 12% -> 12% of each run, Pallas kernels for 8% -> 9%
where the time goes in v4:
time: 99.5 us; the launch traced here: 99.1 us
  starting transfers between devices  36.5 us (37%)
  waiting for transfers between devices  31.6 us (32%)
  Pallas kernels  15.9 us (16%)
  local copies, waits for them, and re-layouts  7.17 us (7%)
  other arithmetic  6.87 us (7%)
  between operations  1.06 us (1%)
    ppermute x14, starting transfers between devices, on_dp(): return lax.ppermute(value, 'dp', pairs)  22.3 us
    ppermute x14, waiting for transfers between devices, on_dp(): return lax.ppermute(value, 'dp', pairs)  20 us
    ppermute x6, waiting for transfers between devices, on_mp(): return lax.ppermute(value, 'mp', pairs)  8.98 us
    ppermute x6, starting transfers between devices, on_mp(): return lax.ppermute(value, 'mp', pairs)  8.05 us
    ppermute x1, starting transfers between devices, on_device(): extra = lax.ppermute(extra, ('dp', 'mp'), SWAP)  6.17 us
    squeeze x3, local copies, waits for them, and re-layouts, part(): return lax.dynamic_slice(parts, start, (1, 1, count, 128, 128))[0, 0]  5.69 us
    pallas_call x1, Pallas kernels, on_device(): local(second_kernel, [SMEM] + [VMEM] * 6, [VMEM, ANY, VMEM, VMEM], [SERVI...  4.83 us
    convert_element_type x4, other arithmetic, add(): return sum((term.astype(f32) for term in terms)).astype(bf16)  4.82 us
  transfers between devices with their start and end apart: 21, of which 10 were waited for; matrix products, arithmetic and copies ran while one was open for 12% of the time, Pallas kernels for 9%

profile of v4, /device:TPU:1, one launch (start us, length us, event | category | flops | bytes accessed | tf_op | source)
XLA Modules:
  0.0 99.1 jit_solution(3580833589293834219)
XLA Ops:
  0.7 2.0 %dynamic-slice_bitcast_fusion.3 = bf16[20,128,128]{2,1,0:T(8,128)(2,1)} fusion(bf16[4,2,20,128,128]{4,3,2,1,0:T(8,128)(2,1)} %bitcast.44, s32[]{:T(128)S(6)} %select_n.83, s32[]{:T(128)S(6)} %select_n.84), kind=kLoop, calls=%fused_computation.13 | loop fusion | bytes 1310728 | tf_op jit(solution)/shard_map/squeeze | solution.py:298
  2.7 1.4 %collective-permute-start = (bf16[20,128,128]{2,1,0:T(8,128)(2,1)}, bf16[20,128,128]{2,1,0:T(8,128)(2,1)S(1)}, u32[]{:S(2)}, u32[]{:S(2)}) collective-permute-start(bf16[20,128,128]{2,1,0:T(8,128)(2,1)} %dynamic-slice_bitcast_fusion.3), channel_id=1, source_target_pairs={{0,16},{16,0},{32,48},{48,32},{64,80},{80,64},{96,112},{112,96},{1... | collective-permute-start | bytes 1966088 | tf_op jit(solution)/shard_map/ppermute | solution.py:42
  4.1 2.6 %dynamic-slice_bitcast_fusion = (bf16[20,128,128]{2,1,0:T(8,128)(2,1)}, bf16[20,128,128]{2,1,0:T(8,128)(2,1)}) fusion(bf16[4,2,20,128,128]{4,3,2,1,0:T(8,128)(2,1)} %bitcast.45, s32[]{:T(128)S(6)} %select_n.87, s32[]{:T(128)S(6)} %select_n.84, s32[]{:T(128)S(6)} %select_n.89), kind=kLoop, calls=%fused_computation.10 | loop fusion | bytes 2621452 | tf_op jit(solution)/shard_map/squeeze | solution.py:298
  6.7 0.5 collective-permute-start.2
  7.2 0.4 copy.21
  7.6 0.6 gather_fusion
  8.2 1.3 %fusion.3 = bf16[20,128,128]{2,1,0:T(8,128)(2,1)S(1)} fusion(bf16[20,128,128]{2,1,0:T(8,128)(2,1)S(1)} %collective-permute-done, bf16[4,2,20,128,128]{4,3,2,1,0:T(8,128)(2,1)} %bitcast.46, s32[]{:T(128)S(6)} %select_n.83, s32[]{:T(128)S(6)} %select_n.85), kind=kLoop, calls=%fused_computation.8 | loop fusion | flops 1310720 | bytes 1966088 | tf_op jit(solution)/shard_map/convert_element_type | solution.py:56
  9.5 3.9 %collective-permute-start.5 = (bf16[20,128,128]{2,1,0:T(8,128)(2,1)S(1)}, bf16[20,128,128]{2,1,0:T(8,128)(2,1)S(1)}, u32[]{:S(2)}, u32[]{:S(2)}) collective-permute-start(bf16[20,128,128]{2,1,0:T(8,128)(2,1)S(1)} %fusion.3), channel_id=1, source_target_pairs={{0,32},{16,112},{32,64},{48,16},{64,96},{80,48},{96,0},{112,80},{1... | collective-permute-start | bytes 1966088 | tf_op jit(solution)/shard_map/ppermute | solution.py:42
  13.4 1.3 %fusion.2.refs_1_ = bf16[20,128,128]{2,1,0:T(8,128)(2,1)S(1)} fusion(bf16[20,128,128]{2,1,0:T(8,128)(2,1)S(1)} %collective-permute-done.1, bf16[4,2,20,128,128]{4,3,2,1,0:T(8,128)(2,1)} %bitcast.47, s32[]{:T(128)S(6)} %select_n.87, s32[]{:T(128)S(6)} %select_n.85), kind=kLoop, calls=%fused_computation.6 | loop fusion | flops 1310720 | bytes 1966088 | tf_op jit(solution)/shard_map/convert_element_type | solution.py:56
  14.7 1.1 %dynamic-slice_bitcast_fusion.1.refs_2_ = bf16[20,128,128]{2,1,0:T(8,128)(2,1)S(1)} fusion(bf16[4,2,20,128,128]{4,3,2,1,0:T(8,128)(2,1)} %bitcast.48, s32[]{:T(128)S(6)} %select_n.90, s32[]{:T(128)S(6)} %select_n.84), kind=kLoop, calls=%fused_computation.11 | loop fusion | bytes 1310728 | tf_op jit(solution)/shard_map/squeeze | solution.py:298
  15.8 0.1 collective-permute-start.3
  15.9 1.3 %fusion.1.refs_1_ = bf16[20,128,128]{2,1,0:T(8,128)(2,1)S(1)} fusion(bf16[20,128,128]{2,1,0:T(8,128)(2,1)S(1)} %shard_map.128, bf16[4,2,20,128,128]{4,3,2,1,0:T(8,128)(2,1)} %bitcast.49, s32[]{:T(128)S(6)} %select_n.89, s32[]{:T(128)S(6)} %select_n.85), kind=kLoop, calls=%fused_computation.4 | loop fusion | flops 1310720 | bytes 1966088 | tf_op jit(solution)/shard_map/convert_element_type | solution.py:56
  17.2 0.1 collective-permute-start.4
  17.3 0.1 pad_select_fusion.refs_2_.picked
  17.4 5.6 %collective-permute-done.5.refs_0_ = bf16[20,128,128]{2,1,0:T(8,128)(2,1)S(1)} collective-permute-done((bf16[20,128,128]{2,1,0:T(8,128)(2,1)S(1)}, bf16[20,128,128]{2,1,0:T(8,128)(2,1)S(1)}, u32[]{:S(2)}, u32[]{:S(2)}) %collective-permute-start.5) | collective-permute-done | bytes 655392 | tf_op jit(solution)/shard_map/ppermute | solution.py:42
  23.0 1.0 %add_convert_fusion = bf16[20,128,128]{2,1,0:T(8,128)(2,1)} fusion(bf16[20,128,128]{2,1,0:T(8,128)(2,1)S(1)} %shard_map.129, bf16[20,128,128]{2,1,0:T(8,128)(2,1)S(1)} %fusion.2.refs_1_), kind=kLoop, calls=%fused_computation.9 | loop fusion | flops 1310720 | bytes 1966080 | tf_op jit(solution)/shard_map/convert_element_type | solution.py:56
  24.0 3.5 %collective-permute-start.6 = (bf16[20,128,128]{2,1,0:T(8,128)(2,1)}, bf16[20,128,128]{2,1,0:T(8,128)(2,1)S(1)}, u32[]{:S(2)}, u32[]{:S(2)}) collective-permute-start(bf16[20,128,128]{2,1,0:T(8,128)(2,1)} %add_convert_fusion), channel_id=1, source_target_pairs={{0,32},{16,112},{32,64},{48,16},{64,96},{80,48},{96,0},{112,80},{1... | collective-permute-start | bytes 1966088 | tf_op jit(solution)/shard_map/ppermute | solution.py:42
  27.5 0.1 stack.42.place
  27.6 1.1 %collective-permute-done.4 = bf16[20,128,128]{2,1,0:T(8,128)(2,1)} collective-permute-done((bf16[20,128,128]{2,1,0:T(8,128)(2,1)S(1)}, bf16[20,128,128]{2,1,0:T(8,128)(2,1)}, u32[]{:S(2)}, u32[]{:S(2)}) %collective-permute-start.4) | collective-permute-done | bytes 655392 | tf_op jit(solution)/shard_map/ppermute | solution.py:42
  28.7 1.9 %fusion.near = f32[20,128,128]{2,1,0:T(8,128)S(1)} fusion(bf16[20,128,128]{2,1,0:T(8,128)(2,1)} %collective-permute-done.4, bf16[20,128,128]{2,1,0:T(8,128)(2,1)} %collective-permute-done.3, bf16[4,2,20,128,128]{4,3,2,1,0:T(8,128)(2,1)} %bitcast.50, s32[]{:T(128)S(6)} %select_n.90, s32[]{:T(128)S(6)} %select_n.85), kind=kLoop, calls=%fused_computation.2 | loop fusion | flops 1638400 | bytes 3276808 | tf_op jit(solution)/shard_map/add | solution.py:318
  30.7 4.7 %collective-permute-done.6.relay = bf16[20,128,128]{2,1,0:T(8,128)(2,1)S(1)} collective-permute-done((bf16[20,128,128]{2,1,0:T(8,128)(2,1)}, bf16[20,128,128]{2,1,0:T(8,128)(2,1)S(1)}, u32[]{:S(2)}, u32[]{:S(2)}) %collective-permute-start.6) | collective-permute-done | bytes 655392 | tf_op jit(solution)/shard_map/ppermute | solution.py:42
  35.3 4.3 %shard_map.130 = (f32[20,128,128]{2,1,0:T(8,128)}, f32[20,128,128]{2,1,0:T(8,128)}, f32[20,128,128]{2,1,0:T(8,128)}, bf16[560,128]{1,0:T(8,128)(2,1)S(1)}, bf16[...) custom-call(s32[6]{0:T(128)S(1)} %stack.42.place, ...), custom_call_target="tpu_custom_call" | custom-call | flops 1000 | bytes 1000 | tf_op jit(solution)/shard_map/pallas_call | solution.py:112
  39.6 2.5 %collective-permute-start.9 = (bf16[560,128]{1,0:T(8,128)(2,1)S(1)}, bf16[560,128]{1,0:T(8,128)(2,1)S(1)}, u32[]{:S(2)}, u32[]{:S(2)}) collective-permute-start(bf16[560,128]{1,0:T(8,128)(2,1)S(1)} %get-tuple-element.48), channel_id=1, source_target_pairs={{0,12},{1,13},{2,14},{3,15},{4,0},{5,1},{6,2},{7,3},{8,4},{9,5},{1... | collective-permute-start | bytes 430088 | tf_op jit(solution)/shard_map/ppermute | solution.py:46
  42.1 0.5 collective-permute-start.8
  42.6 0.6 collective-permute-start.7
  43.2 6.2 %collective-permute-start.10 = (bf16[512,128]{1,0:T(8,128)(2,1)S(1)}, bf16[512,128]{1,0:T(8,128)(2,1)S(1)}, u32[]{:S(2)}, u32[]{:S(2)}) collective-permute-start(bf16[512,128]{1,0:T(8,128)(2,1)S(1)} %get-tuple-element.49), channel_id=1, source_target_pairs={{0,0},{1,1},{2,2},{3,3},{4,16},{5,17},{6,18},{7,19},{8,32},{9,33},... | collective-permute-start | bytes 393224 | tf_op jit(solution)/shard_map/ppermute | solution.py:325
  49.4 0.2 collective-permute-done.7
  49.7 2.6 %collective-permute-done.10 = bf16[512,128]{1,0:T(8,128)(2,1)S(1)} collective-permute-done((bf16[512,128]{1,0:T(8,128)(2,1)S(1)}, bf16[512,128]{1,0:T(8,128)(2,1)S(1)}, u32[]{:S(2)}, u32[]{:S(2)}) %collective-permute-start.10) | collective-permute-done | bytes 131104 | tf_op jit(solution)/shard_map/ppermute | solution.py:325
  52.4 1.4 %collective-permute-start.11 = (bf16[832,128]{1,0:T(8,128)(2,1)S(1)}, bf16[832,128]{1,0:T(8,128)(2,1)S(1)}, u32[]{:S(2)}, u32[]{:S(2)}) collective-permute-start(bf16[832,128]{1,0:T(8,128)(2,1)S(1)} %get-tuple-element.90), channel_id=1, source_target_pairs={{0,1},{1,2},{2,3},{3,0},{4,5},{5,6},{6,7},{7,4},{8,9},{9,10},{10,1... | collective-permute-start | bytes 638984 | tf_op jit(solution)/shard_map/ppermute | solution.py:46
  53.8 1.5 %collective-permute-start.13 = (bf16[832,128]{1,0:T(8,128)(2,1)S(1)}, bf16[832,128]{1,0:T(8,128)(2,1)S(1)}, u32[]{:S(2)}, u32[]{:S(2)}) collective-permute-start(bf16[832,128]{1,0:T(8,128)(2,1)S(1)} %get-tuple-element.92), channel_id=1, source_target_pairs={{0,3},{1,0},{2,1},{3,2},{4,7},{5,4},{6,5},{7,6},{8,11},{9,8},{10,9... | collective-permute-start | bytes 638984 | tf_op jit(solution)/shard_map/ppermute | solution.py:46
  55.3 1.6 %collective-permute-start.12 = (bf16[832,128]{1,0:T(8,128)(2,1)S(1)}, bf16[832,128]{1,0:T(8,128)(2,1)S(1)}, u32[]{:S(2)}, u32[]{:S(2)}) collective-permute-start(bf16[832,128]{1,0:T(8,128)(2,1)S(1)} %get-tuple-element.91), channel_id=1, source_target_pairs={{0,2},{1,3},{2,0},{3,1},{4,6},{5,7},{6,4},{7,5},{8,10},{9,11},{10,... | collective-permute-start | bytes 638984 | tf_op jit(solution)/shard_map/ppermute | solution.py:46
  56.9 3.1 %collective-permute-done.11 = bf16[832,128]{1,0:T(8,128)(2,1)S(1)} collective-permute-done((bf16[832,128]{1,0:T(8,128)(2,1)S(1)}, bf16[832,128]{1,0:T(8,128)(2,1)S(1)}, u32[]{:S(2)}, u32[]{:S(2)}) %collective-permute-start.11) | collective-permute-done | bytes 213024 | tf_op jit(solution)/shard_map/ppermute | solution.py:46
  60.0 5.6 %collective-permute-done.12 = bf16[832,128]{1,0:T(8,128)(2,1)S(1)} collective-permute-done((bf16[832,128]{1,0:T(8,128)(2,1)S(1)}, bf16[832,128]{1,0:T(8,128)(2,1)S(1)}, u32[]{:S(2)}, u32[]{:S(2)}) %collective-permute-start.12) | collective-permute-done | bytes 213024 | tf_op jit(solution)/shard_map/ppermute | solution.py:46
  65.7 1.6 %collective-permute-start.15 = (bf16[20,128,128]{2,1,0:T(8,128)(2,1)S(1)}, bf16[20,128,128]{2,1,0:T(8,128)(2,1)S(1)}, u32[]{:S(2)}, u32[]{:S(2)}) collective-permute-start(bf16[20,128,128]{2,1,0:T(8,128)(2,1)S(1)} %bitcast.39), channel_id=1, source_target_pairs={{0,16},{16,0},{32,48},{48,32},{64,80},{80,64},{96,112},{112,96},{1... | collective-permute-start | bytes 1966088 | tf_op jit(solution)/shard_map/ppermute | solution.py:42
  67.3 4.5 %collective-permute-start.14 = (bf16[20,128,128]{2,1,0:T(8,128)(2,1)S(1)}, bf16[20,128,128]{2,1,0:T(8,128)(2,1)S(1)}, u32[]{:S(2)}, u32[]{:S(2)}) collective-permute-start(bf16[20,128,128]{2,1,0:T(8,128)(2,1)S(1)} %bitcast.40), channel_id=1, source_target_pairs={{0,32},{16,112},{32,64},{48,16},{64,96},{80,48},{96,0},{112,80},{1... | collective-permute-start | bytes 1966088 | tf_op jit(solution)/shard_map/ppermute | solution.py:42
  71.8 1.7 %collective-permute-start.17 = (bf16[20,128,128]{2,1,0:T(8,128)(2,1)S(1)}, bf16[20,128,128]{2,1,0:T(8,128)(2,1)S(1)}, u32[]{:S(2)}, u32[]{:S(2)}) collective-permute-start(bf16[20,128,128]{2,1,0:T(8,128)(2,1)S(1)} %collective-permute-done.15.paired), channel_id=1, source_target_pairs={{0,32},{16,112},{32,64},{48,16},{64,96},{80,48},{96,0},{112,80},{1... | collective-permute-start | bytes 1966088 | tf_op jit(solution)/shard_map/ppermute | solution.py:42
  73.5 2.7 %shard_map.131 = (bf16[5120,512]{1,0:T(8,128)(2,1)S(1)}, bf16[40,128,128]{2,1,0:T(8,128)(2,1)S(1)}) custom-call(s32[6]{0:T(128)S(1)} %stack.42.place, bf16[5120,512]{1,0:T(8,128)(2,1)S(1)} %bitcast.38, bf16[20,128,128]{2,1,0:T(8,128)(2,1)S(1)} %bitcast.41, bf16[20,128,128]{2,1,0:T(8,128)(2,1)S(1)} %collective-permute-done.15.paired), custom_call_target="tpu_custom_call" | custom-call | flops 1000 | bytes 1000 | tf_op jit(solution)/shard_map/pallas_call | solution.py:342
  76.3 3.1 %collective-permute-done.14.refs_0_ = bf16[20,128,128]{2,1,0:T(8,128)(2,1)S(1)} collective-permute-done((bf16[20,128,128]{2,1,0:T(8,128)(2,1)S(1)}, bf16[20,128,128]{2,1,0:T(8,128)(2,1)S(1)}, u32[]{:S(2)}, u32[]{:S(2)}) %collective-permute-start.14) | collective-permute-done | bytes 655392 | tf_op jit(solution)/shard_map/ppermute | solution.py:42
  79.3 1.4 %collective-permute-start.16 = (bf16[20,128,128]{2,1,0:T(8,128)(2,1)S(1)}, bf16[20,128,128]{2,1,0:T(8,128)(2,1)S(1)}, u32[]{:S(2)}, u32[]{:S(2)}) collective-permute-start(bf16[20,128,128]{2,1,0:T(8,128)(2,1)S(1)} %shard_map.132.refs_0_), channel_id=1, source_target_pairs={{0,16},{16,0},{32,48},{48,32},{64,80},{80,64},{96,112},{112,96},{1... | collective-permute-start | bytes 1966088 | tf_op jit(solution)/shard_map/ppermute | solution.py:42
  80.7 1.7 %collective-permute-start.19 = (bf16[20,128,128]{2,1,0:T(8,128)(2,1)S(1)}, bf16[20,128,128]{2,1,0:T(8,128)(2,1)S(1)}, u32[]{:S(2)}, u32[]{:S(2)}) collective-permute-start(bf16[20,128,128]{2,1,0:T(8,128)(2,1)S(1)} %shard_map.132.refs_0_), channel_id=1, source_target_pairs={{0,32},{16,112},{32,64},{48,16},{64,96},{80,48},{96,0},{112,80},{1... | collective-permute-start | bytes 1966088 | tf_op jit(solution)/shard_map/ppermute | solution.py:42
  82.5 3.9 %collective-permute-done.17.refs_2_ = bf16[20,128,128]{2,1,0:T(8,128)(2,1)S(1)} collective-permute-done((bf16[20,128,128]{2,1,0:T(8,128)(2,1)S(1)}, bf16[20,128,128]{2,1,0:T(8,128)(2,1)S(1)}, u32[]{:S(2)}, u32[]{:S(2)}) %collective-permute-start.17) | collective-permute-done | bytes 655392 | tf_op jit(solution)/shard_map/ppermute | solution.py:42
  86.3 1.4 %collective-permute-start.18 = (bf16[20,128,128]{2,1,0:T(8,128)(2,1)S(1)}, bf16[20,128,128]{2,1,0:T(8,128)(2,1)S(1)}, u32[]{:S(2)}, u32[]{:S(2)}) collective-permute-start(bf16[20,128,128]{2,1,0:T(8,128)(2,1)S(1)} %collective-permute-done.17.refs_2_), channel_id=1, source_target_pairs={{0,16},{16,0},{32,48},{48,32},{64,80},{80,64},{96,112},{112,96},{1... | collective-permute-start | bytes 1966088 | tf_op jit(solution)/shard_map/ppermute | solution.py:42
  87.8 1.7 %collective-permute-done.18.refs_3_ = bf16[20,128,128]{2,1,0:T(8,128)(2,1)S(1)} collective-permute-done((bf16[20,128,128]{2,1,0:T(8,128)(2,1)S(1)}, bf16[20,128,128]{2,1,0:T(8,128)(2,1)S(1)}, u32[]{:S(2)}, u32[]{:S(2)}) %collective-permute-start.18) | collective-permute-done | bytes 655392 | tf_op jit(solution)/shard_map/ppermute | solution.py:42
  89.5 4.8 %shard_map.133 = (bf16[5120,512]{1,0:T(8,128)(2,1)S(1)}, bf16[5120,512]{1,0:T(8,128)(2,1)}, f32[4,16,128]{2,1,0:T(8,128)S(1)}, bf16[40,16,128]{2,1,0:T(8,128)(2,1)S(1)}) custom-call(s32[6]{0:T(128)S(1)} %stack.42.place, bf16[4,192,128]{2,1,0:T(8,128)(2,1)S(1)} %pad_maximum_fusion.picked, ...), custom_call_target="tpu_custom_call", output_to_operand_aliasing={{0}: (6, {})} | custom-call | flops 1000 | bytes 1000 | tf_op jit(solution)/shard_map/pallas_call | solution.py:352
  94.3 0.5 collective-permute-start.20
  94.8 0.2 copy-done.3
  95.0 1.8 %shard_map.135 = (bf16[5120,512]{1,0:T(8,128)(2,1)}, f32[4,16,128]{2,1,0:T(8,128)S(1)}) custom-call(s32[6]{0:T(128)S(1)} %stack.42.place, bf16[40,16,128]{2,1,0:T(8,128)(2,1)S(1)} %get-tuple-element.52.features, f32[1,128]{1,0:T(1,128)S(1)} %bitcast.42, f32[4,16,128]{2,1,0:T(8,128)S(1)} %get-tuple-element.53.refs_1_.before, ...), custom_call_target="tpu_custom_call", output_to_operand_aliasing={{0}: (6, {})} | custom-call | flops 1000 | bytes 1000 | tf_op jit(solution)/shard_map/pallas_call | solution.py:364
  96.7 2.4 %shard_map.136 = (bf16[5120,512]{1,0:T(8,128)(2,1)}, bf16[16,512]{1,0:T(8,128)(2,1)}) custom-call(s32[6]{0:T(128)S(1)} %stack.42.place, bf16[40,16,128]{2,1,0:T(8,128)(2,1)S(1)} %get-tuple-element.52.features, f32[1,128]{1,0:T(1,128)S(1)} %bitcast.43, f32[4,16,128]{2,1,0:T(8,128)S(1)} %get-tuple-element.55.before, ...), custom_call_target="tpu_custom_call", output_to_operand_aliasing={{0}: (6, {})} | custom-call | flops 1000 | bytes 1000 | tf_op jit(solution)/shard_map/pallas_call | solution.py:364
  (52 shorter events, 0.4 us)
Async XLA Ops:
  2.7 5.5 %collective-permute-start = (bf16[20,128,128]{2,1,0:T(8,128)(2,1)}, bf16[20,128,128]{2,1,0:T(8,128)(2,1)S(1)}, u32[]{:S(2)}, u32[]{:S(2)}) collective-permute-start(bf16[20,128,128]{2,1,0:T(8,128)(2,1)} %dynamic-slice_bitcast_fusion.3), channel_id=1, source_target_pairs={{0,16},{16,0},{32,48},{48,32},{64,80},{80,64},{96,112},{112,96},{1... | collective-permute-start | bytes 1966088 | tf_op jit(solution)/shard_map/ppermute | solution.py:42
  4.1 3.1 %copy-start.6 = (s32[16]{0:T(128)S(1)}, s32[16]{0:T(128)}, u32[]{:S(2)}) copy-start(s32[16]{0:T(128)} %param.16) | copy-start | bytes 196
  4.1 3.1 %copy-start.5 = (bf16[1024,320]{0,1:T(8,128)(2,1)S(1)}, bf16[1024,320]{0,1:T(8,128)(2,1)}, u32[]{:S(2)}) copy-start(bf16[1024,320]{0,1:T(8,128)(2,1)} %param.15) | copy-start | bytes 1966084
  6.7 6.8 %collective-permute-start.1 = (bf16[20,128,128]{2,1,0:T(8,128)(2,1)}, bf16[20,128,128]{2,1,0:T(8,128)(2,1)S(1)}, u32[]{:S(2)}, u32[]{:S(2)}) collective-permute-start(bf16[20,128,128]{2,1,0:T(8,128)(2,1)} %get-tuple-element.60), channel_id=1, source_target_pairs={{0,16},{16,0},{32,48},{48,32},{64,80},{80,64},{96,112},{112,96},{1... | collective-permute-start | bytes 1966088 | tf_op jit(solution)/shard_map/ppermute | solution.py:42
  6.7 9.3 %collective-permute-start.2 = (bf16[20,128,128]{2,1,0:T(8,128)(2,1)}, bf16[20,128,128]{2,1,0:T(8,128)(2,1)S(1)}, u32[]{:S(2)}, u32[]{:S(2)}) collective-permute-start(bf16[20,128,128]{2,1,0:T(8,128)(2,1)} %get-tuple-element.59), channel_id=1, source_target_pairs={{0,16},{16,0},{32,48},{48,32},{64,80},{80,64},{96,112},{112,96},{1... | collective-permute-start | bytes 1966088 | tf_op jit(solution)/shard_map/ppermute | solution.py:42
  9.5 13.5 %collective-permute-start.5 = (bf16[20,128,128]{2,1,0:T(8,128)(2,1)S(1)}, bf16[20,128,128]{2,1,0:T(8,128)(2,1)S(1)}, u32[]{:S(2)}, u32[]{:S(2)}) collective-permute-start(bf16[20,128,128]{2,1,0:T(8,128)(2,1)S(1)} %fusion.3), channel_id=1, source_target_pairs={{0,32},{16,112},{32,64},{48,16},{64,96},{80,48},{96,0},{112,80},{1... | collective-permute-start | bytes 1966088 | tf_op jit(solution)/shard_map/ppermute | solution.py:42
  15.8 12.9 %collective-permute-start.3 = (bf16[20,128,128]{2,1,0:T(8,128)(2,1)S(1)}, bf16[20,128,128]{2,1,0:T(8,128)(2,1)}, u32[]{:S(2)}, u32[]{:S(2)}) collective-permute-start(bf16[20,128,128]{2,1,0:T(8,128)(2,1)S(1)} %dynamic-slice_bitcast_fusion.1.refs_2_), channel_id=1, source_target_pairs={{0,16},{16,0},{32,48},{48,32},{64,80},{80,64},{96,112},{112,96},{1... | collective-permute-start | bytes 1966088 | tf_op jit(solution)/shard_map/ppermute | solution.py:42
  17.2 11.5 %collective-permute-start.4 = (bf16[20,128,128]{2,1,0:T(8,128)(2,1)S(1)}, bf16[20,128,128]{2,1,0:T(8,128)(2,1)}, u32[]{:S(2)}, u32[]{:S(2)}) collective-permute-start(bf16[20,128,128]{2,1,0:T(8,128)(2,1)S(1)} %fusion.1.refs_1_), channel_id=1, source_target_pairs={{0,96},{16,48},{32,0},{48,80},{64,32},{80,112},{96,64},{112,16},{1... | collective-permute-start | bytes 1966088 | tf_op jit(solution)/shard_map/ppermute | solution.py:42
  23.0 12.4 %copy-start.2 = (f32[20,128,128]{2,1,0:T(8,128)S(1)}, f32[20,128,128]{2,1,0:T(8,128)}, u32[]{:S(2)}) copy-start(f32[20,128,128]{2,1,0:T(8,128)} %second.1) | copy-start | bytes 3932164
  24.0 11.4 %collective-permute-start.6 = (bf16[20,128,128]{2,1,0:T(8,128)(2,1)}, bf16[20,128,128]{2,1,0:T(8,128)(2,1)S(1)}, u32[]{:S(2)}, u32[]{:S(2)}) collective-permute-start(bf16[20,128,128]{2,1,0:T(8,128)(2,1)} %add_convert_fusion), channel_id=1, source_target_pairs={{0,32},{16,112},{32,64},{48,16},{64,96},{80,48},{96,0},{112,80},{1... | collective-permute-start | bytes 1966088 | tf_op jit(solution)/shard_map/ppermute | solution.py:42
  27.6 7.8 %copy-start = (f32[20,128,128]{2,1,0:T(8,128)S(1)}, f32[20,128,128]{2,1,0:T(8,128)}, u32[]{:S(2)}) copy-start(f32[20,128,128]{2,1,0:T(8,128)} %master.1) | copy-start | bytes 3932164
  27.6 7.8 %copy-start.1 = (f32[20,128,128]{2,1,0:T(8,128)S(1)}, f32[20,128,128]{2,1,0:T(8,128)}, u32[]{:S(2)}) copy-start(f32[20,128,128]{2,1,0:T(8,128)} %first.1) | copy-start | bytes 3932164
  27.6 7.8 %copy-start.4 = (s32[20]{0:T(128)S(1)}, s32[20]{0:T(128)}, u32[]{:S(2)}) copy-start(s32[20]{0:T(128)} %marked.1) | copy-start | bytes 244
  28.7 44.8 %slice-start = ((s8[5242880]{0:T(1024)(128)(4,1)}), s8[4194304]{0:T(1024)(128)(4,1)S(1)}, s32[]{:S(2)}) async-start(s8[5242880]{0:T(1024)(128)(4,1)} %bitcast.37), calls=%async_computation | async-start | bytes 8388608
  30.6 42.9 %slice-start.1 = ((s8[5242880]{0:T(1024)(128)(4,1)}), s8[1048576]{0:T(1024)(128)(4,1)S(1)}, s32[]{:S(2)}) async-start(s8[5242880]{0:T(1024)(128)(4,1)} %bitcast.37), calls=%async_computation.1 | async-start | bytes 2097152
  39.6 10.1 %collective-permute-start.9 = (bf16[560,128]{1,0:T(8,128)(2,1)S(1)}, bf16[560,128]{1,0:T(8,128)(2,1)S(1)}, u32[]{:S(2)}, u32[]{:S(2)}) collective-permute-start(bf16[560,128]{1,0:T(8,128)(2,1)S(1)} %get-tuple-element.48), channel_id=1, source_target_pairs={{0,12},{1,13},{2,14},{3,15},{4,0},{5,1},{6,2},{7,3},{8,4},{9,5},{1... | collective-permute-start | bytes 430088 | tf_op jit(solution)/shard_map/ppermute | solution.py:46
  42.1 7.6 %collective-permute-start.8 = (bf16[560,128]{1,0:T(8,128)(2,1)S(1)}, bf16[560,128]{1,0:T(8,128)(2,1)S(1)}, u32[]{:S(2)}, u32[]{:S(2)}) collective-permute-start(bf16[560,128]{1,0:T(8,128)(2,1)S(1)} %get-tuple-element.47), channel_id=1, source_target_pairs={{0,8},{1,9},{2,10},{3,11},{4,12},{5,13},{6,14},{7,15},{8,0},{9,1},... | collective-permute-start | bytes 430088 | tf_op jit(solution)/shard_map/ppermute | solution.py:46
  42.6 7.0 %collective-permute-start.7 = (bf16[560,128]{1,0:T(8,128)(2,1)S(1)}, bf16[560,128]{1,0:T(8,128)(2,1)S(1)}, u32[]{:S(2)}, u32[]{:S(2)}) collective-permute-start(bf16[560,128]{1,0:T(8,128)(2,1)S(1)} %get-tuple-element.46), channel_id=1, source_target_pairs={{0,4},{1,5},{2,6},{3,7},{4,8},{5,9},{6,10},{7,11},{8,12},{9,13},{1... | collective-permute-start | bytes 430088 | tf_op jit(solution)/shard_map/ppermute | solution.py:46
  43.2 9.1 %collective-permute-start.10 = (bf16[512,128]{1,0:T(8,128)(2,1)S(1)}, bf16[512,128]{1,0:T(8,128)(2,1)S(1)}, u32[]{:S(2)}, u32[]{:S(2)}) collective-permute-start(bf16[512,128]{1,0:T(8,128)(2,1)S(1)} %get-tuple-element.49), channel_id=1, source_target_pairs={{0,0},{1,1},{2,2},{3,3},{4,16},{5,17},{6,18},{7,19},{8,32},{9,33},... | collective-permute-start | bytes 393224 | tf_op jit(solution)/shard_map/ppermute | solution.py:325
  52.4 7.6 %collective-permute-start.11 = (bf16[832,128]{1,0:T(8,128)(2,1)S(1)}, bf16[832,128]{1,0:T(8,128)(2,1)S(1)}, u32[]{:S(2)}, u32[]{:S(2)}) collective-permute-start(bf16[832,128]{1,0:T(8,128)(2,1)S(1)} %get-tuple-element.90), channel_id=1, source_target_pairs={{0,1},{1,2},{2,3},{3,0},{4,5},{5,6},{6,7},{7,4},{8,9},{9,10},{10,1... | collective-permute-start | bytes 638984 | tf_op jit(solution)/shard_map/ppermute | solution.py:46
  53.8 11.9 %collective-permute-start.13 = (bf16[832,128]{1,0:T(8,128)(2,1)S(1)}, bf16[832,128]{1,0:T(8,128)(2,1)S(1)}, u32[]{:S(2)}, u32[]{:S(2)}) collective-permute-start(bf16[832,128]{1,0:T(8,128)(2,1)S(1)} %get-tuple-element.92), channel_id=1, source_target_pairs={{0,3},{1,0},{2,1},{3,2},{4,7},{5,4},{6,5},{7,6},{8,11},{9,8},{10,9... | collective-permute-start | bytes 638984 | tf_op jit(solution)/shard_map/ppermute | solution.py:46
  55.3 10.4 %collective-permute-start.12 = (bf16[832,128]{1,0:T(8,128)(2,1)S(1)}, bf16[832,128]{1,0:T(8,128)(2,1)S(1)}, u32[]{:S(2)}, u32[]{:S(2)}) collective-permute-start(bf16[832,128]{1,0:T(8,128)(2,1)S(1)} %get-tuple-element.91), channel_id=1, source_target_pairs={{0,2},{1,3},{2,0},{3,1},{4,6},{5,7},{6,4},{7,5},{8,10},{9,11},{10,... | collective-permute-start | bytes 638984 | tf_op jit(solution)/shard_map/ppermute | solution.py:46
  65.7 6.1 %collective-permute-start.15 = (bf16[20,128,128]{2,1,0:T(8,128)(2,1)S(1)}, bf16[20,128,128]{2,1,0:T(8,128)(2,1)S(1)}, u32[]{:S(2)}, u32[]{:S(2)}) collective-permute-start(bf16[20,128,128]{2,1,0:T(8,128)(2,1)S(1)} %bitcast.39), channel_id=1, source_target_pairs={{0,16},{16,0},{32,48},{48,32},{64,80},{80,64},{96,112},{112,96},{1... | collective-permute-start | bytes 1966088 | tf_op jit(solution)/shard_map/ppermute | solution.py:42
  67.3 12.0 %collective-permute-start.14 = (bf16[20,128,128]{2,1,0:T(8,128)(2,1)S(1)}, bf16[20,128,128]{2,1,0:T(8,128)(2,1)S(1)}, u32[]{:S(2)}, u32[]{:S(2)}) collective-permute-start(bf16[20,128,128]{2,1,0:T(8,128)(2,1)S(1)} %bitcast.40), channel_id=1, source_target_pairs={{0,32},{16,112},{32,64},{48,16},{64,96},{80,48},{96,0},{112,80},{1... | collective-permute-start | bytes 1966088 | tf_op jit(solution)/shard_map/ppermute | solution.py:42
  71.8 14.5 %collective-permute-start.17 = (bf16[20,128,128]{2,1,0:T(8,128)(2,1)S(1)}, bf16[20,128,128]{2,1,0:T(8,128)(2,1)S(1)}, u32[]{:S(2)}, u32[]{:S(2)}) collective-permute-start(bf16[20,128,128]{2,1,0:T(8,128)(2,1)S(1)} %collective-permute-done.15.paired), channel_id=1, source_target_pairs={{0,32},{16,112},{32,64},{48,16},{64,96},{80,48},{96,0},{112,80},{1... | collective-permute-start | bytes 1966088 | tf_op jit(solution)/shard_map/ppermute | solution.py:42
  79.3 8.5 %collective-permute-start.16 = (bf16[20,128,128]{2,1,0:T(8,128)(2,1)S(1)}, bf16[20,128,128]{2,1,0:T(8,128)(2,1)S(1)}, u32[]{:S(2)}, u32[]{:S(2)}) collective-permute-start(bf16[20,128,128]{2,1,0:T(8,128)(2,1)S(1)} %shard_map.132.refs_0_), channel_id=1, source_target_pairs={{0,16},{16,0},{32,48},{48,32},{64,80},{80,64},{96,112},{112,96},{1... | collective-permute-start | bytes 1966088 | tf_op jit(solution)/shard_map/ppermute | solution.py:42
  80.7 13.6 %collective-permute-start.19 = (bf16[20,128,128]{2,1,0:T(8,128)(2,1)S(1)}, bf16[20,128,128]{2,1,0:T(8,128)(2,1)S(1)}, u32[]{:S(2)}, u32[]{:S(2)}) collective-permute-start(bf16[20,128,128]{2,1,0:T(8,128)(2,1)S(1)} %shard_map.132.refs_0_), channel_id=1, source_target_pairs={{0,32},{16,112},{32,64},{48,16},{64,96},{80,48},{96,0},{112,80},{1... | collective-permute-start | bytes 1966088 | tf_op jit(solution)/shard_map/ppermute | solution.py:42
  86.3 3.1 %collective-permute-start.18 = (bf16[20,128,128]{2,1,0:T(8,128)(2,1)S(1)}, bf16[20,128,128]{2,1,0:T(8,128)(2,1)S(1)}, u32[]{:S(2)}, u32[]{:S(2)}) collective-permute-start(bf16[20,128,128]{2,1,0:T(8,128)(2,1)S(1)} %collective-permute-done.17.refs_2_), channel_id=1, source_target_pairs={{0,16},{16,0},{32,48},{48,32},{64,80},{80,64},{96,112},{112,96},{1... | collective-permute-start | bytes 1966088 | tf_op jit(solution)/shard_map/ppermute | solution.py:42
  94.3 0.7 copy-start.3
  94.3 2.4 %collective-permute-start.20 = (bf16[20,128,128]{2,1,0:T(8,128)(2,1)S(1)}, bf16[20,128,128]{2,1,0:T(8,128)(2,1)S(1)}, u32[]{:S(2)}, u32[]{:S(2)}) collective-permute-start(bf16[20,128,128]{2,1,0:T(8,128)(2,1)S(1)} %shard_map.134.piece), channel_id=1, source_target_pairs={{0,16},{16,0},{32,48},{48,32},{64,80},{80,64},{96,112},{112,96},{1... | collective-permute-start | bytes 1966088 | tf_op jit(solution)/shard_map/ppermute | solution.py:42

commit v5 on v4

--- a/solution.py
+++ b/solution.py
@@ -287,7 +287,9 @@
     down = (z + 3 + 2 * core) % 4
     opposite = (z + 2) % 4
 
-    picked = jnp.take(hidden_pool, row_ids, axis=0, mode="clip")
+    pool = jnp.arange(hidden_pool.shape[0], dtype=jnp.int32)
+    chosen = (row_ids[:, None] == pool[None, :]).astype(bf16)
+    picked = jnp.dot(chosen, hidden_pool, preferred_element_type=f32).astype(bf16)
     even, odd = (jnp.pad(picked, ((0, 0), ends)) for ends in ((0, 64), (64, 0)))
     picked = jnp.where(y % 2 == 1, odd, even)
 

time: 99.5 us -> 99.3 us (level)
  transfers between devices with their start and end apart: 21 -> 21, of which waited for: 10 -> 10; matrix products, arithmetic and copies ran while one was open for 12% -> 11% of each run, Pallas kernels for 9% -> 9%
where the time goes in v5:
time: 99.3 us; the launch traced here: 98.9 us
  starting transfers between devices  36.5 us (37%)
  waiting for transfers between devices  31.6 us (32%)
  Pallas kernels  15.9 us (16%)
  other arithmetic  6.89 us (7%)
  local copies, waits for them, and re-layouts  6.68 us (7%)
    ppermute x14, starting transfers between devices, on_dp(): return lax.ppermute(value, 'dp', pairs)  22.2 us
    ppermute x14, waiting for transfers between devices, on_dp(): return lax.ppermute(value, 'dp', pairs)  20 us
    ppermute x6, waiting for transfers between devices, on_mp(): return lax.ppermute(value, 'mp', pairs)  8.92 us
    ppermute x6, starting transfers between devices, on_mp(): return lax.ppermute(value, 'mp', pairs)  8.05 us
    ppermute x1, starting transfers between devices, on_device(): extra = lax.ppermute(extra, ('dp', 'mp'), SWAP)  6.23 us
    convert_element_type x4, other arithmetic, add(): return sum((term.astype(f32) for term in terms)).astype(bf16)  4.84 us
    squeeze x3, local copies, waits for them, and re-layouts, part(): return lax.dynamic_slice(parts, start, (1, 1, count, 128, 128))[0, 0]  4.83 us
    pallas_call x1, Pallas kernels, on_device(): local(second_kernel, [SMEM] + [VMEM] * 6, [VMEM, ANY, VMEM, VMEM], [SERVI...  4.83 us
  transfers between devices with their start and end apart: 21, of which 10 were waited for; matrix products, arithmetic and copies ran while one was open for 11% of the time, Pallas kernels for 9%

profile of v5, /device:TPU:1, one launch (start us, length us, event | category | flops | bytes accessed | tf_op | source)
XLA Modules:
  0.0 98.9 jit_solution(9585800449366795168)
XLA Ops:
  0.7 1.2 %dynamic-slice_bitcast_fusion.3 = bf16[20,128,128]{2,1,0:T(8,128)(2,1)S(1)} fusion(bf16[4,2,20,128,128]{4,3,2,1,0:T(8,128)(2,1)} %bitcast.45, s32[]{:T(128)S(6)} %select_n.83, s32[]{:T(128)S(6)} %select_n.84), kind=kLoop, calls=%fused_computation.13 | loop fusion | bytes 1310728 | tf_op jit(solution)/shard_map/squeeze | solution.py:300
  1.9 1.5 %collective-permute-start = (bf16[20,128,128]{2,1,0:T(8,128)(2,1)S(1)}, bf16[20,128,128]{2,1,0:T(8,128)(2,1)S(1)}, u32[]{:S(2)}, u32[]{:S(2)}) collective-permute-start(bf16[20,128,128]{2,1,0:T(8,128)(2,1)S(1)} %dynamic-slice_bitcast_fusion.3), channel_id=1, source_target_pairs={{0,16},{16,0},{32,48},{48,32},{64,80},{80,64},{96,112},{112,96},{1... | collective-permute-start | bytes 1966088 | tf_op jit(solution)/shard_map/ppermute | solution.py:42
  3.4 2.5 %dynamic-slice_bitcast_fusion = (bf16[20,128,128]{2,1,0:T(8,128)(2,1)}, bf16[20,128,128]{2,1,0:T(8,128)(2,1)}) fusion(bf16[4,2,20,128,128]{4,3,2,1,0:T(8,128)(2,1)} %bitcast.46, s32[]{:T(128)S(6)} %select_n.87, s32[]{:T(128)S(6)} %select_n.84, s32[]{:T(128)S(6)} %select_n.89), kind=kLoop, calls=%fused_computation.10 | loop fusion | bytes 2621452 | tf_op jit(solution)/shard_map/squeeze | solution.py:300
  6.0 0.4 collective-permute-start.2
  6.4 0.3 convolution_convert_fusion
  6.7 1.3 %fusion.3 = bf16[20,128,128]{2,1,0:T(8,128)(2,1)S(1)} fusion(bf16[20,128,128]{2,1,0:T(8,128)(2,1)S(1)} %collective-permute-done, bf16[4,2,20,128,128]{4,3,2,1,0:T(8,128)(2,1)} %bitcast.47, s32[]{:T(128)S(6)} %select_n.83, s32[]{:T(128)S(6)} %select_n.85), kind=kLoop, calls=%fused_computation.7 | loop fusion | flops 1310720 | bytes 1966088 | tf_op jit(solution)/shard_map/convert_element_type | solution.py:56
  8.0 3.9 %collective-permute-start.5 = (bf16[20,128,128]{2,1,0:T(8,128)(2,1)S(1)}, bf16[20,128,128]{2,1,0:T(8,128)(2,1)S(1)}, u32[]{:S(2)}, u32[]{:S(2)}) collective-permute-start(bf16[20,128,128]{2,1,0:T(8,128)(2,1)S(1)} %fusion.3), channel_id=1, source_target_pairs={{0,32},{16,112},{32,64},{48,16},{64,96},{80,48},{96,0},{112,80},{1... | collective-permute-start | bytes 1966088 | tf_op jit(solution)/shard_map/ppermute | solution.py:42
  11.9 1.3 %fusion.2.refs_1_ = bf16[20,128,128]{2,1,0:T(8,128)(2,1)S(1)} fusion(bf16[20,128,128]{2,1,0:T(8,128)(2,1)S(1)} %collective-permute-done.1, bf16[4,2,20,128,128]{4,3,2,1,0:T(8,128)(2,1)} %bitcast.48, s32[]{:T(128)S(6)} %select_n.87, s32[]{:T(128)S(6)} %select_n.85), kind=kLoop, calls=%fused_computation.5 | loop fusion | flops 1310720 | bytes 1966088 | tf_op jit(solution)/shard_map/convert_element_type | solution.py:56
  13.2 1.1 %dynamic-slice_bitcast_fusion.1.refs_2_ = bf16[20,128,128]{2,1,0:T(8,128)(2,1)S(1)} fusion(bf16[4,2,20,128,128]{4,3,2,1,0:T(8,128)(2,1)} %bitcast.49, s32[]{:T(128)S(6)} %select_n.90, s32[]{:T(128)S(6)} %select_n.84), kind=kLoop, calls=%fused_computation.11 | loop fusion | bytes 1310728 | tf_op jit(solution)/shard_map/squeeze | solution.py:300
  14.3 0.1 collective-permute-start.3
  14.5 1.3 %fusion.1.refs_1_ = bf16[20,128,128]{2,1,0:T(8,128)(2,1)S(1)} fusion(bf16[20,128,128]{2,1,0:T(8,128)(2,1)S(1)} %shard_map.128, bf16[4,2,20,128,128]{4,3,2,1,0:T(8,128)(2,1)} %bitcast.50, s32[]{:T(128)S(6)} %select_n.89, s32[]{:T(128)S(6)} %select_n.85), kind=kLoop, calls=%fused_computation.3 | loop fusion | flops 1310720 | bytes 1966088 | tf_op jit(solution)/shard_map/convert_element_type | solution.py:56
  15.7 0.1 collective-permute-start.4
  15.8 0.1 pad_select_fusion.refs_2_.picked
  15.9 5.6 %collective-permute-done.5.refs_0_ = bf16[20,128,128]{2,1,0:T(8,128)(2,1)S(1)} collective-permute-done((bf16[20,128,128]{2,1,0:T(8,128)(2,1)S(1)}, bf16[20,128,128]{2,1,0:T(8,128)(2,1)S(1)}, u32[]{:S(2)}, u32[]{:S(2)}) %collective-permute-start.5) | collective-permute-done | bytes 655392 | tf_op jit(solution)/shard_map/ppermute | solution.py:42
  21.5 1.0 %add_convert_fusion = bf16[20,128,128]{2,1,0:T(8,128)(2,1)} fusion(bf16[20,128,128]{2,1,0:T(8,128)(2,1)S(1)} %shard_map.129, bf16[20,128,128]{2,1,0:T(8,128)(2,1)S(1)} %fusion.2.refs_1_), kind=kLoop, calls=%fused_computation.8 | loop fusion | flops 1310720 | bytes 1966080 | tf_op jit(solution)/shard_map/convert_element_type | solution.py:56
  22.5 3.5 %collective-permute-start.6 = (bf16[20,128,128]{2,1,0:T(8,128)(2,1)}, bf16[20,128,128]{2,1,0:T(8,128)(2,1)S(1)}, u32[]{:S(2)}, u32[]{:S(2)}) collective-permute-start(bf16[20,128,128]{2,1,0:T(8,128)(2,1)} %add_convert_fusion), channel_id=1, source_target_pairs={{0,32},{16,112},{32,64},{48,16},{64,96},{80,48},{96,0},{112,80},{1... | collective-permute-start | bytes 1966088 | tf_op jit(solution)/shard_map/ppermute | solution.py:42
  26.0 0.1 stack.42.place
  26.1 1.2 %collective-permute-done.4 = bf16[20,128,128]{2,1,0:T(8,128)(2,1)} collective-permute-done((bf16[20,128,128]{2,1,0:T(8,128)(2,1)S(1)}, bf16[20,128,128]{2,1,0:T(8,128)(2,1)}, u32[]{:S(2)}, u32[]{:S(2)}) %collective-permute-start.4) | collective-permute-done | bytes 655392 | tf_op jit(solution)/shard_map/ppermute | solution.py:42
  27.3 1.9 %fusion.near = f32[20,128,128]{2,1,0:T(8,128)S(1)} fusion(bf16[20,128,128]{2,1,0:T(8,128)(2,1)} %collective-permute-done.4, bf16[20,128,128]{2,1,0:T(8,128)(2,1)} %collective-permute-done.3, bf16[4,2,20,128,128]{4,3,2,1,0:T(8,128)(2,1)} %bitcast.51, s32[]{:T(128)S(6)} %select_n.90, s32[]{:T(128)S(6)} %select_n.85), kind=kLoop, calls=%fused_computation.1 | loop fusion | flops 1638400 | bytes 3276808 | tf_op jit(solution)/shard_map/add | solution.py:320
  29.2 4.6 %collective-permute-done.6.relay = bf16[20,128,128]{2,1,0:T(8,128)(2,1)S(1)} collective-permute-done((bf16[20,128,128]{2,1,0:T(8,128)(2,1)}, bf16[20,128,128]{2,1,0:T(8,128)(2,1)S(1)}, u32[]{:S(2)}, u32[]{:S(2)}) %collective-permute-start.6) | collective-permute-done | bytes 655392 | tf_op jit(solution)/shard_map/ppermute | solution.py:42
  33.9 1.3 %copy-done.3 = f32[20,128,128]{2,1,0:T(8,128)S(1)} copy-done((f32[20,128,128]{2,1,0:T(8,128)S(1)}, f32[20,128,128]{2,1,0:T(8,128)}, u32[]{:S(2)}) %copy-start.3) | copy-done | bytes 1310744
  35.2 4.2 %shard_map.130 = (f32[20,128,128]{2,1,0:T(8,128)}, f32[20,128,128]{2,1,0:T(8,128)}, f32[20,128,128]{2,1,0:T(8,128)}, bf16[560,128]{1,0:T(8,128)(2,1)S(1)}, bf16[...) custom-call(s32[6]{0:T(128)S(1)} %stack.42.place, ...), custom_call_target="tpu_custom_call" | custom-call | flops 1000 | bytes 1000 | tf_op jit(solution)/shard_map/pallas_call | solution.py:112
  39.4 2.5 %collective-permute-start.9 = (bf16[560,128]{1,0:T(8,128)(2,1)S(1)}, bf16[560,128]{1,0:T(8,128)(2,1)S(1)}, u32[]{:S(2)}, u32[]{:S(2)}) collective-permute-start(bf16[560,128]{1,0:T(8,128)(2,1)S(1)} %get-tuple-element.48), channel_id=1, source_target_pairs={{0,12},{1,13},{2,14},{3,15},{4,0},{5,1},{6,2},{7,3},{8,4},{9,5},{1... | collective-permute-start | bytes 430088 | tf_op jit(solution)/shard_map/ppermute | solution.py:46
  41.9 0.5 collective-permute-start.8
  42.4 0.6 collective-permute-start.7
  43.0 6.2 %collective-permute-start.10 = (bf16[512,128]{1,0:T(8,128)(2,1)S(1)}, bf16[512,128]{1,0:T(8,128)(2,1)S(1)}, u32[]{:S(2)}, u32[]{:S(2)}) collective-permute-start(bf16[512,128]{1,0:T(8,128)(2,1)S(1)} %get-tuple-element.49), channel_id=1, source_target_pairs={{0,0},{1,1},{2,2},{3,3},{4,16},{5,17},{6,18},{7,19},{8,32},{9,33},... | collective-permute-start | bytes 393224 | tf_op jit(solution)/shard_map/ppermute | solution.py:327
  49.3 0.1 collective-permute-done.7
  49.5 2.7 %collective-permute-done.10 = bf16[512,128]{1,0:T(8,128)(2,1)S(1)} collective-permute-done((bf16[512,128]{1,0:T(8,128)(2,1)S(1)}, bf16[512,128]{1,0:T(8,128)(2,1)S(1)}, u32[]{:S(2)}, u32[]{:S(2)}) %collective-permute-start.10) | collective-permute-done | bytes 131104 | tf_op jit(solution)/shard_map/ppermute | solution.py:327
  52.3 1.4 %collective-permute-start.11 = (bf16[832,128]{1,0:T(8,128)(2,1)S(1)}, bf16[832,128]{1,0:T(8,128)(2,1)S(1)}, u32[]{:S(2)}, u32[]{:S(2)}) collective-permute-start(bf16[832,128]{1,0:T(8,128)(2,1)S(1)} %get-tuple-element.90), channel_id=1, source_target_pairs={{0,1},{1,2},{2,3},{3,0},{4,5},{5,6},{6,7},{7,4},{8,9},{9,10},{10,1... | collective-permute-start | bytes 638984 | tf_op jit(solution)/shard_map/ppermute | solution.py:46
  53.7 1.5 %collective-permute-start.13 = (bf16[832,128]{1,0:T(8,128)(2,1)S(1)}, bf16[832,128]{1,0:T(8,128)(2,1)S(1)}, u32[]{:S(2)}, u32[]{:S(2)}) collective-permute-start(bf16[832,128]{1,0:T(8,128)(2,1)S(1)} %get-tuple-element.92), channel_id=1, source_target_pairs={{0,3},{1,0},{2,1},{3,2},{4,7},{5,4},{6,5},{7,6},{8,11},{9,8},{10,9... | collective-permute-start | bytes 638984 | tf_op jit(solution)/shard_map/ppermute | solution.py:46
  55.2 1.6 %collective-permute-start.12 = (bf16[832,128]{1,0:T(8,128)(2,1)S(1)}, bf16[832,128]{1,0:T(8,128)(2,1)S(1)}, u32[]{:S(2)}, u32[]{:S(2)}) collective-permute-start(bf16[832,128]{1,0:T(8,128)(2,1)S(1)} %get-tuple-element.91), channel_id=1, source_target_pairs={{0,2},{1,3},{2,0},{3,1},{4,6},{5,7},{6,4},{7,5},{8,10},{9,11},{10,... | collective-permute-start | bytes 638984 | tf_op jit(solution)/shard_map/ppermute | solution.py:46
  56.8 3.2 %collective-permute-done.11 = bf16[832,128]{1,0:T(8,128)(2,1)S(1)} collective-permute-done((bf16[832,128]{1,0:T(8,128)(2,1)S(1)}, bf16[832,128]{1,0:T(8,128)(2,1)S(1)}, u32[]{:S(2)}, u32[]{:S(2)}) %collective-permute-start.11) | collective-permute-done | bytes 213024 | tf_op jit(solution)/shard_map/ppermute | solution.py:46
  60.0 5.6 %collective-permute-done.12 = bf16[832,128]{1,0:T(8,128)(2,1)S(1)} collective-permute-done((bf16[832,128]{1,0:T(8,128)(2,1)S(1)}, bf16[832,128]{1,0:T(8,128)(2,1)S(1)}, u32[]{:S(2)}, u32[]{:S(2)}) %collective-permute-start.12) | collective-permute-done | bytes 213024 | tf_op jit(solution)/shard_map/ppermute | solution.py:46
  65.7 1.5 %collective-permute-start.15 = (bf16[20,128,128]{2,1,0:T(8,128)(2,1)S(1)}, bf16[20,128,128]{2,1,0:T(8,128)(2,1)S(1)}, u32[]{:S(2)}, u32[]{:S(2)}) collective-permute-start(bf16[20,128,128]{2,1,0:T(8,128)(2,1)S(1)} %bitcast.40), channel_id=1, source_target_pairs={{0,16},{16,0},{32,48},{48,32},{64,80},{80,64},{96,112},{112,96},{1... | collective-permute-start | bytes 1966088 | tf_op jit(solution)/shard_map/ppermute | solution.py:42
  67.2 4.4 %collective-permute-start.14 = (bf16[20,128,128]{2,1,0:T(8,128)(2,1)S(1)}, bf16[20,128,128]{2,1,0:T(8,128)(2,1)S(1)}, u32[]{:S(2)}, u32[]{:S(2)}) collective-permute-start(bf16[20,128,128]{2,1,0:T(8,128)(2,1)S(1)} %bitcast.41), channel_id=1, source_target_pairs={{0,32},{16,112},{32,64},{48,16},{64,96},{80,48},{96,0},{112,80},{1... | collective-permute-start | bytes 1966088 | tf_op jit(solution)/shard_map/ppermute | solution.py:42
  71.6 1.7 %collective-permute-start.17 = (bf16[20,128,128]{2,1,0:T(8,128)(2,1)S(1)}, bf16[20,128,128]{2,1,0:T(8,128)(2,1)S(1)}, u32[]{:S(2)}, u32[]{:S(2)}) collective-permute-start(bf16[20,128,128]{2,1,0:T(8,128)(2,1)S(1)} %collective-permute-done.15.paired), channel_id=1, source_target_pairs={{0,32},{16,112},{32,64},{48,16},{64,96},{80,48},{96,0},{112,80},{1... | collective-permute-start | bytes 1966088 | tf_op jit(solution)/shard_map/ppermute | solution.py:42
  73.4 2.7 %shard_map.131 = (bf16[5120,512]{1,0:T(8,128)(2,1)S(1)}, bf16[40,128,128]{2,1,0:T(8,128)(2,1)S(1)}) custom-call(s32[6]{0:T(128)S(1)} %stack.42.place, bf16[5120,512]{1,0:T(8,128)(2,1)S(1)} %bitcast.39, bf16[20,128,128]{2,1,0:T(8,128)(2,1)S(1)} %bitcast.42, bf16[20,128,128]{2,1,0:T(8,128)(2,1)S(1)} %collective-permute-done.15.paired), custom_call_target="tpu_custom_call" | custom-call | flops 1000 | bytes 1000 | tf_op jit(solution)/shard_map/pallas_call | solution.py:344
  76.1 3.1 %collective-permute-done.14.refs_0_ = bf16[20,128,128]{2,1,0:T(8,128)(2,1)S(1)} collective-permute-done((bf16[20,128,128]{2,1,0:T(8,128)(2,1)S(1)}, bf16[20,128,128]{2,1,0:T(8,128)(2,1)S(1)}, u32[]{:S(2)}, u32[]{:S(2)}) %collective-permute-start.14) | collective-permute-done | bytes 655392 | tf_op jit(solution)/shard_map/ppermute | solution.py:42
  79.1 1.4 %collective-permute-start.16 = (bf16[20,128,128]{2,1,0:T(8,128)(2,1)S(1)}, bf16[20,128,128]{2,1,0:T(8,128)(2,1)S(1)}, u32[]{:S(2)}, u32[]{:S(2)}) collective-permute-start(bf16[20,128,128]{2,1,0:T(8,128)(2,1)S(1)} %shard_map.132.refs_0_), channel_id=1, source_target_pairs={{0,16},{16,0},{32,48},{48,32},{64,80},{80,64},{96,112},{112,96},{1... | collective-permute-start | bytes 1966088 | tf_op jit(solution)/shard_map/ppermute | solution.py:42
  80.5 1.7 %collective-permute-start.19 = (bf16[20,128,128]{2,1,0:T(8,128)(2,1)S(1)}, bf16[20,128,128]{2,1,0:T(8,128)(2,1)S(1)}, u32[]{:S(2)}, u32[]{:S(2)}) collective-permute-start(bf16[20,128,128]{2,1,0:T(8,128)(2,1)S(1)} %shard_map.132.refs_0_), channel_id=1, source_target_pairs={{0,32},{16,112},{32,64},{48,16},{64,96},{80,48},{96,0},{112,80},{1... | collective-permute-start | bytes 1966088 | tf_op jit(solution)/shard_map/ppermute | solution.py:42
  82.3 3.9 %collective-permute-done.17.refs_2_ = bf16[20,128,128]{2,1,0:T(8,128)(2,1)S(1)} collective-permute-done((bf16[20,128,128]{2,1,0:T(8,128)(2,1)S(1)}, bf16[20,128,128]{2,1,0:T(8,128)(2,1)S(1)}, u32[]{:S(2)}, u32[]{:S(2)}) %collective-permute-start.17) | collective-permute-done | bytes 655392 | tf_op jit(solution)/shard_map/ppermute | solution.py:42
  86.2 1.4 %collective-permute-start.18 = (bf16[20,128,128]{2,1,0:T(8,128)(2,1)S(1)}, bf16[20,128,128]{2,1,0:T(8,128)(2,1)S(1)}, u32[]{:S(2)}, u32[]{:S(2)}) collective-permute-start(bf16[20,128,128]{2,1,0:T(8,128)(2,1)S(1)} %collective-permute-done.17.refs_2_), channel_id=1, source_target_pairs={{0,16},{16,0},{32,48},{48,32},{64,80},{80,64},{96,112},{112,96},{1... | collective-permute-start | bytes 1966088 | tf_op jit(solution)/shard_map/ppermute | solution.py:42
  87.6 1.7 %collective-permute-done.18.refs_3_ = bf16[20,128,128]{2,1,0:T(8,128)(2,1)S(1)} collective-permute-done((bf16[20,128,128]{2,1,0:T(8,128)(2,1)S(1)}, bf16[20,128,128]{2,1,0:T(8,128)(2,1)S(1)}, u32[]{:S(2)}, u32[]{:S(2)}) %collective-permute-start.18) | collective-permute-done | bytes 655392 | tf_op jit(solution)/shard_map/ppermute | solution.py:42
  89.3 4.8 %shard_map.133 = (bf16[5120,512]{1,0:T(8,128)(2,1)S(1)}, bf16[5120,512]{1,0:T(8,128)(2,1)}, f32[4,16,128]{2,1,0:T(8,128)S(1)}, bf16[40,16,128]{2,1,0:T(8,128)(2,1)S(1)}) custom-call(s32[6]{0:T(128)S(1)} %stack.42.place, bf16[4,192,128]{2,1,0:T(8,128)(2,1)S(1)} %pad_maximum_fusion.picked, ...), custom_call_target="tpu_custom_call", output_to_operand_aliasing={{0}: (6, {})} | custom-call | flops 1000 | bytes 1000 | tf_op jit(solution)/shard_map/pallas_call | solution.py:354
  94.2 0.5 collective-permute-start.20
  94.6 0.2 copy-done.4
  94.8 1.7 %shard_map.135 = (bf16[5120,512]{1,0:T(8,128)(2,1)}, f32[4,16,128]{2,1,0:T(8,128)S(1)}) custom-call(s32[6]{0:T(128)S(1)} %stack.42.place, bf16[40,16,128]{2,1,0:T(8,128)(2,1)S(1)} %get-tuple-element.52.features, f32[1,128]{1,0:T(1,128)S(1)} %bitcast.43, f32[4,16,128]{2,1,0:T(8,128)S(1)} %get-tuple-element.53.refs_1_.before, ...), custom_call_target="tpu_custom_call", output_to_operand_aliasing={{0}: (6, {})} | custom-call | flops 1000 | bytes 1000 | tf_op jit(solution)/shard_map/pallas_call | solution.py:366
  96.5 2.4 %shard_map.136 = (bf16[5120,512]{1,0:T(8,128)(2,1)}, bf16[16,512]{1,0:T(8,128)(2,1)}) custom-call(s32[6]{0:T(128)S(1)} %stack.42.place, bf16[40,16,128]{2,1,0:T(8,128)(2,1)S(1)} %get-tuple-element.52.features, f32[1,128]{1,0:T(1,128)S(1)} %bitcast.44, f32[4,16,128]{2,1,0:T(8,128)S(1)} %get-tuple-element.55.before, ...), custom_call_target="tpu_custom_call", output_to_operand_aliasing={{0}: (6, {})} | custom-call | flops 1000 | bytes 1000 | tf_op jit(solution)/shard_map/pallas_call | solution.py:366
  (50 shorter events, 0.4 us)
Async XLA Ops:
  0.6 5.8 %copy-start = (bf16[1024,320]{0,1:T(8,128)(2,1)S(1)}, bf16[1024,320]{0,1:T(8,128)(2,1)}, u32[]{:S(2)}) copy-start(bf16[1024,320]{0,1:T(8,128)(2,1)} %param.15) | copy-start | bytes 1966084
  1.9 4.8 %collective-permute-start = (bf16[20,128,128]{2,1,0:T(8,128)(2,1)S(1)}, bf16[20,128,128]{2,1,0:T(8,128)(2,1)S(1)}, u32[]{:S(2)}, u32[]{:S(2)}) collective-permute-start(bf16[20,128,128]{2,1,0:T(8,128)(2,1)S(1)} %dynamic-slice_bitcast_fusion.3), channel_id=1, source_target_pairs={{0,16},{16,0},{32,48},{48,32},{64,80},{80,64},{96,112},{112,96},{1... | collective-permute-start | bytes 1966088 | tf_op jit(solution)/shard_map/ppermute | solution.py:42
  3.4 3.0 %copy-start.6 = (s32[16]{0:T(128)S(1)}, s32[16]{0:T(128)}, u32[]{:S(2)}) copy-start(s32[16]{0:T(128)} %param.16) | copy-start | bytes 196
  5.9 6.0 %collective-permute-start.1 = (bf16[20,128,128]{2,1,0:T(8,128)(2,1)}, bf16[20,128,128]{2,1,0:T(8,128)(2,1)S(1)}, u32[]{:S(2)}, u32[]{:S(2)}) collective-permute-start(bf16[20,128,128]{2,1,0:T(8,128)(2,1)} %get-tuple-element.60), channel_id=1, source_target_pairs={{0,16},{16,0},{32,48},{48,32},{64,80},{80,64},{96,112},{112,96},{1... | collective-permute-start | bytes 1966088 | tf_op jit(solution)/shard_map/ppermute | solution.py:42
  6.0 8.5 %collective-permute-start.2 = (bf16[20,128,128]{2,1,0:T(8,128)(2,1)}, bf16[20,128,128]{2,1,0:T(8,128)(2,1)S(1)}, u32[]{:S(2)}, u32[]{:S(2)}) collective-permute-start(bf16[20,128,128]{2,1,0:T(8,128)(2,1)} %get-tuple-element.59), channel_id=1, source_target_pairs={{0,16},{16,0},{32,48},{48,32},{64,80},{80,64},{96,112},{112,96},{1... | collective-permute-start | bytes 1966088 | tf_op jit(solution)/shard_map/ppermute | solution.py:42
  8.0 13.5 %collective-permute-start.5 = (bf16[20,128,128]{2,1,0:T(8,128)(2,1)S(1)}, bf16[20,128,128]{2,1,0:T(8,128)(2,1)S(1)}, u32[]{:S(2)}, u32[]{:S(2)}) collective-permute-start(bf16[20,128,128]{2,1,0:T(8,128)(2,1)S(1)} %fusion.3), channel_id=1, source_target_pairs={{0,32},{16,112},{32,64},{48,16},{64,96},{80,48},{96,0},{112,80},{1... | collective-permute-start | bytes 1966088 | tf_op jit(solution)/shard_map/ppermute | solution.py:42
  14.3 12.9 %collective-permute-start.3 = (bf16[20,128,128]{2,1,0:T(8,128)(2,1)S(1)}, bf16[20,128,128]{2,1,0:T(8,128)(2,1)}, u32[]{:S(2)}, u32[]{:S(2)}) collective-permute-start(bf16[20,128,128]{2,1,0:T(8,128)(2,1)S(1)} %dynamic-slice_bitcast_fusion.1.refs_2_), channel_id=1, source_target_pairs={{0,16},{16,0},{32,48},{48,32},{64,80},{80,64},{96,112},{112,96},{1... | collective-permute-start | bytes 1966088 | tf_op jit(solution)/shard_map/ppermute | solution.py:42
  15.7 11.5 %collective-permute-start.4 = (bf16[20,128,128]{2,1,0:T(8,128)(2,1)S(1)}, bf16[20,128,128]{2,1,0:T(8,128)(2,1)}, u32[]{:S(2)}, u32[]{:S(2)}) collective-permute-start(bf16[20,128,128]{2,1,0:T(8,128)(2,1)S(1)} %fusion.1.refs_1_), channel_id=1, source_target_pairs={{0,96},{16,48},{32,0},{48,80},{64,32},{80,112},{96,64},{112,16},{1... | collective-permute-start | bytes 1966088 | tf_op jit(solution)/shard_map/ppermute | solution.py:42
  22.5 11.4 %collective-permute-start.6 = (bf16[20,128,128]{2,1,0:T(8,128)(2,1)}, bf16[20,128,128]{2,1,0:T(8,128)(2,1)S(1)}, u32[]{:S(2)}, u32[]{:S(2)}) collective-permute-start(bf16[20,128,128]{2,1,0:T(8,128)(2,1)} %add_convert_fusion), channel_id=1, source_target_pairs={{0,32},{16,112},{32,64},{48,16},{64,96},{80,48},{96,0},{112,80},{1... | collective-permute-start | bytes 1966088 | tf_op jit(solution)/shard_map/ppermute | solution.py:42
  26.0 7.8 %copy-start.5 = (s32[20]{0:T(128)S(1)}, s32[20]{0:T(128)}, u32[]{:S(2)}) copy-start(s32[20]{0:T(128)} %marked.1) | copy-start | bytes 244
  26.1 7.8 %copy-start.1 = (f32[20,128,128]{2,1,0:T(8,128)S(1)}, f32[20,128,128]{2,1,0:T(8,128)}, u32[]{:S(2)}) copy-start(f32[20,128,128]{2,1,0:T(8,128)} %master.1) | copy-start | bytes 3932164
  26.1 7.8 %copy-start.2 = (f32[20,128,128]{2,1,0:T(8,128)S(1)}, f32[20,128,128]{2,1,0:T(8,128)}, u32[]{:S(2)}) copy-start(f32[20,128,128]{2,1,0:T(8,128)} %first.1) | copy-start | bytes 3932164
  27.3 46.1 %slice-start = ((s8[5242880]{0:T(1024)(128)(4,1)}), s8[4194304]{0:T(1024)(128)(4,1)S(1)}, s32[]{:S(2)}) async-start(s8[5242880]{0:T(1024)(128)(4,1)} %bitcast.38), calls=%async_computation | async-start | bytes 8388608
  29.2 44.1 %slice-start.1 = ((s8[5242880]{0:T(1024)(128)(4,1)}), s8[1048576]{0:T(1024)(128)(4,1)S(1)}, s32[]{:S(2)}) async-start(s8[5242880]{0:T(1024)(128)(4,1)} %bitcast.38), calls=%async_computation.1 | async-start | bytes 2097152
  33.9 1.3 %copy-start.3 = (f32[20,128,128]{2,1,0:T(8,128)S(1)}, f32[20,128,128]{2,1,0:T(8,128)}, u32[]{:S(2)}) copy-start(f32[20,128,128]{2,1,0:T(8,128)} %second.1) | copy-start | bytes 3932164
  39.4 10.0 %collective-permute-start.9 = (bf16[560,128]{1,0:T(8,128)(2,1)S(1)}, bf16[560,128]{1,0:T(8,128)(2,1)S(1)}, u32[]{:S(2)}, u32[]{:S(2)}) collective-permute-start(bf16[560,128]{1,0:T(8,128)(2,1)S(1)} %get-tuple-element.48), channel_id=1, source_target_pairs={{0,12},{1,13},{2,14},{3,15},{4,0},{5,1},{6,2},{7,3},{8,4},{9,5},{1... | collective-permute-start | bytes 430088 | tf_op jit(solution)/shard_map/ppermute | solution.py:46
  41.9 7.5 %collective-permute-start.8 = (bf16[560,128]{1,0:T(8,128)(2,1)S(1)}, bf16[560,128]{1,0:T(8,128)(2,1)S(1)}, u32[]{:S(2)}, u32[]{:S(2)}) collective-permute-start(bf16[560,128]{1,0:T(8,128)(2,1)S(1)} %get-tuple-element.47), channel_id=1, source_target_pairs={{0,8},{1,9},{2,10},{3,11},{4,12},{5,13},{6,14},{7,15},{8,0},{9,1},... | collective-permute-start | bytes 430088 | tf_op jit(solution)/shard_map/ppermute | solution.py:46
  42.4 6.9 %collective-permute-start.7 = (bf16[560,128]{1,0:T(8,128)(2,1)S(1)}, bf16[560,128]{1,0:T(8,128)(2,1)S(1)}, u32[]{:S(2)}, u32[]{:S(2)}) collective-permute-start(bf16[560,128]{1,0:T(8,128)(2,1)S(1)} %get-tuple-element.46), channel_id=1, source_target_pairs={{0,4},{1,5},{2,6},{3,7},{4,8},{5,9},{6,10},{7,11},{8,12},{9,13},{1... | collective-permute-start | bytes 430088 | tf_op jit(solution)/shard_map/ppermute | solution.py:46
  43.0 9.2 %collective-permute-start.10 = (bf16[512,128]{1,0:T(8,128)(2,1)S(1)}, bf16[512,128]{1,0:T(8,128)(2,1)S(1)}, u32[]{:S(2)}, u32[]{:S(2)}) collective-permute-start(bf16[512,128]{1,0:T(8,128)(2,1)S(1)} %get-tuple-element.49), channel_id=1, source_target_pairs={{0,0},{1,1},{2,2},{3,3},{4,16},{5,17},{6,18},{7,19},{8,32},{9,33},... | collective-permute-start | bytes 393224 | tf_op jit(solution)/shard_map/ppermute | solution.py:327
  52.3 7.6 %collective-permute-start.11 = (bf16[832,128]{1,0:T(8,128)(2,1)S(1)}, bf16[832,128]{1,0:T(8,128)(2,1)S(1)}, u32[]{:S(2)}, u32[]{:S(2)}) collective-permute-start(bf16[832,128]{1,0:T(8,128)(2,1)S(1)} %get-tuple-element.90), channel_id=1, source_target_pairs={{0,1},{1,2},{2,3},{3,0},{4,5},{5,6},{6,7},{7,4},{8,9},{9,10},{10,1... | collective-permute-start | bytes 638984 | tf_op jit(solution)/shard_map/ppermute | solution.py:46
  53.7 12.0 %collective-permute-start.13 = (bf16[832,128]{1,0:T(8,128)(2,1)S(1)}, bf16[832,128]{1,0:T(8,128)(2,1)S(1)}, u32[]{:S(2)}, u32[]{:S(2)}) collective-permute-start(bf16[832,128]{1,0:T(8,128)(2,1)S(1)} %get-tuple-element.92), channel_id=1, source_target_pairs={{0,3},{1,0},{2,1},{3,2},{4,7},{5,4},{6,5},{7,6},{8,11},{9,8},{10,9... | collective-permute-start | bytes 638984 | tf_op jit(solution)/shard_map/ppermute | solution.py:46
  55.2 10.4 %collective-permute-start.12 = (bf16[832,128]{1,0:T(8,128)(2,1)S(1)}, bf16[832,128]{1,0:T(8,128)(2,1)S(1)}, u32[]{:S(2)}, u32[]{:S(2)}) collective-permute-start(bf16[832,128]{1,0:T(8,128)(2,1)S(1)} %get-tuple-element.91), channel_id=1, source_target_pairs={{0,2},{1,3},{2,0},{3,1},{4,6},{5,7},{6,4},{7,5},{8,10},{9,11},{10,... | collective-permute-start | bytes 638984 | tf_op jit(solution)/shard_map/ppermute | solution.py:46
  65.7 5.9 %collective-permute-start.15 = (bf16[20,128,128]{2,1,0:T(8,128)(2,1)S(1)}, bf16[20,128,128]{2,1,0:T(8,128)(2,1)S(1)}, u32[]{:S(2)}, u32[]{:S(2)}) collective-permute-start(bf16[20,128,128]{2,1,0:T(8,128)(2,1)S(1)} %bitcast.40), channel_id=1, source_target_pairs={{0,16},{16,0},{32,48},{48,32},{64,80},{80,64},{96,112},{112,96},{1... | collective-permute-start | bytes 1966088 | tf_op jit(solution)/shard_map/ppermute | solution.py:42
  67.2 11.9 %collective-permute-start.14 = (bf16[20,128,128]{2,1,0:T(8,128)(2,1)S(1)}, bf16[20,128,128]{2,1,0:T(8,128)(2,1)S(1)}, u32[]{:S(2)}, u32[]{:S(2)}) collective-permute-start(bf16[20,128,128]{2,1,0:T(8,128)(2,1)S(1)} %bitcast.41), channel_id=1, source_target_pairs={{0,32},{16,112},{32,64},{48,16},{64,96},{80,48},{96,0},{112,80},{1... | collective-permute-start | bytes 1966088 | tf_op jit(solution)/shard_map/ppermute | solution.py:42
  71.6 14.5 %collective-permute-start.17 = (bf16[20,128,128]{2,1,0:T(8,128)(2,1)S(1)}, bf16[20,128,128]{2,1,0:T(8,128)(2,1)S(1)}, u32[]{:S(2)}, u32[]{:S(2)}) collective-permute-start(bf16[20,128,128]{2,1,0:T(8,128)(2,1)S(1)} %collective-permute-done.15.paired), channel_id=1, source_target_pairs={{0,32},{16,112},{32,64},{48,16},{64,96},{80,48},{96,0},{112,80},{1... | collective-permute-start | bytes 1966088 | tf_op jit(solution)/shard_map/ppermute | solution.py:42
  79.1 8.5 %collective-permute-start.16 = (bf16[20,128,128]{2,1,0:T(8,128)(2,1)S(1)}, bf16[20,128,128]{2,1,0:T(8,128)(2,1)S(1)}, u32[]{:S(2)}, u32[]{:S(2)}) collective-permute-start(bf16[20,128,128]{2,1,0:T(8,128)(2,1)S(1)} %shard_map.132.refs_0_), channel_id=1, source_target_pairs={{0,16},{16,0},{32,48},{48,32},{64,80},{80,64},{96,112},{112,96},{1... | collective-permute-start | bytes 1966088 | tf_op jit(solution)/shard_map/ppermute | solution.py:42
  80.5 13.6 %collective-permute-start.19 = (bf16[20,128,128]{2,1,0:T(8,128)(2,1)S(1)}, bf16[20,128,128]{2,1,0:T(8,128)(2,1)S(1)}, u32[]{:S(2)}, u32[]{:S(2)}) collective-permute-start(bf16[20,128,128]{2,1,0:T(8,128)(2,1)S(1)} %shard_map.132.refs_0_), channel_id=1, source_target_pairs={{0,32},{16,112},{32,64},{48,16},{64,96},{80,48},{96,0},{112,80},{1... | collective-permute-start | bytes 1966088 | tf_op jit(solution)/shard_map/ppermute | solution.py:42
  86.2 3.1 %collective-permute-start.18 = (bf16[20,128,128]{2,1,0:T(8,128)(2,1)S(1)}, bf16[20,128,128]{2,1,0:T(8,128)(2,1)S(1)}, u32[]{:S(2)}, u32[]{:S(2)}) collective-permute-start(bf16[20,128,128]{2,1,0:T(8,128)(2,1)S(1)} %collective-permute-done.17.refs_2_), channel_id=1, source_target_pairs={{0,16},{16,0},{32,48},{48,32},{64,80},{80,64},{96,112},{112,96},{1... | collective-permute-start | bytes 1966088 | tf_op jit(solution)/shard_map/ppermute | solution.py:42
  94.1 0.7 copy-start.4
  94.2 2.4 %collective-permute-start.20 = (bf16[20,128,128]{2,1,0:T(8,128)(2,1)S(1)}, bf16[20,128,128]{2,1,0:T(8,128)(2,1)S(1)}, u32[]{:S(2)}, u32[]{:S(2)}) collective-permute-start(bf16[20,128,128]{2,1,0:T(8,128)(2,1)S(1)} %shard_map.134.piece), channel_id=1, source_target_pairs={{0,16},{16,0},{32,48},{48,32},{64,80},{80,64},{96,112},{112,96},{1... | collective-permute-start | bytes 1966088 | tf_op jit(solution)/shard_map/ppermute | solution.py:42
